TPU v7x, 32 devices: a whole 2x2x4 slice. The times are simulated.
32 devices in a mesh: seq: 8 (over y, x, core), shard: 4 (over z).
Axes of the slice: x: 2, y: 2, z: 4, core: 2. Of those that a mesh axis runs over, the one named last changes fastest.
Arguments:
- tokens: bfloat16 [4, 1024, 768], P('shard', 'seq'), may hold values from -6 to 6
- norm_gain: bfloat16 [768], P('shard'), may hold values from 0.5 to 1.5
- w_qkv: bfloat16 [768, 2304], P('shard'), may hold values from -0.3125 to 0.3125
- w_out: bfloat16 [768, 768], P('shard'), may hold values from -0.875 to 0.875
- ffn_gain: bfloat16 [768], P('shard'), may hold values from 0.5 to 1.5
- w_in: bfloat16 [768, 2304], P('shard'), may hold values from -0.21875 to 0.21875
- w_back: bfloat16 [1152, 768], P('shard'), may hold values from -0.375 to 0.375
- seq_ids: int32 [4, 16], P('shard'), may hold values from 0 to 0, as said below
- cotangent: bfloat16 [4, 1024, 768], P('shard', 'seq'), may hold values from -6 to 6
Outputs:
- mixed: bfloat16 [4, 1024, 768], P('shard', 'seq')
- grad_tokens: bfloat16 [4, 1024, 768], P('shard', 'seq')
- grad_norm_gain: float32 [768], P('shard')
- grad_w_qkv: float32 [768, 2304], P('shard')
- grad_w_out: float32 [768, 768], P('shard')
- grad_ffn_gain: float32 [768], P('shard')
- grad_w_in: float32 [768, 2304], P('shard')
- grad_w_back: float32 [1152, 768], P('shard')
Inputs may be any that keep to these rules, and one draw needn't show every extreme that they name: `seq_ids`: along a row ids never fall and each id 0 to 0 appears; the j-th boundary (j = 1 .. 0) lies within 16 spans of j * 64, the last sequence takes the rest of the set.
All inputs are finite; a program needn't handle non-finite values.
Results may differ from a plain program's by a relative error of at most 0.02.
Values may be sent and summed in bfloat16 or wider, within the bound.
No kernel may reach another device: no remote copies, remote signals or barrier semaphores. Data moves between devices by JAX's collectives and lax.ppermute only.
A program may use at most 128 MiB of HBM per device.

v0:
```python
import jax
import jax.numpy as jnp
from jax import lax
from jax.sharding import PartitionSpec as P

HEADS = 12
HEAD_DIM = 64
FF = 1152
HALF = 64


def extended(cells, sides, width):
    for axis, dim in sides:
        count = lax.axis_size(axis)
        ends = count - 1
        head = lax.slice_in_dim(cells, 0, width, axis=dim)
        tail = lax.slice_in_dim(cells, cells.shape[dim] - width, cells.shape[dim], axis=dim)
        cells = jnp.concatenate(
            [
                lax.ppermute(tail, axis, [(i, (i + 1) % count) for i in range(ends)]),
                cells,
                lax.ppermute(head, axis, [((i + 1) % count, i) for i in range(ends)]),
            ],
            axis=dim,
        )
    return cells


def passed_along(value, axis, steps):
    count = lax.axis_size(axis)
    initial, last = (max(0, -steps), min(count, count - steps))
    return lax.ppermute(value, axis, [(source, source + steps) for source in range(initial, last)])


def norm_parts(values):
    center = values - jnp.mean(values, axis=-1, keepdims=True)
    factor = lax.rsqrt(jnp.mean(center * center, axis=-1, keepdims=True) + 1e-05)
    return (center * factor, factor)


def norm_back(upward, gain_full, normed, factor):
    scaled = upward * gain_full
    gain_term = jnp.sum(upward * normed, axis=0)
    inward = factor * (
        scaled
        - jnp.mean(scaled, axis=-1, keepdims=True)
        - normed * jnp.mean(scaled * normed, axis=-1, keepdims=True)
    )
    return (inward, gain_term)


def rotate(values, cosine, sine):
    middle = values.shape[-1] // 2
    turned = jnp.concatenate([-values[..., middle:], values[..., :middle]], axis=-1)
    return values * cosine + turned * sine


def rotate_back(upward, cosine, sine):
    middle = upward.shape[-1] // 2
    sined = upward * sine
    turned = jnp.concatenate([sined[..., middle:], -sined[..., :middle]], axis=-1)
    return upward * cosine + turned


def shards(tokens, norm_gain, w_qkv, w_out, ffn_gain, w_in, w_back, seq_ids, cotangent):
    single = jnp.float32
    narrow = jnp.bfloat16
    inputs = tokens[0].astype(single)
    length, width = inputs.shape
    heads = HEADS
    head_size = HEAD_DIM
    window = HALF
    hidden_units = FF
    extent = length + 2 * window
    scaling = head_size ** (-0.5)
    gathered = (
        lax.all_gather(norm_gain, "shard", axis=0, tiled=True),
        lax.all_gather(w_qkv, "shard", axis=0, tiled=True),
        lax.all_gather(w_out, "shard", axis=0, tiled=True),
        lax.all_gather(ffn_gain, "shard", axis=0, tiled=True),
        lax.all_gather(w_in, "shard", axis=0, tiled=True),
        lax.all_gather(w_back, "shard", axis=0, tiled=True),
    )
    gain_one = gathered[0].astype(single)
    matrix_qkv = gathered[1]
    matrix_out = gathered[2]
    gain_two = gathered[3].astype(single)
    matrix_in = gathered[4]
    matrix_back = gathered[5]
    device = lax.axis_index("seq")
    position = (device * length + jnp.arange(length)).astype(single)
    frequency = 10000.0 ** (-jnp.arange(0, head_size, 2).astype(single) / head_size)
    angles = position[:, None] * frequency[None, :]
    angles = jnp.concatenate([angles, angles], axis=-1)[:, None, :]
    cosine = jnp.cos(angles)
    sine = jnp.sin(angles)
    blocks = length // window
    span_ids = jnp.pad(seq_ids[0], (1, 1), constant_values=-1)
    span_ids = lax.dynamic_slice_in_dim(span_ids, device * blocks, blocks + 2, 0)
    key_ids = jnp.repeat(span_ids, window)
    query_ids = key_ids[window : window + length]
    offset = jnp.arange(extent)[None, :] - window - jnp.arange(length)[:, None]
    allowed = ((jnp.abs(offset) <= window) & (query_ids[:, None] == key_ids[None, :]))[None]
    normed_one, factor_one = norm_parts(inputs)
    input_low = (normed_one * gain_one).astype(narrow)
    projected = jnp.dot(input_low, matrix_qkv, preferred_element_type=single)
    queries = rotate(projected[:, :width].reshape(length, heads, head_size), cosine, sine).astype(
        narrow
    )
    keys_own = rotate(
        projected[:, width : 2 * width].reshape(length, heads, head_size), cosine, sine
    ).astype(narrow)
    values_own = projected[:, 2 * width :].astype(narrow)
    paired = jnp.concatenate([keys_own.reshape(length, width), values_own], axis=1)
    paired_ext = extended(paired, (("seq", 0),), window)
    keys_ext = paired_ext[:, :width].reshape(extent, heads, head_size)
    values_ext = paired_ext[:, width:].reshape(extent, heads, head_size)

    def logits_of():
        scores = jnp.einsum("qhd,khd->hqk", queries, keys_ext, preferred_element_type=single)
        return jnp.where(allowed, scores * scaling, -1e30)

    logits = logits_of()
    highest = jnp.max(logits, axis=-1, keepdims=True)
    exponent = jnp.exp(logits - highest)
    summed = jnp.sum(exponent, axis=-1, keepdims=True)
    probs_low = (exponent / summed).astype(narrow)
    log_total = highest + jnp.log(summed)
    context = jnp.einsum("hqk,khd->qhd", probs_low, values_ext, preferred_element_type=single)
    attended = context.reshape(length, width).astype(narrow)
    residual = inputs + jnp.dot(attended, matrix_out, preferred_element_type=single)
    normed_two, factor_two = norm_parts(residual)
    middle_low = (normed_two * gain_two).astype(narrow)
    expanded = jnp.dot(middle_low, matrix_in, preferred_element_type=single)
    entering = expanded[:, :hidden_units]
    gating = expanded[:, hidden_units:]
    activated, gelu_pull = jax.vjp(lambda values: jax.nn.gelu(values, approximate=False), entering)
    hidden_low = (activated * gating).astype(narrow)
    mixed = residual + jnp.dot(hidden_low, matrix_back, preferred_element_type=single)
    upward = cotangent[0].astype(single)
    upward_low = upward.astype(narrow)
    grad_back = jnp.einsum("tf,td->fd", hidden_low, upward_low, preferred_element_type=single)
    grad_hidden = jnp.einsum("td,fd->tf", upward_low, matrix_back, preferred_element_type=single)
    grad_entering = gelu_pull(grad_hidden * gating)[0]
    grad_expanded = jnp.concatenate([grad_entering, grad_hidden * activated], axis=1).astype(narrow)
    grad_in = jnp.einsum("td,tf->df", middle_low, grad_expanded, preferred_element_type=single)
    grad_middle = jnp.einsum("tf,df->td", grad_expanded, matrix_in, preferred_element_type=single)
    residual_norm, grad_gain_two = norm_back(grad_middle, gain_two, normed_two, factor_two)
    grad_residual = upward + residual_norm
    residual_low = grad_residual.astype(narrow)
    grad_out = jnp.einsum("td,te->de", attended, residual_low, preferred_element_type=single)
    grad_context = jnp.einsum("te,de->td", residual_low, matrix_out, preferred_element_type=single)
    grad_context = grad_context.astype(narrow).reshape(length, heads, head_size)
    logits_again = logits_of()
    probs_full = jnp.exp(logits_again - log_total)
    probs_again = probs_full.astype(narrow)
    grad_values_ext = jnp.einsum(
        "hqk,qhd->khd", probs_again, grad_context, preferred_element_type=single
    )
    grad_probs = jnp.einsum("qhd,khd->hqk", grad_context, values_ext, preferred_element_type=single)
    row_inner = jnp.sum(probs_full * grad_probs, axis=-1, keepdims=True)
    grad_scores = (probs_full * (grad_probs - row_inner) * scaling).astype(narrow)
    grad_queries = jnp.einsum("hqk,khd->qhd", grad_scores, keys_ext, preferred_element_type=single)
    grad_keys_ext = jnp.einsum("hqk,qhd->khd", grad_scores, queries, preferred_element_type=single)
    grad_pair_ext = jnp.concatenate(
        [grad_keys_ext.reshape(extent, width), grad_values_ext.reshape(extent, width)], axis=1
    )
    from_above = passed_along(grad_pair_ext[:window].astype(jnp.bfloat16), "seq", -1).astype(
        jnp.float32
    )
    from_below = passed_along(
        grad_pair_ext[extent - window :].astype(jnp.bfloat16), "seq", 1
    ).astype(jnp.float32)
    grad_pair = (
        grad_pair_ext[window : window + length]
        + jnp.pad(from_below, ((0, length - window), (0, 0)))
        + jnp.pad(from_above, ((length - window, 0), (0, 0)))
    )
    query_raw = rotate_back(grad_queries, cosine, sine).reshape(length, width)
    key_raw = rotate_back(
        grad_pair[:, :width].reshape(length, heads, head_size), cosine, sine
    ).reshape(length, width)
    grad_projected = jnp.concatenate([query_raw, key_raw, grad_pair[:, width:]], axis=1).astype(
        narrow
    )
    grad_qkv = jnp.einsum("td,te->de", input_low, grad_projected, preferred_element_type=single)
    grad_input_low = jnp.einsum(
        "te,de->td", grad_projected, matrix_qkv, preferred_element_type=single
    )
    input_norm, grad_gain_one = norm_back(grad_input_low, gain_one, normed_one, factor_one)
    grad_inputs = grad_residual + input_norm
    owned = (
        lax.psum_scatter(
            grad_gain_one.astype(jnp.bfloat16), "shard", scatter_dimension=0, tiled=True
        ).astype(jnp.float32),
        lax.psum_scatter(
            grad_qkv.astype(jnp.bfloat16), "shard", scatter_dimension=0, tiled=True
        ).astype(jnp.float32),
        lax.psum_scatter(
            grad_out.astype(jnp.bfloat16), "shard", scatter_dimension=0, tiled=True
        ).astype(jnp.float32),
        lax.psum_scatter(
            grad_gain_two.astype(jnp.bfloat16), "shard", scatter_dimension=0, tiled=True
        ).astype(jnp.float32),
        lax.psum_scatter(
            grad_in.astype(jnp.bfloat16), "shard", scatter_dimension=0, tiled=True
        ).astype(jnp.float32),
        lax.psum_scatter(
            grad_back.astype(jnp.bfloat16), "shard", scatter_dimension=0, tiled=True
        ).astype(jnp.float32),
    )
    owned = lax.psum((owned[0], owned[1], owned[2], owned[3], owned[4], owned[5]), "seq")
    return (
        mixed.astype(narrow)[None],
        grad_inputs.astype(narrow)[None],
        owned[0],
        owned[1],
        owned[2],
        owned[3],
        owned[4],
        owned[5],
    )


def solution(mesh):
    return jax.shard_map(
        shards,
        mesh=mesh,
        in_specs=(
            P("shard", "seq", None),
            P("shard"),
            P("shard", None),
            P("shard", None),
            P("shard"),
            P("shard", None),
            P("shard", None),
            P("shard", None),
            P("shard", "seq", None),
        ),
        out_specs=(
            P("shard", "seq", None),
            P("shard", "seq", None),
            P("shard"),
            P("shard", None),
            P("shard", None),
            P("shard"),
            P("shard", None),
            P("shard", None),
        ),
        check_vma=False,
    )
```

profile of v0, /device:TPU:0, one launch (start us, length us, event | category | flops | bytes accessed | tf_op | source)
XLA Modules:
  0.0 548.6 jit_solution(12641563876741457765)
XLA Ops:
  12.7 13.6 %all-reduce.9 = (bf16[768]{0:T(1024)(128)(2,1)S(1)}, bf16[768]{0:T(1024)(128)(2,1)S(1)}) all-reduce(bf16[768]{0:T(1024)(128)(2,1)S(1)} %dynamic-update-slice, bf16[768]{0:T(1024)(128)(2,1)S(1)} %dynamic-update-slice.1), channel_id=1, replica_groups=mesh['seq'=8,'shard'=4] {'shard'}, use_global_device_ids=true, to_apply=%add.3 | all-reduce | flops 1536 | bytes 6144
  27.4 55.0 %all-gather.5.cloned.1.call-done = bf16[768,2304]{1,0:T(8,128)(2,1)} async-done(((bf16[192,2304]{1,0:T(8,128)(2,1)}), bf16[768,2304]{1,0:T(8,128)(2,1)}) %all-gather.5.cloned.1.call-update) | async-done | bytes 3538960 | tf_op jit(solution)/shard_map/all_gather | solution.py:78
  82.4 2.7 fusion.77
  89.1 3.2 collective-permute-done.1
  95.8 17.2 %all-gather.7.cloned.1.call-done = bf16[768,768]{1,0:T(8,128)(2,1)} async-done(((bf16[192,768]{1,0:T(8,128)(2,1)}), bf16[768,768]{1,0:T(8,128)(2,1)}) %all-gather.7.cloned.1.call-update) | async-done | bytes 1179664 | tf_op jit(solution)/shard_map/all_gather | solution.py:79
  115.0 68.8 %all-gather.9.cloned.1.call-done = bf16[768,2304]{1,0:T(8,128)(2,1)} async-done(((bf16[192,2304]{1,0:T(8,128)(2,1)}), bf16[768,2304]{1,0:T(8,128)(2,1)}) %all-gather.9.cloned.1.call-update) | async-done | bytes 3538960 | tf_op jit(solution)/shard_map/all_gather | solution.py:81
  183.8 3.7 fusion.79
  187.5 36.7 %all-gather.11.cloned.1.call-done = bf16[1152,768]{1,0:T(8,128)(2,1)} async-done(((bf16[288,768]{1,0:T(8,128)(2,1)}), bf16[1152,768]{1,0:T(8,128)(2,1)}) %all-gather.11.cloned.1.call-update) | async-done | bytes 1769488 | tf_op jit(solution)/shard_map/all_gather | solution.py:82
  224.2 3.6 add_convert_fusion
  228.0 1.9 multiply_reduce_fusion.1
  231.7 2.8 convolution_convert_fusion.2
  235.5 4.0 convolution_convert_fusion
  239.7 1.8 convolution_convert_fusion.4
  244.0 11.2 %fusion.6 = f32[12,64,256]{2,1,0:T(8,128)} fusion(bf16[128,12,64]{0,2,1:T(8,128)(2,1)S(1)} %copy-done.16, f32[12,128,256]{2,1,0:T(8,128)} %fusion.89, f32[12,128,256]{2,1,0:T(8,128)S(1)} %get-tuple-element.51, f32[12,128]{1,0:T(8,128)S(1)} %log_add_fusion), kind=kOutput, calls=%fused_computation.15 | convolution fusion | flops 53085952 | bytes 4134912 | tf_op jit(solution)/shard_map/hqk,qhd->khd/dot_general | solution.py:164
  257.5 2.5 collective-permute-start.2
  261.3 11.2 %fusion.12 = f32[128,12,64]{0,2,1:T(8,128)} fusion(bf16[256,12,64]{0,2,1:T(8,128)(2,1)} %bitcast.111, f32[12,128,256]{2,1,0:T(8,128)} %fusion.89, f32[12,128,256]{2,1,0:T(8,128)S(1)} %get-tuple-element.51, f32[12,128]{1,0:T(8,128)S(1)} %copy-done.24), kind=kOutput, calls=%fused_computation.19 | convolution fusion | flops 53085952 | bytes 3938304 | tf_op jit(solution)/shard_map/hqk,khd->qhd/dot_general | solution.py:163
  272.6 1.8 fusion.22
  275.8 3.1 convolution_convert_fusion.1
  281.6 3.4 fusion.50
  285.0 10.8 %all-reduce.8 = (bf16[768]{0:T(1024)(128)(2,1)S(1)}, bf16[768]{0:T(1024)(128)(2,1)S(1)}) all-reduce(bf16[768]{0:T(1024)(128)(2,1)S(1)} %get-tuple-element.10, bf16[768]{0:T(1024)(128)(2,1)S(1)} %copy-done.30), channel_id=2, replica_groups=mesh['seq'=8,'shard'=4] {'shard'}, use_global_device_ids=true, to_apply=%region_12.13.clone | all-reduce | flops 1536 | bytes 6144
  296.9 3.2 reduce-scatter.11.cloned.1.call-done
  300.1 67.9 %reduce-scatter.9.cloned.1.call-done = bf16[192,2304]{1,0:T(8,128)(2,1)} async-done(((bf16[768,2304]{1,0:T(8,128)(2,1)}), bf16[192,2304]{1,0:T(8,128)(2,1)}) %reduce-scatter.9.cloned.1.call-update) | async-done | bytes 884752 | tf_op jit(solution)/shard_map/reduce_scatter | solution.py:205
  368.0 69.1 %reduce-scatter.5.cloned.1.call-done = bf16[192,2304]{1,0:T(8,128)(2,1)} async-done(((bf16[768,2304]{1,0:T(8,128)(2,1)}), bf16[192,2304]{1,0:T(8,128)(2,1)}) %reduce-scatter.5.cloned.1.call-update) | async-done | bytes 884752 | tf_op jit(solution)/shard_map/reduce_scatter | solution.py:196
  437.1 104.6 %all-reduce.11 = (f32[192]{0:T(256)}, f32[192,2304]{1,0:T(8,128)}, f32[192,768]{1,0:T(8,128)}, f32[192]{0:T(256)}, f32[192,2304]{1,0:T(8,128)}, /*index=5*/f32[288,768]{1,0:T(8,128)}) all-reduce(f32[192]{0:T(256)S(1)} %dynamic-slice_convert_fusion.1, ...), channel_id=1, replica_groups=mesh['seq'=8,'shard'=4] {'seq'}, use_global_device_ids=true, to_apply=%region_13.14 | all-reduce | flops 1253760 | bytes 7523328 | tf_op jit(solution)/shard_map/psum | solution.py:212
  (162 shorter events, 28.5 us)
Async XLA Ops:
  7.2 3.8 copy-start.29
  7.2 5.0 copy-start.32
  7.2 5.3 copy-start.33
  7.2 75.2 %all-gather.5.cloned.1.call-start = ((), (), s32[]{:S(2)}) async-start(), calls=%async_computation.4 | async-start | bytes 4423680 | tf_op jit(solution)/shard_map/all_gather | solution.py:78
  8.0 105.1 %all-gather.7.cloned.1.call-start = ((), (), s32[]{:S(2)}) async-start(), calls=%async_computation.5 | async-start | bytes 1474560 | tf_op jit(solution)/shard_map/all_gather | solution.py:79
  8.7 175.1 %all-gather.9.cloned.1.call-start = ((), (), s32[]{:S(2)}) async-start(), calls=%async_computation.6 | async-start | bytes 4423680 | tf_op jit(solution)/shard_map/all_gather | solution.py:81
  9.4 214.7 %all-gather.11.cloned.1.call-start = ((), (), s32[]{:S(2)}) async-start(), calls=%async_computation.7 | async-start | bytes 2211840 | tf_op jit(solution)/shard_map/all_gather | solution.py:82
  10.0 286.8 %reduce-scatter.7.cloned.1.call-start = ((), (), s32[]{:S(2)}) async-start(), calls=%async_computation.9 | async-start | bytes 1474560 | tf_op jit(solution)/shard_map/reduce_scatter | solution.py:199
  10.6 74.5 %copy-start.25 = (f32[128]{0:T(128)}, f32[128]{0:T(128)S(1)}, u32[]{:S(2)}) copy-start(f32[128]{0:T(128)S(1)} %broadcast_multiply_fusion.8) | copy-start | bytes 1540
  10.8 74.3 %copy-start.27 = (f32[128]{0:T(128)}, f32[128]{0:T(128)S(1)}, u32[]{:S(2)}) copy-start(f32[128]{0:T(128)S(1)} %add_rsqrt_fusion.1) | copy-start | bytes 1540
  26.5 62.5 %copy-start.11 = (f32[128,64]{0,1:T(8,128)}, f32[128,64]{0,1:T(8,128)S(1)}, u32[]{:S(2)}) copy-start(f32[128,64]{0,1:T(8,128)S(1)} %get-tuple-element.46) | copy-start | bytes 98308
  26.5 62.5 %copy-start.19 = (f32[128,64]{0,1:T(8,128)}, f32[128,64]{0,1:T(8,128)S(1)}, u32[]{:S(2)}) copy-start(f32[128,64]{0,1:T(8,128)S(1)} %get-tuple-element.47) | copy-start | bytes 98308
  85.9 3.1 collective-permute-start
  87.7 4.6 collective-permute-start.1
  89.1 3.7 copy-start.15
  115.0 109.2 %copy-start.17 = (bf16[1,128,768]{2,1,0:T(8,128)(2,1)S(1)}, bf16[1,128,768]{2,1,0:T(8,128)(2,1)}, u32[]{:S(2)}) copy-start(bf16[1,128,768]{2,1,0:T(8,128)(2,1)} %param.17) | copy-start | bytes 589828
  224.2 3.8 copy-start.2
  227.9 3.8 copy-start.4
  231.7 68.4 %reduce-scatter.11.cloned.1.call-start = ((), (), s32[]{:S(2)}) async-start(), calls=%async_computation.11 | async-start | bytes 2211840 | tf_op jit(solution)/shard_map/reduce_scatter | solution.py:208
  234.5 133.5 %reduce-scatter.9.cloned.1.call-start = ((), (), s32[]{:S(2)}) async-start(), calls=%async_computation.10 | async-start | bytes 4423680 | tf_op jit(solution)/shard_map/reduce_scatter | solution.py:205
  239.5 197.6 %reduce-scatter.5.cloned.1.call-start = ((), (), s32[]{:S(2)}) async-start(), calls=%async_computation.8 | async-start | bytes 4423680 | tf_op jit(solution)/shard_map/reduce_scatter | solution.py:196
  256.4 4.9 copy-start.24
  257.5 15.0 %collective-permute-start.2 = (bf16[64,1536]{0,1:T(8,128)(2,1)}, bf16[64,1536]{0,1:T(8,128)(2,1)}, u32[]{:S(2)}, u32[]{:S(2)}) collective-permute-start(bf16[64,1536]{0,1:T(8,128)(2,1)} %get-tuple-element.30), channel_id=1, source_target_pairs={{0,4},{4,8},{8,12},{12,16},{16,20},{20,24},{24,28},{1,5},{5,9},{9,... | collective-permute-start | bytes 589832 | tf_op jit(solution)/shard_map/ppermute | solution.py:32
  260.0 12.5 %collective-permute-start.3 = (bf16[64,1536]{0,1:T(8,128)(2,1)}, bf16[64,1536]{0,1:T(8,128)(2,1)}, u32[]{:S(2)}, u32[]{:S(2)}) collective-permute-start(bf16[64,1536]{0,1:T(8,128)(2,1)} %get-tuple-element.31), channel_id=1, source_target_pairs={{4,0},{8,4},{12,8},{16,12},{20,16},{24,20},{28,24},{5,1},{9,5},{13... | collective-permute-start | bytes 589832 | tf_op jit(solution)/shard_map/ppermute | solution.py:32
  (22 other events, 41.0 us)
Sparse Core Ops, SparseCore 0:
  9.6 72.7 all-gather.4
  84.0 29.0 all-gather.6
  114.6 69.0 all-gather.8
  185.2 38.8 all-gather.10
  231.8 28.0 reduce-scatter.6
  262.6 37.3 reduce-scatter.10
  302.5 65.4 reduce-scatter.8
  370.4 66.6 reduce-scatter.4
where the time goes:
time: 549 us
  waiting for transfers between devices  324 us (59%)
  blocking collectives  129 us (23%)
  matrix products  58.5 us (11%)
  between operations  16.3 us (3%)
  local copies, waits for them, and re-layouts  7.33 us (1%)
  starting transfers between devices  7.25 us (1%)
  other arithmetic  6.39 us (1%)
    psum x1, blocking collectives, shards(): lax.psum((owned[0], owned[1], owned[2], owned[3], owned[4], owned[5]), 's...  105 us
    reduce_scatter x1, waiting for transfers between devices, shards(): lax.psum_scatter(grad_qkv.astype(jnp.bfloat16), 'shard', scatter_dimensio...  69.1 us
    all_gather x1, waiting for transfers between devices, shards(): lax.all_gather(w_in, 'shard', axis=0, tiled=True)  68.8 us
    reduce_scatter x1, waiting for transfers between devices, shards(): lax.psum_scatter(grad_in.astype(jnp.bfloat16), 'shard', scatter_dimension...  67.9 us
    all_gather x1, waiting for transfers between devices, shards(): lax.all_gather(w_qkv, 'shard', axis=0, tiled=True)  55 us
    all_gather x1, waiting for transfers between devices, shards(): lax.all_gather(w_back, 'shard', axis=0, tiled=True)  36.7 us
    unnamed x2, blocking collectives  24.4 us
    all_gather x1, waiting for transfers between devices, shards(): lax.all_gather(w_out, 'shard', axis=0, tiled=True)  17.2 us
  transfers between devices with their start and end apart: 12, of which 8 were waited for; matrix products, arithmetic and copies ran while one was open for 11% of the time, Pallas kernels for 0%

commit v1 on v0

v1 whole, which is shorter than its diff:
```python
import functools

import jax
import jax.numpy as jnp
from jax import lax
from jax.experimental import pallas as pl
from jax.experimental.pallas import tpu as pltpu
from jax.sharding import PartitionSpec as P

HEADS = 12
HEAD_DIM = 64
FF = 1152
HALF = 64
CHIPS = 4
CORES = 2
MEMBERS = CHIPS * CORES
f32 = jnp.float32
bf16 = jnp.bfloat16
SCALE = HEAD_DIM ** (-0.5)
VMEM = 48 * 1024 * 1024


def dot(left, right):
    return lax.dot_general(left, right, (((1,), (0,)), ((), ())), preferred_element_type=f32)


def dot_t(left, right):
    return lax.dot_general(left, right, (((1,), (1,)), ((), ())), preferred_element_type=f32)


def t_dot(left, right):
    return lax.dot_general(left, right, (((0,), (0,)), ((), ())), preferred_element_type=f32)


def swap_seq(value, bits):
    count = lax.axis_size("seq")
    return lax.ppermute(value, "seq", [(i, i ^ bits) for i in range(count)])


def swap_shard(value, bits):
    count = lax.axis_size("shard")
    return lax.ppermute(value, "shard", [(i, i ^ bits) for i in range(count)])


def swap_core(value):
    return swap_seq(value, 1)


def over_chips(value):
    return [value] + [swap_seq(value, CORES * j) for j in range(1, CHIPS)]


def pick(index, items):
    return lax.select_n(index, *items)


def unxor(index, items):
    return [pick(index, [items[place ^ at] for at in range(4)]) for place in range(4)]


def by_core(core, own, other):
    return (jnp.where(core == 0, own, other), jnp.where(core == 0, other, own))


def norm_parts(values):
    center = values - jnp.mean(values, axis=-1, keepdims=True)
    factor = lax.rsqrt(jnp.mean(center * center, axis=-1, keepdims=True) + 1e-05)
    return center * factor, factor


def norm_inward(upward, gain, normed, factor):
    scaled = upward * gain
    return factor * (
        scaled
        - jnp.mean(scaled, axis=-1, keepdims=True)
        - normed * jnp.mean(scaled * normed, axis=-1, keepdims=True)
    )


def first_half(shape):
    return lax.broadcasted_iota(jnp.int32, shape, 1) % HEAD_DIM < HEAD_DIM // 2


def shifted(values):
    return pltpu.roll(values, 96, 1), pltpu.roll(values, 32, 1)


def qkv_kernel(x0, x1, x2, x3, gain, weight, cos, sin, a_out, q_out, kv_out):
    width = x0.shape[-1]
    rows = x0.shape[0]
    local = weight.shape[1] // 3
    for j, ref in enumerate((x0, x1, x2, x3)):
        normed, _ = norm_parts(ref[...].astype(f32))
        a_out[j * rows : (j + 1) * rows, :] = (normed * gain[...]).astype(bf16)
    out = dot(a_out[...], weight[...])
    front = first_half((CHIPS * rows, 128))
    parts = []
    for at in range(0, 2 * local, 128):
        u = out[:, at : at + 128]
        up, down = shifted(u)
        parts.append((u * cos[...] + jnp.where(front, -up, down) * sin[...]).astype(bf16))
    qk = jnp.concatenate(parts, axis=1)
    q_out[...] = qk[:, :local]
    kv_out[:, :local] = qk[:, local:]
    kv_out[:, local:] = out[:, 2 * local :].astype(bf16)


def probs_of(q, k, bias):
    logits = dot_t(q, k) * SCALE + bias
    highest = jnp.max(logits, axis=-1, keepdims=True)
    exponent = jnp.exp(logits - highest)
    return exponent / jnp.sum(exponent, axis=-1, keepdims=True)


def attend_kernel(q, kv, bias, out):
    local = q.shape[-1]
    heads = local // HEAD_DIM
    parts = []
    for h in range(heads):
        lanes = slice(h * HEAD_DIM, (h + 1) * HEAD_DIM)
        prob = probs_of(q[0, :, lanes], kv[0, :, lanes], bias[0]).astype(bf16)
        value = kv[0, :, local + h * HEAD_DIM : local + (h + 1) * HEAD_DIM]
        parts.append(dot(prob, value))
    out[0] = jnp.concatenate(parts, axis=1).astype(bf16)


def attend_back_kernel(q, kv, bias, dh, w_out, attn, dq_out, dkv_out, gw_out):
    local = q.shape[-1]
    heads = local // HEAD_DIM
    dctx = dot_t(dh[0], w_out[...]).astype(bf16)

    @pl.when(pl.program_id(0) == 0)
    def _():
        gw_out[...] = jnp.zeros_like(gw_out)

    gw_out[...] += t_dot(attn[0], dh[0])
    dqs, dks, dvs = [], [], []
    for h in range(heads):
        lanes = slice(h * HEAD_DIM, (h + 1) * HEAD_DIM)
        qh = q[0, :, lanes]
        kh = kv[0, :, lanes]
        vh = kv[0, :, local + h * HEAD_DIM : local + (h + 1) * HEAD_DIM]
        dch = dctx[:, lanes]
        prob = probs_of(qh, kh, bias[0])
        dprob = dot_t(dch, vh)
        inner = jnp.sum(prob * dprob, axis=-1, keepdims=True)
        dscore = (prob * (dprob - inner) * SCALE).astype(bf16)
        dqs.append(dot(dscore, kh))
        dks.append(t_dot(dscore, qh))
        dvs.append(t_dot(prob.astype(bf16), dch))
    dq_out[0] = jnp.concatenate(dqs, axis=1)
    dkv_out[0] = jnp.concatenate(dks + dvs, axis=1)


def turn_back_kernel(dq, dkv, cos, sin, out):
    local = dq.shape[-1]
    front = first_half((dq.shape[0], 128))
    g = jnp.concatenate([dq[...], dkv[:, :local]], axis=1)
    parts = []
    for at in range(0, 2 * local, 128):
        u = g[:, at : at + 128]
        up, down = shifted(u * sin[...])
        parts.append((u * cos[...] + jnp.where(front, up, -down)).astype(bf16))
    out[...] = jnp.concatenate(parts + [dkv[:, local:].astype(bf16)], axis=1)


def cost(flops, moved):
    return pl.CostEstimate(flops=int(flops), bytes_accessed=int(moved), transcendentals=0)


def params():
    return pltpu.CompilerParams(vmem_limit_bytes=VMEM)


def columns_of(rows, chip, parts):
    width = rows.shape[1] // parts
    share = width // CHIPS
    return pick(
        chip,
        [
            jnp.concatenate(
                [rows[:, p * width + b * share : p * width + (b + 1) * share] for p in range(parts)],
                axis=1,
            )
            for b in range(CHIPS)
        ],
    )


def columns_joined(pieces, parts):
    share = pieces[0].shape[1] // parts
    return jnp.concatenate(
        [piece[:, p * share : (p + 1) * share] for p in range(parts) for piece in pieces], axis=1
    )


def shards(tokens, norm_gain, w_qkv, w_out, ffn_gain, w_in, w_back, seq_ids, cotangent):
    length, width = tokens.shape[1:]
    me = lax.axis_index("seq")
    plane = lax.axis_index("shard")
    seq_count = lax.axis_size("seq")
    shard_count = lax.axis_size("shard")
    groups = seq_count // MEMBERS
    group = me // MEMBERS
    chip = (me % MEMBERS) // CORES
    core = me % CORES
    local = width // CHIPS
    units = FF // CHIPS
    many = CHIPS * length

    def gather_columns(weight, parts):
        half = weight.shape[0] // CORES
        piece = columns_of(lax.dynamic_slice_in_dim(weight, core * half, half, 0), chip, parts)
        pieces = [piece] + [swap_shard(piece, i) for i in range(1, shard_count)]
        mine = jnp.stack(unxor(plane, pieces))
        both = by_core(core, mine, swap_core(mine))
        return jnp.stack(both, axis=1).reshape(CORES * shard_count * half, -1)

    def gather_rows(weight):
        half = weight.shape[0] // CORES
        piece = lax.dynamic_slice_in_dim(weight, core * half, half, 0)
        pieces = [piece]
        for i in range(1, shard_count):
            pairs = [
                (m * shard_count + (m % MEMBERS) // CORES, m * shard_count + ((m % MEMBERS) // CORES ^ i))
                for m in range(seq_count)
            ]
            pieces.append(lax.ppermute(piece, ("seq", "shard"), pairs))
        mine = pick(plane ^ chip, pieces)
        both = by_core(core, mine, swap_core(mine))
        return jnp.concatenate(both, axis=0)

    x_own = tokens[0]
    xs = over_chips(x_own)
    wq = gather_columns(w_qkv, 3)
    gain_parts = lax.all_gather(jnp.stack([norm_gain, ffn_gain]), "shard", axis=1, tiled=True)
    gain_one = gain_parts[0].astype(f32)[None]
    gain_two = gain_parts[1].astype(f32)[None]
    w_out_full = lax.all_gather(w_out, "shard", axis=0, tiled=True).reshape(CHIPS, local, width)
    wo = unxor(chip, [w_out_full[b] for b in range(CHIPS)])
    wi = gather_columns(w_in, 2)
    wb = gather_rows(w_back)
    gys = over_chips(cotangent[0])

    block_chip = chip ^ jnp.arange(CHIPS)
    block = (group * CHIPS + block_chip) * CORES + core
    position = (block[:, None] * length + jnp.arange(length)[None]).astype(f32).reshape(many)
    frequency = 10000.0 ** (-jnp.arange(0, HEAD_DIM, 2).astype(f32) / HEAD_DIM)
    angles = position[:, None] * frequency[None]
    cosine, sine = lax.optimization_barrier((jnp.cos(angles), jnp.sin(angles)))
    cosine = jnp.tile(cosine, (1, 4))
    sine = jnp.tile(sine, (1, 4))
    extent = length + 2 * HALF
    spans = length // HALF
    ids = jnp.pad(seq_ids[0], (1, 1), constant_values=-1)
    key_ids = jnp.stack(
        [lax.dynamic_slice_in_dim(ids, block[j] * spans, spans + 2, 0) for j in range(CHIPS)]
    )
    key_ids = jnp.repeat(key_ids, HALF, axis=1)
    query_ids = key_ids[:, HALF : HALF + length]
    offset = jnp.arange(extent)[None, :] - HALF - jnp.arange(length)[:, None]
    allowed = (jnp.abs(offset) <= HALF)[None] & (query_ids[:, :, None] == key_ids[:, None, :])
    bias = jnp.where(allowed, 0.0, -1e30).astype(f32)

    low_one, query, kv = pl.pallas_call(
        qkv_kernel,
        out_shape=(
            jax.ShapeDtypeStruct((many, width), bf16),
            jax.ShapeDtypeStruct((many, local), bf16),
            jax.ShapeDtypeStruct((many, 2 * local), bf16),
        ),
        cost_estimate=cost(2 * many * width * 3 * local, 4e6),
        compiler_params=params(),
        name="qkv",
    )(*xs, gain_one, wq, cosine, sine)
    kv = kv.reshape(CHIPS, length, 2 * local)
    query = query.reshape(CHIPS, length, local)
    kv_other = swap_core(kv)
    others = unxor(chip, [kv_other[j] for j in range(CHIPS)])
    if groups > 1:
        mine_abs = unxor(chip, [kv[j] for j in range(CHIPS)])
        edge = jnp.where(core == 0, mine_abs[0][:HALF], mine_abs[CHIPS - 1][length - HALF :])

        def beyond(value):
            pairs = []
            for m in range(seq_count):
                c, k = (m % MEMBERS) // CORES, m % CORES
                to = m - MEMBERS + 1 if k == 0 else m + MEMBERS - 1
                if 0 <= to < seq_count:
                    pairs.append((m, to))
            return lax.ppermute(value, "seq", pairs)

        rim = beyond(edge)
    else:
        rim = jnp.zeros((HALF, 2 * local), bf16)
    heads_of = [o[:HALF] for o in others]
    tails_of = [o[length - HALF :] for o in others]
    before = [jnp.where(core == 0, ([rim] + tails_of)[b], tails_of[b]) for b in range(CHIPS)]
    after = [jnp.where(core == 0, heads_of[b], (heads_of + [rim])[b + 1]) for b in range(CHIPS)]
    kv_ext = jnp.concatenate(
        [jnp.stack(unxor(chip, before)), kv, jnp.stack(unxor(chip, after))], axis=1
    )

    def block_spec(rows, lanes):
        return pl.BlockSpec((1, rows, lanes), lambda j: (j, 0, 0))

    attn = pl.pallas_call(
        attend_kernel,
        grid=(CHIPS,),
        in_specs=[block_spec(length, local), block_spec(extent, 2 * local), block_spec(length, extent)],
        out_specs=block_spec(length, local),
        out_shape=jax.ShapeDtypeStruct((CHIPS, length, local), bf16),
        cost_estimate=cost(4 * many * extent * local, 2e6),
        compiler_params=params(),
        name="attend",
    )(query, kv_ext, bias)

    received = over_chips(attn)
    hidden = jnp.concatenate(xs, axis=0).astype(f32)
    for i in range(CHIPS):
        rows = jnp.concatenate([received[i][j ^ i] for j in range(CHIPS)], axis=0)
        hidden = hidden + dot(rows, wo[i])
    normed_two, factor_two = norm_parts(hidden)
    low_two = (normed_two * gain_two).astype(bf16)
    expanded = dot(low_two, wi)
    entering = expanded[:, :units]
    gating = expanded[:, units:]
    activated, gelu_pull = jax.vjp(lambda v: jax.nn.gelu(v, approximate=False), entering)
    hidden_low = (activated * gating).astype(bf16)
    upward_low = jnp.concatenate(gys, axis=0)
    grad_hidden = dot_t(upward_low, wb)
    grad_entering = gelu_pull(grad_hidden * gating)[0]
    grad_expanded = jnp.concatenate([grad_entering, grad_hidden * activated], axis=1).astype(bf16)
    grad_middle = dot_t(grad_expanded, wi)

    def sum_over_chips(partial):
        blocks = partial.reshape(CHIPS, length, width)
        total = blocks[0]
        for j in range(1, CHIPS):
            total = total + swap_seq(blocks[j].astype(bf16), CORES * j).astype(f32)
        return total

    grad_middle_own = sum_over_chips(grad_middle)
    grad_residual = cotangent[0].astype(f32) + norm_inward(
        grad_middle_own, gain_two, normed_two[:length], factor_two[:length]
    )
    residual_low = grad_residual.astype(bf16)
    dhs = jnp.stack(over_chips(residual_low))

    mixed = hidden[:length] + sum_over_chips(dot(hidden_low, wb))
    gain_two_sum = jnp.sum(grad_middle * normed_two, axis=0)
    grad_in = t_dot(low_two, grad_expanded)
    grad_back = t_dot(hidden_low, upward_low)

    def whole(*dims):
        return pl.BlockSpec(dims, lambda j: (0,) * len(dims))

    grad_query, grad_kv_ext, grad_out = pl.pallas_call(
        attend_back_kernel,
        grid=(CHIPS,),
        in_specs=[
            block_spec(length, local),
            block_spec(extent, 2 * local),
            block_spec(length, extent),
            block_spec(length, width),
            whole(local, width),
            block_spec(length, local),
        ],
        out_specs=(block_spec(length, local), block_spec(extent, 2 * local), whole(local, width)),
        out_shape=(
            jax.ShapeDtypeStruct((CHIPS, length, local), f32),
            jax.ShapeDtypeStruct((CHIPS, extent, 2 * local), f32),
            jax.ShapeDtypeStruct((local, width), f32),
        ),
        cost_estimate=cost(10 * many * extent * local, 4e6),
        compiler_params=params(),
        name="attend_back",
    )(query, kv_ext, bias, dhs, wo[0], attn)

    before = unxor(chip, [grad_kv_ext[j, :HALF].astype(bf16) for j in range(CHIPS)])
    after = unxor(chip, [grad_kv_ext[j, extent - HALF :].astype(bf16) for j in range(CHIPS)])
    zero = jnp.zeros((HALF, 2 * local), bf16)
    upper = [jnp.where(core == 0, after[b], ([zero] + after)[b]) for b in range(CHIPS)]
    lower = [jnp.where(core == 0, (before + [zero])[b + 1], before[b]) for b in range(CHIPS)]
    back = jnp.stack(
        unxor(chip, [jnp.concatenate([u, l], axis=0) for u, l in zip(upper, lower)])
    )
    grad_kv = grad_kv_ext[:, HALF : HALF + length] + swap_core(back).astype(f32)
    if groups > 1:
        rim = beyond(jnp.where(core == 0, before[0], after[CHIPS - 1])).astype(f32)
        edge_chip = jnp.where(core == 0, 0, CHIPS - 1)
        placed = jnp.where(
            core == 0,
            jnp.pad(rim, ((0, length - HALF), (0, 0))),
            jnp.pad(rim, ((length - HALF, 0), (0, 0))),
        )
        grad_kv = grad_kv + jnp.where((block_chip == edge_chip)[:, None, None], placed[None], 0.0)
    grad_projected = pl.pallas_call(
        turn_back_kernel,
        out_shape=jax.ShapeDtypeStruct((many, 3 * local), bf16),
        cost_estimate=cost(10 * many * 3 * local, 4e6),
        compiler_params=params(),
        name="turn_back",
    )(grad_query.reshape(many, local), grad_kv.reshape(many, 2 * local), cosine, sine)
    grad_qkv = t_dot(low_one, grad_projected)
    grad_low = dot_t(grad_projected, wq)
    normed_all, _ = norm_parts(jnp.concatenate(xs, axis=0).astype(f32))
    gain_one_sum = jnp.sum(grad_low * normed_all, axis=0)
    grad_low_own = sum_over_chips(grad_low)
    normed_one, factor_one = norm_parts(x_own.astype(f32))
    grad_inputs = grad_residual + norm_inward(grad_low_own, gain_one, normed_one, factor_one)

    def over_groups(total):
        step = MEMBERS
        while step < seq_count:
            total = total + swap_seq(total.astype(bf16), step).astype(f32)
            step *= 2
        return total

    def reduce_columns(grad, parts):
        half = grad.shape[0] // (CORES * shard_count)
        split = grad.reshape(shard_count, CORES, half, grad.shape[1])
        keep = pick(core, [split[:, 0], split[:, 1]])
        away = pick(core, [split[:, 1], split[:, 0]]).astype(bf16)
        keep = keep + swap_core(away).astype(f32)
        blocks = unxor(plane, [keep[b] for b in range(shard_count)])
        total = blocks[0]
        for i in range(1, shard_count):
            total = total + swap_shard(blocks[i].astype(bf16), i).astype(f32)
        total = over_groups(total)
        pieces = unxor(chip, over_chips(total.astype(bf16)))
        mine = columns_joined(pieces, parts)
        return jnp.concatenate(by_core(core, mine, swap_core(mine)), axis=0).astype(f32)

    def reduce_rows(grads):
        halves = [g.shape[0] // CORES for g in grads]

        def halves_of(k):
            return jnp.concatenate([g[k * h : (k + 1) * h] for g, h in zip(grads, halves)], axis=0)

        first, second = halves_of(0), halves_of(1)
        keep = pick(core, [first, second])
        away = pick(core, [second, first]).astype(bf16)
        keep = keep + swap_core(away).astype(f32)
        low = keep.astype(bf16)
        total = keep
        for i in range(1, shard_count):
            pairs = [
                (m * shard_count + ((m % MEMBERS) // CORES ^ i), m * shard_count + (m % MEMBERS) // CORES)
                for m in range(seq_count)
            ]
            total = total + lax.ppermute(low, ("seq", "shard"), pairs).astype(f32)
        total = over_groups(total).astype(bf16)
        pieces = [total]
        for j in range(1, CHIPS):
            pairs = []
            for m in range(seq_count):
                z = (m % MEMBERS) // CORES
                pairs.append((m * shard_count + z, (m ^ (CORES * j)) * shard_count + z))
            pieces.append(lax.ppermute(total, ("seq", "shard"), pairs))
        mine = pick(chip ^ plane, pieces)
        both = by_core(core, mine, swap_core(mine))
        results, at = [], 0
        for h in halves:
            results.append(jnp.concatenate([b[at : at + h] for b in both], axis=0).astype(f32))
            at += h
        return results

    owned_in = reduce_columns(grad_in, 2)
    owned_back, owned_out = reduce_rows((grad_back, grad_out))
    owned_qkv = reduce_columns(grad_qkv, 3)
    gains = jnp.stack([gain_one_sum, gain_two_sum])
    step = 1
    while step < seq_count:
        gains = gains + swap_seq(gains, step)
        step *= 2
    step = 1
    while step < shard_count:
        gains = gains + swap_shard(gains, step)
        step *= 2
    share = norm_gain.shape[0]
    gains = lax.dynamic_slice_in_dim(gains, plane * share, share, 1)
    return (
        mixed.astype(bf16)[None],
        grad_inputs.astype(bf16)[None],
        gains[0],
        owned_qkv,
        owned_out,
        gains[1],
        owned_in,
        owned_back,
    )


def solution(mesh):
    return jax.shard_map(
        shards,
        mesh=mesh,
        in_specs=(
            P("shard", "seq", None),
            P("shard"),
            P("shard", None),
            P("shard", None),
            P("shard"),
            P("shard", None),
            P("shard", None),
            P("shard", None),
            P("shard", "seq", None),
        ),
        out_specs=(
            P("shard", "seq", None),
            P("shard", "seq", None),
            P("shard"),
            P("shard", None),
            P("shard", None),
            P("shard"),
            P("shard", None),
            P("shard", None),
        ),
        check_vma=False,
    )
```

time: 549 us -> 272 us (0.50)
  waiting for transfers between devices: 324 us -> 101 us
  blocking collectives: 129 us -> 10.6 us
  starting transfers between devices: 7.25 us -> 76.8 us
  matrix products: 58.5 us -> 13.1 us
  other arithmetic: 6.39 us -> 22 us
  Pallas kernels: 0 us -> 14.9 us
  local copies, waits for them, and re-layouts: 7.33 us -> 13.8 us
    all_gather x3 -> x0, waiting for transfers between devices: 160 us -> none  [the longest x1 68.8 us: shards(): lax.all_gather(w_in, 'shard', axis=0, tiled=True)]
    reduce_scatter x4 -> x0, waiting for transfers between devices: 140 us -> none  [the longest x1 69.1 us: shards(): lax.psum_scatter(grad_qkv.astype(jnp.bfloat16), 'shard', scatter_dimensio...]
    psum x1 -> x0, blocking collectives: 105 us -> none  [shards(): lax.psum((owned[0], owned[1], owned[2], owned[3], owned[4], owned[5]), 's...]
    ppermute x4 -> x64, waiting for transfers between devices: 3.21 us -> 101 us  [the longest x41 40.5 us: swap_seq(): return lax.ppermute(value, 'seq', [(i, i ^ bits) for i in range(count)])]
    ppermute x4 -> x64, starting transfers between devices: 6.76 us -> 76.8 us  [the longest x41 35.2 us: swap_seq(): return lax.ppermute(value, 'seq', [(i, i ^ bits) for i in range(count)])]
    dot_general x18 -> x12, matrix products: 58.5 us -> 13.1 us  [the longest x3 5.93 us: dot_t(): lax.dot_general(left, right, (((1,), (1,)), ((), ())), preferred_element_...]
    unnamed x2 -> x0, blocking collectives: 24.4 us -> none
    all_gather x1, waiting for transfers between devices: 17.2 us -> 0.01 us  [shards(): lax.all_gather(w_out, 'shard', axis=0, tiled=True)]
  transfers between devices with their start and end apart: 12 -> 65, of which waited for: 8 -> 28; matrix products, arithmetic and copies ran while one was open for 11% -> 14% of each run, Pallas kernels for 0% -> 6%
where the time goes in v1:
time: 272 us; the launch traced here: 271 us
  waiting for transfers between devices  101 us (37%)
  starting transfers between devices  76.8 us (28%)
  other arithmetic  22 us (8%)
  between operations  18.1 us (7%)
  Pallas kernels  14.9 us (5%)
  local copies, waits for them, and re-layouts  13.8 us (5%)
  matrix products  13.1 us (5%)
  blocking collectives  10.6 us (4%)
    ppermute x41, waiting for transfers between devices, swap_seq(): return lax.ppermute(value, 'seq', [(i, i ^ bits) for i in range(count)])  40.5 us
    ppermute x14, waiting for transfers between devices, swap_shard(): return lax.ppermute(value, 'shard', [(i, i ^ bits) for i in range(count)])  38.6 us
    ppermute x41, starting transfers between devices, swap_seq(): return lax.ppermute(value, 'seq', [(i, i ^ bits) for i in range(count)])  35.2 us
    ppermute x14, starting transfers between devices, swap_shard(): return lax.ppermute(value, 'shard', [(i, i ^ bits) for i in range(count)])  23.7 us
    ppermute x3, waiting for transfers between devices, reduce_rows(): pieces.append(lax.ppermute(total, ('seq', 'shard'), pairs))  13.3 us
    all_gather x1, blocking collectives, shards(): lax.all_gather(jnp.stack([norm_gain, ffn_gain]), 'shard', axis=1, tiled=T...  10.6 us
    ppermute x3, starting transfers between devices, gather_rows(): pieces.append(lax.ppermute(piece, ('seq', 'shard'), pairs))  9.39 us
    pallas_call x1, Pallas kernels, shards(): pl.pallas_call(attend_back_kernel, grid=(CHIPS,), in_specs=[block_spec(le...  8.92 us
  transfers between devices with their start and end apart: 65, of which 28 were waited for; matrix products, arithmetic and copies ran while one was open for 14% of the time, Pallas kernels for 6%

profile of v1, /device:TPU:0, one launch (start us, length us, event | category | flops | bytes accessed | tf_op | source)
XLA Modules:
  0.0 270.8 jit_solution(7934847439627835125)
XLA Ops:
  9.0 4.1 %collective-permute-start.12 = (bf16[96,576]{1,0:T(8,128)(2,1)S(1)}, bf16[96,576]{1,0:T(8,128)(2,1)S(1)}, u32[]{:S(2)}, u32[]{:S(2)}) collective-permute-start(bf16[96,576]{1,0:T(8,128)(2,1)S(1)} %fusion.121), channel_id=1, source_target_pairs={{0,2},{1,3},{2,0},{3,1},{4,6},{5,7},{6,4},{7,5},{8,10},{9,11},{10,... | collective-permute-start | bytes 331784 | tf_op jit(solution)/shard_map/ppermute | solution.py:42
  21.2 10.6 %all-gather = bf16[4,192,2]{1,2,0:T(2,128)(2,1)S(1)} all-gather(bf16[1,192,2]{1,2,0:T(2,128)(2,1)S(1)} %maximum_bitcast_fusion), channel_id=1, replica_groups=mesh['seq'=8,'shard'=4] {'shard'}, dimensions={0}, use_global_device_ids=true | all-gather | bytes 3840 | tf_op jit(solution)/shard_map/all_gather | solution.py:236
  39.3 12.4 %collective-permute-done.4 = bf16[96,576]{1,0:T(8,128)(2,1)S(1)} collective-permute-done((bf16[96,576]{1,0:T(8,128)(2,1)S(1)}, bf16[96,576]{1,0:T(8,128)(2,1)S(1)}, u32[]{:S(2)}, u32[]{:S(2)}) %collective-permute-start.4) | collective-permute-done | bytes 110624 | tf_op jit(solution)/shard_map/ppermute | solution.py:42
  52.7 6.8 %collective-permute-start.16 = (bf16[144,768]{1,0:T(8,128)(2,1)S(1)}, bf16[144,768]{1,0:T(8,128)(2,1)S(1)}, u32[]{:S(2)}, u32[]{:S(2)}) collective-permute-start(bf16[144,768]{1,0:T(8,128)(2,1)S(1)} %constant_dynamic-slice_fusion.2), channel_id=1, source_target_pairs={{0,2},{4,6},{9,11},{13,15},{18,16},{22,20},{27,25},{31,29}} | collective-permute-start | bytes 663560 | tf_op jit(solution)/shard_map/ppermute | solution.py:228
  66.6 3.4 %collective-permute-done.17 = bf16[144,768]{1,0:T(8,128)(2,1)S(1)} collective-permute-done((bf16[144,768]{1,0:T(8,128)(2,1)S(1)}, bf16[144,768]{1,0:T(8,128)(2,1)S(1)}, u32[]{:S(2)}, u32[]{:S(2)}) %collective-permute-start.17) | collective-permute-done | bytes 221216 | tf_op jit(solution)/shard_map/ppermute | solution.py:228
  70.0 3.3 %collective-permute-done.15 = bf16[144,768]{1,0:T(8,128)(2,1)S(1)} collective-permute-done((bf16[144,768]{1,0:T(8,128)(2,1)S(1)}, bf16[144,768]{1,0:T(8,128)(2,1)S(1)}, u32[]{:S(2)}, u32[]{:S(2)}) %collective-permute-start.15) | collective-permute-done | bytes 221216 | tf_op jit(solution)/shard_map/ppermute | solution.py:228
  80.0 3.8 %attend.1.attn = bf16[4,128,192]{2,1,0:T(8,128)(2,1)S(1)} custom-call(bf16[4,128,192]{2,1,0:T(8,128)(2,1)S(1)} %bitcast.194, bf16[4,256,384]{2,1,0:T(8,128)(2,1)S(1)} %maximum_maximum_fusion.kv, f32[4,128,256]{2,1,0:T(8,128)S(1)} %and_select_fusion.bias), custom_call_target="tpu_custom_call" | custom-call | flops 100663296 | bytes 2000000 | tf_op jit(solution)/shard_map/attend/pallas_call | solution.py:307
  87.3 6.2 %collective-permute-done.10 = bf16[4,128,192]{2,1,0:T(8,128)(2,1)S(1)} collective-permute-done((bf16[4,128,192]{2,1,0:T(8,128)(2,1)S(1)}, bf16[4,128,192]{2,1,0:T(8,128)(2,1)S(1)}, u32[]{:S(2)}, u32[]{:S(2)}) %collective-permute-start.10) | collective-permute-done | bytes 196640 | tf_op jit(solution)/shard_map/ppermute | solution.py:37
  94.2 4.9 %collective-permute-done.9 = bf16[4,128,192]{2,1,0:T(8,128)(2,1)S(1)} collective-permute-done((bf16[4,128,192]{2,1,0:T(8,128)(2,1)S(1)}, bf16[4,128,192]{2,1,0:T(8,128)(2,1)S(1)}, u32[]{:S(2)}, u32[]{:S(2)}) %collective-permute-start.9) | collective-permute-done | bytes 196640 | tf_op jit(solution)/shard_map/ppermute | solution.py:37
  122.8 4.8 %collective-permute-done.27 = bf16[128,768]{1,0:T(8,128)(2,1)S(1)} collective-permute-done((bf16[128,768]{1,0:T(8,128)(2,1)S(1)}, bf16[128,768]{1,0:T(8,128)(2,1)S(1)}, u32[]{:S(2)}, u32[]{:S(2)}) %collective-permute-start.27) | collective-permute-done | bytes 196640 | tf_op jit(solution)/shard_map/ppermute | solution.py:37
  127.8 6.0 %collective-permute-done.26 = bf16[128,768]{1,0:T(8,128)(2,1)S(1)} collective-permute-done((bf16[128,768]{1,0:T(8,128)(2,1)S(1)}, bf16[128,768]{1,0:T(8,128)(2,1)S(1)}, u32[]{:S(2)}, u32[]{:S(2)}) %collective-permute-start.26) | collective-permute-done | bytes 196640 | tf_op jit(solution)/shard_map/ppermute | solution.py:37
  140.1 4.4 %collective-permute-done.30 = bf16[128,768]{1,0:T(8,128)(2,1)S(1)} collective-permute-done((bf16[128,768]{1,0:T(8,128)(2,1)S(1)}, bf16[128,768]{1,0:T(8,128)(2,1)S(1)}, u32[]{:S(2)}, u32[]{:S(2)}) %collective-permute-start.30) | collective-permute-done | bytes 196640 | tf_op jit(solution)/shard_map/ppermute | solution.py:37
  144.5 3.8 %collective-permute-done.29 = bf16[128,768]{1,0:T(8,128)(2,1)S(1)} collective-permute-done((bf16[128,768]{1,0:T(8,128)(2,1)S(1)}, bf16[128,768]{1,0:T(8,128)(2,1)S(1)}, u32[]{:S(2)}, u32[]{:S(2)}) %collective-permute-start.29) | collective-permute-done | bytes 196640 | tf_op jit(solution)/shard_map/ppermute | solution.py:37
  148.7 8.9 %attend_back.1 = (f32[4,128,192]{2,1,0:T(8,128)S(1)}, f32[4,256,384]{2,1,0:T(8,128)S(1)}, f32[192,768]{1,0:T(8,128)S(1)}) custom-call(bf16[4,128,192]{2,1,0:T(8,128)(2,1)S(1)} %bitcast.195, bf16[4,256,384]{2,1,0:T(8,128)(2,1)S(1)} %maximum_maximum_fusion.kv, f32[4,128,256]{2,1,0:T(8,128)S(1)} %and_select_fusion.bias, ...), custom_call_target="tpu_custom_call" | custom-call | flops 251658240 | bytes 4000000 | tf_op jit(solution)/shard_map/attend_back/pallas_call | solution.py:358
  162.9 3.6 %collective-permute-done.59 = bf16[96,576]{1,0:T(8,128)(2,1)S(1)} collective-permute-done((bf16[96,576]{1,0:T(8,128)(2,1)S(1)}, bf16[96,576]{1,0:T(8,128)(2,1)S(1)}, u32[]{:S(2)}, u32[]{:S(2)}) %collective-permute-start.59) | collective-permute-done | bytes 110624 | tf_op jit(solution)/shard_map/ppermute | solution.py:42
  166.5 6.8 %collective-permute-done.58 = bf16[96,576]{1,0:T(8,128)(2,1)S(1)} collective-permute-done((bf16[96,576]{1,0:T(8,128)(2,1)S(1)}, bf16[96,576]{1,0:T(8,128)(2,1)S(1)}, u32[]{:S(2)}, u32[]{:S(2)}) %collective-permute-start.58) | collective-permute-done | bytes 110624 | tf_op jit(solution)/shard_map/ppermute | solution.py:42
  193.8 3.5 %collective-permute-start.34 = (bf16[128,768]{1,0:T(8,128)(2,1)S(1)}, bf16[128,768]{1,0:T(8,128)(2,1)S(1)}, u32[]{:S(2)}, u32[]{:S(2)}) collective-permute-start(bf16[128,768]{1,0:T(8,128)(2,1)S(1)} %get-tuple-element.89), channel_id=1, source_target_pairs={{0,24},{4,28},{8,16},{12,20},{16,8},{20,12},{24,0},{28,4},{1,25},{... | collective-permute-start | bytes 589832 | tf_op jit(solution)/shard_map/ppermute | solution.py:37
  200.2 4.9 %collective-permute-done.38 = f32[2,768]{1,0:T(2,128)S(1)} collective-permute-done((f32[2,768]{1,0:T(2,128)S(1)}, f32[2,768]{1,0:T(2,128)S(1)}, u32[]{:S(2)}, u32[]{:S(2)}) %collective-permute-start.38) | collective-permute-done | bytes 6176 | tf_op jit(solution)/shard_map/ppermute | solution.py:42
  217.7 3.5 %collective-permute-start.43 = (bf16[96,576]{1,0:T(8,128)(2,1)S(1)}, bf16[96,576]{1,0:T(8,128)(2,1)S(1)}, u32[]{:S(2)}, u32[]{:S(2)}) collective-permute-start(bf16[96,576]{1,0:T(8,128)(2,1)S(1)} %get-tuple-element.57), channel_id=1, source_target_pairs={{0,3},{1,2},{2,1},{3,0},{4,7},{5,6},{6,5},{7,4},{8,11},{9,10},{10,... | collective-permute-start | bytes 331784 | tf_op jit(solution)/shard_map/ppermute | solution.py:42
  221.4 4.4 %collective-permute-done.43 = bf16[96,576]{1,0:T(8,128)(2,1)S(1)} collective-permute-done((bf16[96,576]{1,0:T(8,128)(2,1)S(1)}, bf16[96,576]{1,0:T(8,128)(2,1)S(1)}, u32[]{:S(2)}, u32[]{:S(2)}) %collective-permute-start.43) | collective-permute-done | bytes 110624 | tf_op jit(solution)/shard_map/ppermute | solution.py:42
  225.8 4.4 %collective-permute-start.41 = (bf16[96,576]{1,0:T(8,128)(2,1)S(1)}, bf16[96,576]{1,0:T(8,128)(2,1)S(1)}, u32[]{:S(2)}, u32[]{:S(2)}) collective-permute-start(bf16[96,576]{1,0:T(8,128)(2,1)S(1)} %get-tuple-element.55), channel_id=1, source_target_pairs={{0,1},{1,0},{2,3},{3,2},{4,5},{5,4},{6,7},{7,6},{8,9},{9,8},{10,11... | collective-permute-start | bytes 331784 | tf_op jit(solution)/shard_map/ppermute | solution.py:42
  232.0 3.6 %collective-permute-done.41 = bf16[96,576]{1,0:T(8,128)(2,1)S(1)} collective-permute-done((bf16[96,576]{1,0:T(8,128)(2,1)S(1)}, bf16[96,576]{1,0:T(8,128)(2,1)S(1)}, u32[]{:S(2)}, u32[]{:S(2)}) %collective-permute-start.41) | collective-permute-done | bytes 110624 | tf_op jit(solution)/shard_map/ppermute | solution.py:42
  245.4 5.6 %collective-permute-done.53 = bf16[240,768]{1,0:T(8,128)(2,1)S(1)} collective-permute-done((bf16[240,768]{1,0:T(8,128)(2,1)S(1)}, bf16[240,768]{1,0:T(8,128)(2,1)S(1)}, u32[]{:S(2)}, u32[]{:S(2)}) %collective-permute-start.53) | collective-permute-done | bytes 368672 | tf_op jit(solution)/shard_map/ppermute | solution.py:460
  252.8 5.9 %collective-permute-done.52 = bf16[240,768]{1,0:T(8,128)(2,1)S(1)} collective-permute-done((bf16[240,768]{1,0:T(8,128)(2,1)S(1)}, bf16[240,768]{1,0:T(8,128)(2,1)S(1)}, u32[]{:S(2)}, u32[]{:S(2)}) %collective-permute-start.52) | collective-permute-done | bytes 368672 | tf_op jit(solution)/shard_map/ppermute | solution.py:460
  (334 shorter events, 123.1 us)
Async XLA Ops:
  7.2 94.8 %all-gather.3.cloned.1.call-start = ((), (), s32[]{:S(2)}) async-start(), calls=%async_computation | async-start | bytes 1474560 | tf_op jit(solution)/shard_map/all_gather | solution.py:239
  9.0 26.6 %collective-permute-start.12 = (bf16[96,576]{1,0:T(8,128)(2,1)S(1)}, bf16[96,576]{1,0:T(8,128)(2,1)S(1)}, u32[]{:S(2)}, u32[]{:S(2)}) collective-permute-start(bf16[96,576]{1,0:T(8,128)(2,1)S(1)} %fusion.121), channel_id=1, source_target_pairs={{0,2},{1,3},{2,0},{3,1},{4,6},{5,7},{6,4},{7,5},{8,10},{9,11},{10,... | collective-permute-start | bytes 331784 | tf_op jit(solution)/shard_map/ppermute | solution.py:42
  13.1 22.6 %collective-permute-start.13 = (bf16[96,576]{1,0:T(8,128)(2,1)S(1)}, bf16[96,576]{1,0:T(8,128)(2,1)S(1)}, u32[]{:S(2)}, u32[]{:S(2)}) collective-permute-start(bf16[96,576]{1,0:T(8,128)(2,1)S(1)} %fusion.121), channel_id=1, source_target_pairs={{0,3},{1,2},{2,1},{3,0},{4,7},{5,6},{6,5},{7,4},{8,11},{9,10},{10,... | collective-permute-start | bytes 331784 | tf_op jit(solution)/shard_map/ppermute | solution.py:42
  14.5 23.1 %collective-permute-start.11 = (bf16[96,576]{1,0:T(8,128)(2,1)S(1)}, bf16[96,576]{1,0:T(8,128)(2,1)S(1)}, u32[]{:S(2)}, u32[]{:S(2)}) collective-permute-start(bf16[96,576]{1,0:T(8,128)(2,1)S(1)} %fusion.121), channel_id=1, source_target_pairs={{0,1},{1,0},{2,3},{3,2},{4,5},{5,4},{6,7},{7,6},{8,9},{9,8},{10,11... | collective-permute-start | bytes 331784 | tf_op jit(solution)/shard_map/ppermute | solution.py:42
  14.7 46.4 %collective-permute-start = (bf16[128,768]{1,0:T(8,128)(2,1)S(1)}, bf16[128,768]{1,0:T(8,128)(2,1)S(1)}, u32[]{:S(2)}, u32[]{:S(2)}) collective-permute-start(bf16[128,768]{1,0:T(8,128)(2,1)S(1)} %bitcast.183), channel_id=1, source_target_pairs={{0,8},{4,12},{8,0},{12,4},{16,24},{20,28},{24,16},{28,20},{1,9},{5... | collective-permute-start | bytes 589832 | tf_op jit(solution)/shard_map/ppermute | solution.py:37
  16.2 46.2 %collective-permute-start.1 = (bf16[128,768]{1,0:T(8,128)(2,1)S(1)}, bf16[128,768]{1,0:T(8,128)(2,1)S(1)}, u32[]{:S(2)}, u32[]{:S(2)}) collective-permute-start(bf16[128,768]{1,0:T(8,128)(2,1)S(1)} %bitcast.184), channel_id=1, source_target_pairs={{0,16},{4,20},{8,24},{12,28},{16,0},{20,4},{24,8},{28,12},{1,17},{... | collective-permute-start | bytes 589832 | tf_op jit(solution)/shard_map/ppermute | solution.py:37
  35.7 16.0 %collective-permute-start.4 = (bf16[96,576]{1,0:T(8,128)(2,1)S(1)}, bf16[96,576]{1,0:T(8,128)(2,1)S(1)}, u32[]{:S(2)}, u32[]{:S(2)}) collective-permute-start(bf16[96,576]{1,0:T(8,128)(2,1)S(1)} %fusion.120), channel_id=1, source_target_pairs={{0,2},{1,3},{2,0},{3,1},{4,6},{5,7},{6,4},{7,5},{8,10},{9,11},{10,... | collective-permute-start | bytes 331784 | tf_op jit(solution)/shard_map/ppermute | solution.py:42
  35.8 16.9 %collective-permute-start.5 = (bf16[96,576]{1,0:T(8,128)(2,1)S(1)}, bf16[96,576]{1,0:T(8,128)(2,1)S(1)}, u32[]{:S(2)}, u32[]{:S(2)}) collective-permute-start(bf16[96,576]{1,0:T(8,128)(2,1)S(1)} %fusion.120), channel_id=1, source_target_pairs={{0,3},{1,2},{2,1},{3,0},{4,7},{5,6},{6,5},{7,4},{8,11},{9,10},{10,... | collective-permute-start | bytes 331784 | tf_op jit(solution)/shard_map/ppermute | solution.py:42
  37.5 21.9 %collective-permute-start.3 = (bf16[96,576]{1,0:T(8,128)(2,1)S(1)}, bf16[96,576]{1,0:T(8,128)(2,1)S(1)}, u32[]{:S(2)}, u32[]{:S(2)}) collective-permute-start(bf16[96,576]{1,0:T(8,128)(2,1)S(1)} %fusion.120), channel_id=1, source_target_pairs={{0,1},{1,0},{2,3},{3,2},{4,5},{5,4},{6,7},{7,6},{8,9},{9,8},{10,11... | collective-permute-start | bytes 331784 | tf_op jit(solution)/shard_map/ppermute | solution.py:42
  62.4 46.5 %collective-permute-start.24 = (bf16[128,768]{1,0:T(8,128)(2,1)}, bf16[128,768]{1,0:T(8,128)(2,1)}, u32[]{:S(2)}, u32[]{:S(2)}) collective-permute-start(bf16[128,768]{1,0:T(8,128)(2,1)} %bitcast.49), channel_id=1, source_target_pairs={{0,24},{4,28},{8,16},{12,20},{16,8},{20,12},{24,0},{28,4},{1,25},{... | collective-permute-start | bytes 589832 | tf_op jit(solution)/shard_map/ppermute | solution.py:37
  62.5 46.4 %collective-permute-start.23 = (bf16[128,768]{1,0:T(8,128)(2,1)}, bf16[128,768]{1,0:T(8,128)(2,1)}, u32[]{:S(2)}, u32[]{:S(2)}) collective-permute-start(bf16[128,768]{1,0:T(8,128)(2,1)} %bitcast.49), channel_id=1, source_target_pairs={{0,16},{4,20},{8,24},{12,28},{16,0},{20,4},{24,8},{28,12},{1,17},{... | collective-permute-start | bytes 589832 | tf_op jit(solution)/shard_map/ppermute | solution.py:37
  65.3 43.6 %collective-permute-start.22 = (bf16[128,768]{1,0:T(8,128)(2,1)}, bf16[128,768]{1,0:T(8,128)(2,1)}, u32[]{:S(2)}, u32[]{:S(2)}) collective-permute-start(bf16[128,768]{1,0:T(8,128)(2,1)} %bitcast.49), channel_id=1, source_target_pairs={{0,8},{4,12},{8,0},{12,4},{16,24},{20,28},{24,16},{28,20},{1,9},{5... | collective-permute-start | bytes 589832 | tf_op jit(solution)/shard_map/ppermute | solution.py:37
  114.7 22.9 %collective-permute-start.21 = (bf16[128,768]{1,0:T(8,128)(2,1)S(1)}, bf16[128,768]{1,0:T(8,128)(2,1)S(1)}, u32[]{:S(2)}, u32[]{:S(2)}) collective-permute-start(bf16[128,768]{1,0:T(8,128)(2,1)S(1)} %get-tuple-element.103), channel_id=1, source_target_pairs={{0,24},{4,28},{8,16},{12,20},{16,8},{20,12},{24,0},{28,4},{1,25},{... | collective-permute-start | bytes 589832 | tf_op jit(solution)/shard_map/ppermute | solution.py:37
  117.4 20.5 %collective-permute-start.20 = (bf16[128,768]{1,0:T(8,128)(2,1)S(1)}, bf16[128,768]{1,0:T(8,128)(2,1)S(1)}, u32[]{:S(2)}, u32[]{:S(2)}) collective-permute-start(bf16[128,768]{1,0:T(8,128)(2,1)S(1)} %get-tuple-element.104), channel_id=1, source_target_pairs={{0,16},{4,20},{8,24},{12,28},{16,0},{20,4},{24,8},{28,12},{1,17},{... | collective-permute-start | bytes 589832 | tf_op jit(solution)/shard_map/ppermute | solution.py:37
  119.3 14.5 %collective-permute-start.26 = (bf16[128,768]{1,0:T(8,128)(2,1)S(1)}, bf16[128,768]{1,0:T(8,128)(2,1)S(1)}, u32[]{:S(2)}, u32[]{:S(2)}) collective-permute-start(bf16[128,768]{1,0:T(8,128)(2,1)S(1)} %get-tuple-element.101), channel_id=1, source_target_pairs={{0,16},{4,20},{8,24},{12,28},{16,0},{20,4},{24,8},{28,12},{1,17},{... | collective-permute-start | bytes 589832 | tf_op jit(solution)/shard_map/ppermute | solution.py:37
  133.8 24.4 %collective-permute-start.56 = (bf16[4,96,576]{2,1,0:T(8,128)(2,1)S(1)}, bf16[4,96,576]{2,1,0:T(8,128)(2,1)S(1)}, u32[]{:S(2)}, u32[]{:S(2)}) collective-permute-start(bf16[4,96,576]{2,1,0:T(8,128)(2,1)S(1)} %fusion.18), channel_id=1, source_target_pairs={{0,4},{4,0},{8,12},{12,8},{16,20},{20,16},{24,28},{28,24},{1,5},{5... | collective-permute-start | bytes 1327112 | tf_op jit(solution)/shard_map/ppermute | solution.py:37
  158.1 25.4 %collective-permute-start.31 = (bf16[4,128,384]{2,1,0:T(8,128)(2,1)S(1)}, bf16[4,128,384]{2,1,0:T(8,128)(2,1)S(1)}, u32[]{:S(2)}, u32[]{:S(2)}) collective-permute-start(bf16[4,128,384]{2,1,0:T(8,128)(2,1)S(1)} %pad_maximum_fusion.11), channel_id=1, source_target_pairs={{0,4},{4,0},{8,12},{12,8},{16,20},{20,16},{24,28},{28,24},{1,5},{5... | collective-permute-start | bytes 1179656 | tf_op jit(solution)/shard_map/ppermute | solution.py:37
  188.0 33.1 %collective-permute-start.63 = (bf16[96,2304]{1,0:T(8,128)(2,1)S(1)}, bf16[96,2304]{1,0:T(8,128)(2,1)S(1)}, u32[]{:S(2)}, u32[]{:S(2)}) collective-permute-start(bf16[96,2304]{1,0:T(8,128)(2,1)S(1)} %concatenate.227), channel_id=1, source_target_pairs={{0,4},{4,0},{8,12},{12,8},{16,20},{20,16},{24,28},{28,24},{1,5},{5... | collective-permute-start | bytes 1327112 | tf_op jit(solution)/shard_map/ppermute | solution.py:37
  191.4 45.5 %collective-permute-start.51 = (bf16[240,768]{1,0:T(8,128)(2,1)S(1)}, bf16[240,768]{1,0:T(8,128)(2,1)S(1)}, u32[]{:S(2)}, u32[]{:S(2)}) collective-permute-start(bf16[240,768]{1,0:T(8,128)(2,1)S(1)} %fusion.140), channel_id=1, source_target_pairs={{3,0},{7,4},{10,9},{14,13},{17,18},{21,22},{24,27},{28,31}} | collective-permute-start | bytes 1105928 | tf_op jit(solution)/shard_map/ppermute | solution.py:452
  193.8 16.5 %collective-permute-start.34 = (bf16[128,768]{1,0:T(8,128)(2,1)S(1)}, bf16[128,768]{1,0:T(8,128)(2,1)S(1)}, u32[]{:S(2)}, u32[]{:S(2)}) collective-permute-start(bf16[128,768]{1,0:T(8,128)(2,1)S(1)} %get-tuple-element.89), channel_id=1, source_target_pairs={{0,24},{4,28},{8,16},{12,20},{16,8},{20,12},{24,0},{28,4},{1,25},{... | collective-permute-start | bytes 589832 | tf_op jit(solution)/shard_map/ppermute | solution.py:37
  197.2 14.4 %collective-permute-start.33 = (bf16[128,768]{1,0:T(8,128)(2,1)S(1)}, bf16[128,768]{1,0:T(8,128)(2,1)S(1)}, u32[]{:S(2)}, u32[]{:S(2)}) collective-permute-start(bf16[128,768]{1,0:T(8,128)(2,1)S(1)} %get-tuple-element.90), channel_id=1, source_target_pairs={{0,16},{4,20},{8,24},{12,28},{16,0},{20,4},{24,8},{28,12},{1,17},{... | collective-permute-start | bytes 589832 | tf_op jit(solution)/shard_map/ppermute | solution.py:37
  210.3 28.9 %collective-permute-start.50 = (bf16[240,768]{1,0:T(8,128)(2,1)S(1)}, bf16[240,768]{1,0:T(8,128)(2,1)S(1)}, u32[]{:S(2)}, u32[]{:S(2)}) collective-permute-start(bf16[240,768]{1,0:T(8,128)(2,1)S(1)} %fusion.140), channel_id=1, source_target_pairs={{2,0},{6,4},{11,9},{15,13},{16,18},{20,22},{25,27},{29,31}} | collective-permute-start | bytes 1105928 | tf_op jit(solution)/shard_map/ppermute | solution.py:452
  211.6 27.6 %collective-permute-start.49 = (bf16[240,768]{1,0:T(8,128)(2,1)S(1)}, bf16[240,768]{1,0:T(8,128)(2,1)S(1)}, u32[]{:S(2)}, u32[]{:S(2)}) collective-permute-start(bf16[240,768]{1,0:T(8,128)(2,1)S(1)} %fusion.140), channel_id=1, source_target_pairs={{1,0},{5,4},{8,9},{12,13},{19,18},{23,22},{26,27},{30,31}} | collective-permute-start | bytes 1105928 | tf_op jit(solution)/shard_map/ppermute | solution.py:452
  243.8 14.9 %collective-permute-start.52 = (bf16[240,768]{1,0:T(8,128)(2,1)S(1)}, bf16[240,768]{1,0:T(8,128)(2,1)S(1)}, u32[]{:S(2)}, u32[]{:S(2)}) collective-permute-start(bf16[240,768]{1,0:T(8,128)(2,1)S(1)} %add_convert_fusion), channel_id=1, source_target_pairs={{0,8},{4,12},{9,1},{13,5},{18,26},{22,30},{27,19},{31,23}} | collective-permute-start | bytes 1105928 | tf_op jit(solution)/shard_map/ppermute | solution.py:460
  (81 other events, 720.2 us)
Sparse Core Ops, SparseCore 0:
  17.9 39.6 all-gather.2

commit v2 on v0

v2 whole, which is shorter than its diff:
```python
import functools

import jax
import jax.numpy as jnp
from jax import lax
from jax.experimental import pallas as pl
from jax.experimental.pallas import tpu as pltpu
from jax.sharding import PartitionSpec as P

HEADS = 12
HEAD_DIM = 64
FF = 1152
HALF = 64
CHIPS = 4
CORES = 2
MEMBERS = CHIPS * CORES
PLANES = 4
EXTRA = 16
f32 = jnp.float32
bf16 = jnp.bfloat16
SCALE = HEAD_DIM ** (-0.5)
VMEM = 20 * 1024 * 1024


def dot(left, right):
    return lax.dot_general(left, right, (((1,), (0,)), ((), ())), preferred_element_type=f32)


def dot_t(left, right):
    return lax.dot_general(left, right, (((1,), (1,)), ((), ())), preferred_element_type=f32)


def t_dot(left, right):
    return lax.dot_general(left, right, (((0,), (0,)), ((), ())), preferred_element_type=f32)


def swap_seq(value, bits):
    count = lax.axis_size("seq")
    return lax.ppermute(value, "seq", [(i, i ^ bits) for i in range(count)])


def swap_shard(value, bits):
    count = lax.axis_size("shard")
    return lax.ppermute(value, "shard", [(i, i ^ bits) for i in range(count)])


def swap_core(value):
    return swap_seq(value, 1)


def over_chips(value):
    return [value] + [swap_seq(value, CORES * j) for j in range(1, CHIPS)]


def over_planes(value):
    return [value] + [swap_shard(value, i) for i in range(1, PLANES)]


def shape(*dims, dtype=bf16):
    return jax.ShapeDtypeStruct(dims, dtype)


def places():
    me = lax.axis_index("seq")
    return (me % MEMBERS) // CORES, me % CORES, lax.axis_index("shard")


def call(kernel, name, outs, *operands, after=(), scratch=(), flops=1e6):
    taken = len(operands)
    specs = [pl.BlockSpec(memory_space=pltpu.VMEM)] * taken
    specs += [pl.BlockSpec(memory_space=pl.ANY)] * len(after)

    def body(*refs):
        kernel(places(), *refs[:taken], *refs[taken + len(after) :])

    moved = sum(o.size * o.dtype.itemsize for o in operands)
    return pl.pallas_call(
        body,
        out_shape=outs,
        in_specs=specs,
        out_specs=jax.tree.map(lambda _: pl.BlockSpec(memory_space=pltpu.VMEM), outs),
        scratch_shapes=list(scratch),
        cost_estimate=pl.CostEstimate(
            flops=int(flops), bytes_accessed=int(moved), transcendentals=0
        ),
        compiler_params=pltpu.CompilerParams(vmem_limit_bytes=VMEM),
        name=name,
    )(*operands, *after)


def norm_parts(values):
    center = values - jnp.mean(values, axis=-1, keepdims=True)
    factor = lax.rsqrt(jnp.mean(center * center, axis=-1, keepdims=True) + 1e-05)
    return center * factor, factor


def norm_inward(upward, gain, normed, factor):
    scaled = upward * gain
    return factor * (
        scaled
        - jnp.mean(scaled, axis=-1, keepdims=True)
        - normed * jnp.mean(scaled * normed, axis=-1, keepdims=True)
    )


def first_half(shape_of):
    return lax.broadcasted_iota(jnp.int32, shape_of, 1) % HEAD_DIM < HEAD_DIM // 2


def shifted(values):
    return pltpu.roll(values, 96, 1), pltpu.roll(values, 32, 1)


def rows_at(start, size):
    return pl.ds(pl.multiple_of(start, 16), size)


def extra_rows(first, second, lanes):
    row = lax.broadcasted_iota(jnp.int32, (EXTRA, lanes), 0)
    pad = jnp.zeros((1, lanes - first.shape[1]), f32)
    first = jnp.concatenate([first, pad], axis=1)
    second = jnp.concatenate([second, pad], axis=1)
    return jnp.where(row == 0, first, jnp.where(row == 1, second, 0.0))


def qkv_piece_kernel(where, w_qkv, gain_one, gain_two, out):
    half = w_qkv.shape[0] // CORES
    width = w_qkv.shape[1] // 3
    local = width // CHIPS
    rows = rows_at(where[1] * half, half)
    for b in range(CHIPS):

        @pl.when(where[0] == b)
        def _():
            for p in range(3):
                at = p * width + b * local
                out[:half, p * local : (p + 1) * local] = w_qkv[rows, at : at + local]

    out[half:, :] = extra_rows(
        gain_one[...].astype(f32)[None], gain_two[...].astype(f32)[None], 3 * local
    ).astype(bf16)


def ffn_piece_kernel(where, w_in, w_out, w_back, cotangent, out, upward):
    upward[...] = cotangent[...]
    half = w_in.shape[0] // CORES
    width = w_out.shape[1]
    units = FF // PLANES // CHIPS
    rows = rows_at(where[1] * half, half)
    lanes = width // CORES
    at_out = 2 * PLANES * units
    at_back = at_out + width
    out[:, at_out:at_back] = w_out[rows, :]
    out[units:, at_back:] = jnp.zeros((half - units, lanes), bf16)
    for b in range(CHIPS):

        @pl.when(where[0] == b)
        def _():
            for p in range(2):
                for z in range(PLANES):
                    at = p * FF + z * units * CHIPS + b * units
                    to = (p * PLANES + z) * units
                    out[:, to : to + units] = w_in[rows, at : at + units]
            for k in range(CORES):

                @pl.when(where[1] == k)
                def _():
                    out[:units, at_back:] = w_back[b * units : (b + 1) * units, k * lanes : (k + 1) * lanes]


def place_kernel(slot, where, p0, p1, p2, p3, out):
    for i, ref in enumerate((p0, p1, p2, p3)):
        out[where[slot] ^ i] = ref[...]


def qkv_kernel(where, x0, x1, x2, x3, mine, other, cos, sin, a_out, q_out, kv_out, w_out, g_out):
    rows = x0.shape[0]
    half = mine.shape[1] - EXTRA
    local = mine.shape[2] // 3
    share = CORES * half
    core = where[1]
    for z in range(PLANES):
        w_out[rows_at(z * share + core * half, half), :] = mine[z, :half, :]
        w_out[rows_at(z * share + (1 - core) * half, half), :] = other[z, :half, :]
        tail = mine[z, half:, :share].astype(f32)
        g_out[:, z * share : (z + 1) * share] = tail[:8]
    gain = g_out[0:1, :]
    for j, ref in enumerate((x0, x1, x2, x3)):
        normed, _ = norm_parts(ref[...].astype(f32))
        a_out[j * rows : (j + 1) * rows, :] = (normed * gain).astype(bf16)
    out = dot(a_out[...], w_out[...])
    front = first_half((CHIPS * rows, 128))
    parts = []
    for at in range(0, 2 * local, 128):
        u = out[:, at : at + 128]
        up, down = shifted(u)
        parts.append((u * cos[...] + jnp.where(front, -up, down) * sin[...]).astype(bf16))
    qk = jnp.concatenate(parts, axis=1)
    value = out[:, 2 * local :].astype(bf16)
    for j in range(CHIPS):
        at = slice(j * rows, (j + 1) * rows)
        q_out[j] = qk[at, :local]
        kv_out[j, :, :local] = qk[at, local:]
        kv_out[j, :, local:] = value[at]


def extended(where, j, kv, other, rim):
    chip, core = where[0], where[1]
    length = kv.shape[1]
    b = chip ^ j
    below = jnp.where(core == 0, jnp.maximum(b - 1, 0), b) ^ chip
    above = jnp.where(core == 0, b, jnp.minimum(b + 1, CHIPS - 1)) ^ chip
    before = other[below, length - HALF :, :]
    after = other[above, :HALF, :]
    if rim is not None:
        before = jnp.where((core == 0) & (b == 0), rim[...], before)
        after = jnp.where((core == 1) & (b == CHIPS - 1), rim[...], after)
    return jnp.concatenate([before, kv[j], after], axis=0)


def probs_of(q, k, bias):
    logits = dot_t(q, k) * SCALE + bias
    highest = jnp.max(logits, axis=-1, keepdims=True)
    exponent = jnp.exp(logits - highest)
    return exponent / jnp.sum(exponent, axis=-1, keepdims=True)


def attend_kernel(edges, where, q, kv, other, bias, *rest):
    rim, out = rest if edges else (None, rest[0])
    local = q.shape[-1]
    for j in range(CHIPS):
        ext = extended(where, j, kv, other, rim)
        parts = []
        for h in range(local // HEAD_DIM):
            lanes = slice(h * HEAD_DIM, (h + 1) * HEAD_DIM)
            prob = probs_of(q[j, :, lanes], ext[:, lanes], bias[j]).astype(bf16)
            parts.append(dot(prob, ext[:, local + h * HEAD_DIM : local + (h + 1) * HEAD_DIM]))
        out[j] = jnp.concatenate(parts, axis=1).astype(bf16)


def ffn_kernel(
    where, t0, t1, t2, t3, x0, x1, x2, x3, y0, y1, y2, y3, mine, other, gains,
    own_out, d1_out, d2_out, d3_out, hid_out, a_out, m_out, dgu_out, gain_out, wb_out, wc_out,
    wi, wo,
):
    chip, core = where[0], where[1]
    rows = x0.shape[0]
    width = x0.shape[1]
    half = mine.shape[1]
    share = CORES * half
    units = FF // CHIPS
    part = units // PLANES
    lanes = width // CORES
    local = width // CHIPS
    at_out, at_back = 2 * units, 2 * units + width
    for z in range(PLANES):
        for k, ref in ((core, mine), (1 - core, other)):
            wi[rows_at(z * share + k * half, half), :] = ref[z, :, :at_out]
            wo[rows_at(z * share + k * half, half), :] = ref[z, :, at_out:at_back]
    own_back = jnp.concatenate([mine[z, :part, at_back:] for z in range(PLANES)], axis=0)
    other_back = jnp.concatenate([other[z, :part, at_back:] for z in range(PLANES)], axis=0)
    wb_out[:, :lanes] = jnp.where(core == 0, own_back, other_back)
    wb_out[:, lanes:] = jnp.where(core == 0, other_back, own_back)
    wc_out[...] = wo[rows_at(chip * local, local), :]
    xs = (x0, x1, x2, x3)
    gain = gains[1:2, :]
    outward = [
        (ref, wo[rows_at((chip ^ i) * local, local), :]) for i, ref in enumerate((t0, t1, t2, t3))
    ]
    normed = []
    for j in range(CHIPS):
        hidden = xs[j][...].astype(f32)
        for i, (ref, weight) in enumerate(outward):
            hidden = hidden + dot(ref[j ^ i], weight)
        if j == 0:
            hid_out[...] = hidden
        norm, _ = norm_parts(hidden)
        normed.append(norm)
        a_out[j * rows : (j + 1) * rows, :] = (norm * gain).astype(bf16)
    total = jnp.zeros((1, width), f32)
    for j in range(CHIPS):
        at = slice(j * rows, (j + 1) * rows)
        gu = dot(a_out[at, :], wi[...])
        entering, gating = gu[:, :units], gu[:, units:]
        rise = 0.5 * (1.0 + lax.erf(entering * (0.5**0.5)))
        slope = rise + entering * jnp.exp(-0.5 * entering * entering) * 0.3989422804014327
        act = entering * rise
        m_out[at, :] = (act * gating).astype(bf16)
        dm = dot_t((y0, y1, y2, y3)[j][...], wb_out[...])
        dgu = jnp.concatenate([dm * gating * slope, dm * act], axis=1).astype(bf16)
        dgu_out[at, :] = dgu
        da = dot_t(dgu, wi[...])
        total = total + jnp.sum(da * normed[j], axis=0, keepdims=True)
        if j == 0:
            own_out[...] = da
        else:
            (d1_out, d2_out, d3_out)[j - 1][...] = da.astype(bf16)
    gain_out[...] = jnp.broadcast_to(total, gain_out.shape)


def ffn_grads_kernel(where, a, m, dgu, y0, y1, y2, y3, wb, keep, away, mixed_own, m1, m2, m3, gin, gb):
    core = where[1]
    rows = y0.shape[0]
    half = keep.shape[1]
    share = CORES * half
    units = m.shape[1]
    part = units // PLANES
    lanes = y0.shape[1] // CORES
    gin[...] = t_dot(a[...], dgu[...])
    upward = jnp.concatenate([ref[...] for ref in (y0, y1, y2, y3)], axis=0)
    back = t_dot(m[...], upward)
    first, second = back[:, :lanes], back[:, lanes:]
    gb[0] = jnp.where(core == 0, first, second)
    gb[1] = jnp.where(core == 0, second, first)
    for z in range(PLANES):
        at = slice(z * part, (z + 1) * part)
        blank = jnp.zeros((half - part, lanes), f32)
        keep[z, :, : 2 * units] = gin[rows_at(z * share + core * half, half), :]
        keep[z, :, 2 * units :] = jnp.concatenate([gb[0, at, :], blank], axis=0)
        away[z, :, : 2 * units] = gin[rows_at(z * share + (1 - core) * half, half), :].astype(bf16)
        away[z, :, 2 * units :] = jnp.concatenate([gb[1, at, :], blank], axis=0).astype(bf16)
    mixed_own[...] = dot(m[:rows, :], wb[...])
    for j, ref in enumerate((m1, m2, m3)):
        ref[...] = dot(m[(j + 1) * rows : (j + 2) * rows, :], wb[...]).astype(bf16)


def dh_kernel(where, own, r1, r2, r3, y0, hidden, gains, dh_out, low_out):
    total = own[...] + r1[...].astype(f32) + r2[...].astype(f32) + r3[...].astype(f32)
    normed, factor = norm_parts(hidden[...])
    dh = y0[...].astype(f32) + norm_inward(total, gains[1:2, :], normed, factor)
    dh_out[...] = dh
    low_out[...] = dh.astype(bf16)


def attend_back_kernel(edges, where, q, kv, other, bias, h0, h1, h2, h3, w_out, *rest):
    rim, rest = (rest[0], rest[1:]) if edges else (None, rest)
    dq_out, dkv_out, back_out = rest[:3]
    chip, core = where[0], where[1]
    local = q.shape[-1]
    length = q.shape[1]
    back_out[...] = jnp.zeros_like(back_out)
    for j, dh in enumerate((h0, h1, h2, h3)):
        dctx = dot_t(dh[...], w_out[...]).astype(bf16)
        ext = extended(where, j, kv, other, rim)
        dqs, dks, dvs = [], [], []
        for h in range(local // HEAD_DIM):
            lanes = slice(h * HEAD_DIM, (h + 1) * HEAD_DIM)
            qh = q[j, :, lanes]
            kh = ext[:, lanes]
            vh = ext[:, local + h * HEAD_DIM : local + (h + 1) * HEAD_DIM]
            dch = dctx[:, lanes]
            prob = probs_of(qh, kh, bias[j])
            dprob = dot_t(dch, vh)
            inner = jnp.sum(prob * dprob, axis=-1, keepdims=True)
            dscore = (prob * (dprob - inner) * SCALE).astype(bf16)
            dqs.append(dot(dscore, kh))
            dks.append(t_dot(dscore, qh))
            dvs.append(t_dot(prob.astype(bf16), dch))
        dq_out[j] = jnp.concatenate(dqs, axis=1)
        grads = jnp.concatenate(dks + dvs, axis=1)
        dkv_out[j] = grads[HALF : HALF + length]
        before = grads[:HALF].astype(bf16)
        after = grads[HALF + length :].astype(bf16)
        b = chip ^ j
        below = jnp.where(core == 0, b - 1, b)
        above = jnp.where(core == 0, b, b + 1)

        @pl.when(below >= 0)
        def _():
            back_out[jnp.maximum(below, 0) ^ chip, length - HALF :, :] = before

        @pl.when(above < CHIPS)
        def _():
            back_out[jnp.minimum(above, CHIPS - 1) ^ chip, :HALF, :] = after

        if edges:
            rim_out = rest[3]

            @pl.when(below < 0)
            def _():
                rim_out[...] = before

            @pl.when(above >= CHIPS)
            def _():
                rim_out[...] = after


def qkv_grads_kernel(edges, where, dq, dkv, back, cos, sin, a, t0, t1, t2, t3, h0, h1, h2, h3, *rest):
    rim, rest = (rest[0], rest[1:]) if edges else (None, rest)
    keep, away, d_out, acc, cols = rest
    chip, core = where[0], where[1]
    length = dq.shape[1]
    local = dq.shape[2]
    width = a.shape[1]
    front = first_half((length, 128))
    for j in range(CHIPS):
        at = slice(j * length, (j + 1) * length)
        gkv = dkv[j] + back[j].astype(f32)
        if edges:
            b = chip ^ j
            blank = jnp.zeros((length - HALF, 2 * local), f32)
            value = rim[...].astype(f32)
            gkv = gkv + jnp.where(
                (core == 0) & (b == 0), jnp.concatenate([value, blank], axis=0), 0.0
            )
            gkv = gkv + jnp.where(
                (core == 1) & (b == CHIPS - 1), jnp.concatenate([blank, value], axis=0), 0.0
            )
        g = jnp.concatenate([dq[j], gkv[:, :local]], axis=1)
        for lane in range(0, 2 * local, 128):
            u = g[:, lane : lane + 128]
            up, down = shifted(u * sin[at, :])
            d_out[at, lane : lane + 128] = (
                u * cos[at, :] + jnp.where(front, up, -down)
            ).astype(bf16)
        d_out[at, 2 * local :] = gkv[:, local:].astype(bf16)
    acc[:, : 3 * local] = t_dot(a[...], d_out[...])
    for b in range(CHIPS):

        @pl.when(chip == b)
        def _():
            for j, ref in enumerate((h0, h1, h2, h3)):
                cols[j * length : (j + 1) * length, :] = ref[:, b * local : (b + 1) * local]

    for i, ref in enumerate((t0, t1, t2, t3)):
        rows = jnp.concatenate([ref[j ^ i] for j in range(CHIPS)], axis=0)
        acc[rows_at((chip ^ i) * local, local), 3 * local :] = t_dot(rows, cols[...])
    half = keep.shape[1]
    share = CORES * half
    for z in range(PLANES):
        keep[z] = acc[rows_at(z * share + core * half, half), :]
        away[z] = acc[rows_at(z * share + (1 - core) * half, half), :].astype(bf16)


def da_kernel(where, d, w, x0, x1, x2, x3, own_mixed, m1, m2, m3, gain_two, own_out, o1, o2, o3, gain_out):
    rows = x0.shape[0]
    total = jnp.zeros((1, w.shape[0]), f32)
    for j, ref in enumerate((x0, x1, x2, x3)):
        da = dot_t(d[j * rows : (j + 1) * rows, :], w[...])
        normed, _ = norm_parts(ref[...].astype(f32))
        total = total + jnp.sum(da * normed, axis=0, keepdims=True)
        if j == 0:
            own_out[:rows, :] = da
            own_out[rows:, :] = own_mixed[...]
        else:
            out = (o1, o2, o3)[j - 1]
            out[:rows, :] = da.astype(bf16)
            out[rows:, :] = (m1, m2, m3)[j - 1][...]
    share = w.shape[0] // PLANES
    for z in range(PLANES):
        at = slice(z * share, (z + 1) * share)
        gain_out[z] = extra_rows(total[:, at], gain_two[0:1, at], gain_out.shape[2])


def to_planes_kernel(where, keep, got, own, o1, o2, o3):
    plane = where[2]
    own[...] = keep[plane] + got[plane].astype(f32)
    for i, ref in enumerate((o1, o2, o3)):
        at = plane ^ (i + 1)
        ref[...] = (keep[at] + got[at].astype(f32)).astype(bf16)


def to_planes_gains_kernel(where, keep, got, gains, own, o1, o2, o3):
    plane = where[2]
    half = keep.shape[1]
    own[:half, :] = keep[plane] + got[plane].astype(f32)
    own[half:, :] = gains[plane]
    for i, ref in enumerate((o1, o2, o3)):
        at = plane ^ (i + 1)
        ref[:half, :] = (keep[at] + got[at].astype(f32)).astype(bf16)
        ref[half:, :] = gains[at].astype(bf16)


def sum_kernel(where, own, r1, r2, r3, out):
    total = own[...] + r1[...].astype(f32) + r2[...].astype(f32) + r3[...].astype(f32)
    out[...] = total.astype(out.dtype)


def last_kernel(where, own, r1, r2, r3, x0, dh, hidden, gains, mixed_out, grad_out):
    rows = dh.shape[0]
    total = own[...] + r1[...].astype(f32) + r2[...].astype(f32) + r3[...].astype(f32)
    mixed_out[0] = (hidden[...] + total[rows:, :]).astype(bf16)
    normed, factor = norm_parts(x0[...].astype(f32))
    grad = dh[...] + norm_inward(total[:rows, :], gains[0:1, :], normed, factor)
    grad_out[0] = grad.astype(bf16)


def ffn_owned_kernel(where, mine, other, in_out, back_out):
    core = where[1]
    half = mine.shape[1]
    units = FF // CHIPS
    part = units // PLANES
    lanes = mine.shape[2] - 2 * units
    for k, ref in ((core, mine), (1 - core, other)):
        rows = rows_at(k * half, half)
        for p in range(2):
            for z in range(PLANES):
                at = (p * PLANES + z) * part
                for b in range(CHIPS):
                    to = p * FF + (z * CHIPS + b) * part
                    in_out[rows, to : to + part] = ref[b, :, at : at + part].astype(f32)
    for b in range(CHIPS):
        own = mine[b, :part, 2 * units :].astype(f32)
        got = other[b, :part, 2 * units :].astype(f32)
        back_out[b * part : (b + 1) * part, :lanes] = jnp.where(core == 0, own, got)
        back_out[b * part : (b + 1) * part, lanes:] = jnp.where(core == 0, got, own)


def qkv_owned_kernel(where, mine, other, qkv_out, w_out, gain_out):
    core = where[1]
    half = mine.shape[1] - EXTRA
    local = w_out.shape[1] // CHIPS
    total = jnp.zeros((EXTRA, local), f32)
    for k, ref in ((core, mine), (1 - core, other)):
        rows = rows_at(k * half, half)
        for b in range(CHIPS):
            for p in range(3):
                to = (p * CHIPS + b) * local
                qkv_out[rows, to : to + local] = ref[b, :half, p * local : (p + 1) * local].astype(f32)
            w_out[rows, b * local : (b + 1) * local] = ref[b, :half, 3 * local :].astype(f32)
            total = total + ref[b, half:, :local].astype(f32)
    gain_out[...] = total


def shards(tokens, norm_gain, w_qkv, w_out, ffn_gain, w_in, w_back, seq_ids, cotangent):
    length, width = tokens.shape[1:]
    me = lax.axis_index("seq")
    seq_count = lax.axis_size("seq")
    edges = seq_count > MEMBERS
    group = me // MEMBERS
    chip = (me % MEMBERS) // CORES
    core = me % CORES
    local = width // CHIPS
    units = FF // CHIPS
    many = CHIPS * length
    half = width // PLANES // CORES
    lanes = width // CORES
    extent = length + 2 * HALF
    kept = half + EXTRA
    in_lanes = 2 * units + width + lanes
    ffn_lanes = 2 * units + lanes
    qkv_lanes = 4 * local

    piece = call(
        qkv_piece_kernel, "qkv_piece", shape(kept, 3 * local), w_qkv, norm_gain, ffn_gain
    )
    pieces = over_planes(piece)
    xs = over_chips(tokens[0])
    piece, upward = call(
        ffn_piece_kernel,
        "ffn_piece",
        (shape(half, in_lanes), shape(length, width)),
        w_in,
        w_out,
        w_back,
        cotangent[0],
        after=(piece,),
    )
    in_pieces = over_planes(piece)
    gys = over_chips(upward)
    mine = call(
        functools.partial(place_kernel, 2), "qkv_place", shape(PLANES, kept, 3 * local), *pieces
    )
    other = swap_core(mine)

    block = (group * CHIPS + (chip ^ jnp.arange(CHIPS))) * CORES + core
    position = (block[:, None] * length + jnp.arange(length)[None]).astype(f32).reshape(many)
    frequency = 10000.0 ** (-jnp.arange(0, HEAD_DIM, 2).astype(f32) / HEAD_DIM)
    angles = position[:, None] * frequency[None]
    cosine, sine = lax.optimization_barrier((jnp.cos(angles), jnp.sin(angles)))
    cosine = jnp.tile(cosine, (1, 4))
    sine = jnp.tile(sine, (1, 4))
    spans = length // HALF
    ids = jnp.pad(seq_ids[0], (1, 1), constant_values=-1)
    key_ids = jnp.stack(
        [lax.dynamic_slice_in_dim(ids, block[j] * spans, spans + 2, 0) for j in range(CHIPS)]
    )
    key_ids = jnp.repeat(key_ids, HALF, axis=1)
    query_ids = key_ids[:, HALF : HALF + length]
    offset = jnp.arange(extent)[None, :] - HALF - jnp.arange(length)[:, None]
    allowed = (jnp.abs(offset) <= HALF)[None] & (query_ids[:, :, None] == key_ids[:, None, :])
    bias = jnp.where(allowed, 0.0, -1e30).astype(f32)

    low_one, query, kv, wq, gains = call(
        qkv_kernel,
        "qkv",
        (
            shape(many, width),
            shape(CHIPS, length, local),
            shape(CHIPS, length, 2 * local),
            shape(width, 3 * local),
            shape(8, width, dtype=f32),
        ),
        *xs,
        mine,
        other,
        cosine,
        sine,
                flops=2 * many * width * 3 * local,
    )
    kv_other = swap_core(kv)

    def beyond(value):
        pairs = []
        for m in range(seq_count):
            to = m - MEMBERS + 1 if m % CORES == 0 else m + MEMBERS - 1
            if 0 <= to < seq_count:
                pairs.append((m, to))
        return lax.ppermute(value, "seq", pairs)

    rim = ()
    if edges:
        first = lax.dynamic_index_in_dim(kv, chip, 0, False)[:HALF]
        last = lax.dynamic_index_in_dim(kv, chip ^ (CHIPS - 1), 0, False)[length - HALF :]
        rim = (beyond(jnp.where(core == 0, first, last)),)

    attn = call(
        functools.partial(attend_kernel, edges),
        "attend",
        shape(CHIPS, length, local),
        query,
        kv,
        kv_other,
        bias,
        *rim,
                flops=4 * many * extent * local,
    )
    attns = over_chips(attn)
    mine = call(
        functools.partial(place_kernel, 2), "ffn_place", shape(PLANES, half, in_lanes), *in_pieces, after=(attns[1],)
    )
    other = swap_core(mine)
    own, d1, d2, d3, hidden, low_two, hidden_low, grad_expanded, gain_two, wb, wo = call(
        ffn_kernel,
        "ffn",
        (shape(length, width, dtype=f32),)
        + (shape(length, width),) * 3
        + (
            shape(length, width, dtype=f32),
            shape(many, width),
            shape(many, units),
            shape(many, 2 * units),
            shape(8, width, dtype=f32),
            shape(units, width),
            shape(local, width),
        ),
        *attns,
        *xs,
        *gys,
        mine,
        other,
        gains,
                scratch=(pltpu.VMEM((width, 2 * units), bf16), pltpu.VMEM((width, width), bf16)),
        flops=2 * many * width * (width + 5 * units),
    )
    received = [swap_seq(d, CORES * (j + 1)) for j, d in enumerate((d1, d2, d3))]
    keep_ffn, away, mixed_own, mixed1, mixed2, mixed3 = call(
        ffn_grads_kernel,
        "ffn_grads",
        (shape(PLANES, half, ffn_lanes, dtype=f32), shape(PLANES, half, ffn_lanes))
        + (shape(length, width, dtype=f32),)
        + (shape(length, width),) * 3,
        low_two,
        hidden_low,
        grad_expanded,
        *gys,
        wb,
                scratch=(pltpu.VMEM((width, 2 * units), f32), pltpu.VMEM((CORES, units, lanes), f32)),
        flops=2 * many * width * 4 * units,
    )
    got_ffn = swap_core(away)
    dh, dh_low = call(
        dh_kernel, "dh", (shape(length, width, dtype=f32), shape(length, width)), own, *received, gys[0], hidden, gains, after=(away,)
    )
    dhs = over_chips(dh_low)
    sent_ffn = call(
        to_planes_kernel,
        "ffn_to_planes",
        (shape(half, ffn_lanes, dtype=f32),) + (shape(half, ffn_lanes),) * 3,
        keep_ffn,
        got_ffn,
        after=(dh_low,),
            )
    got_ffn = [swap_shard(s, i + 1) for i, s in enumerate(sent_ffn[1:])]

    backs = call(
        functools.partial(attend_back_kernel, edges),
        "attend_back",
        (
            shape(CHIPS, length, local, dtype=f32),
            shape(CHIPS, length, 2 * local, dtype=f32),
            shape(CHIPS, length, 2 * local),
        )
        + ((shape(HALF, 2 * local),) if edges else ()),
        query,
        kv,
        kv_other,
        bias,
        *dhs,
        wo,
        *rim,
        after=(sent_ffn[1],),
                flops=10 * many * extent * local,
    )
    dq, dkv, back = backs[:3]
    back = swap_core(back)
    if edges:
        rim = (beyond(backs[3]),)

    def over_groups(total, kept_type):
        step = MEMBERS
        while step < seq_count:
            total = total + swap_seq(total.astype(bf16), step).astype(f32)
            step *= 2
        return total.astype(kept_type)

    def summed(own, parts, name, after=()):
        out = call(
            sum_kernel, name, shape(*own.shape, dtype=f32 if edges else bf16), own, *parts, after=after
        )
        return over_groups(out, bf16)

    pieces_ffn = over_chips(summed(sent_ffn[0], got_ffn, "ffn_sum", (dq,)))

    keep, away, dqkv = call(
        functools.partial(qkv_grads_kernel, edges),
        "qkv_grads",
        (
            shape(PLANES, half, qkv_lanes, dtype=f32),
            shape(PLANES, half, qkv_lanes),
            shape(many, 3 * local),
        ),
        dq,
        dkv,
        back,
        cosine,
        sine,
        low_one,
        *attns,
        *dhs,
        *rim,
                scratch=(pltpu.VMEM((width, qkv_lanes), f32), pltpu.VMEM((many, local), bf16)),
        flops=2 * many * width * 4 * local,
    )
    got = swap_core(away)
    last_own, o1, o2, o3, gain_sums = call(
        da_kernel,
        "da",
        (shape(2 * length, width, dtype=f32),)
        + (shape(2 * length, width),) * 3
        + (shape(PLANES, EXTRA, qkv_lanes, dtype=f32),),
        dqkv,
        wq,
        *xs,
        mixed_own,
        mixed1,
        mixed2,
        mixed3,
        gain_two,
        flops=2 * many * width * 3 * local,
    )
    received = [swap_seq(o, CORES * (j + 1)) for j, o in enumerate((o1, o2, o3))]
    sent = call(
        to_planes_gains_kernel,
        "qkv_to_planes",
        (shape(kept, qkv_lanes, dtype=f32),) + (shape(kept, qkv_lanes),) * 3,
        keep,
        got,
        gain_sums,
            )
    got = [swap_shard(s, i + 1) for i, s in enumerate(sent[1:])]

    mine = call(
        functools.partial(place_kernel, 0),
        "ffn_gather",
        shape(CHIPS, half, ffn_lanes),
        *pieces_ffn,
        after=(sent[1],),
            )
    owned_in, owned_back = call(
        ffn_owned_kernel,
        "ffn_owned",
        (shape(*w_in.shape, dtype=f32), shape(*w_back.shape, dtype=f32)),
        mine,
        swap_core(mine),
            )
    mixed, grad_tokens = call(
        last_kernel,
        "last",
        (shape(1, length, width), shape(1, length, width)),
        last_own,
        *received,
        xs[0],
        dh,
        hidden,
        gains,
        after=(sent[1],),
    )
    mine = call(
        functools.partial(place_kernel, 0),
        "qkv_gather",
        shape(CHIPS, kept, qkv_lanes),
        *over_chips(summed(sent[0], got, "qkv_sum")),
            )
    owned_qkv, owned_out, gain_sums = call(
        qkv_owned_kernel,
        "qkv_owned",
        (
            shape(*w_qkv.shape, dtype=f32),
            shape(*w_out.shape, dtype=f32),
            shape(EXTRA, local, dtype=f32),
        ),
        mine,
        swap_core(mine),
            )
    return (mixed, grad_tokens, gain_sums[0], owned_qkv, owned_out, gain_sums[1], owned_in, owned_back)


def solution(mesh):
    return jax.shard_map(
        shards,
        mesh=mesh,
        in_specs=(
            P("shard", "seq", None),
            P("shard"),
            P("shard", None),
            P("shard", None),
            P("shard"),
            P("shard", None),
            P("shard", None),
            P("shard", None),
            P("shard", "seq", None),
        ),
        out_specs=(
            P("shard", "seq", None),
            P("shard", "seq", None),
            P("shard"),
            P("shard", None),
            P("shard", None),
            P("shard"),
            P("shard", None),
            P("shard", None),
        ),
        check_vma=False,
    )
```

time: 549 us -> 190 us (0.35)
  waiting for transfers between devices: 324 us -> 91 us
  blocking collectives: 129 us -> 0 us
  matrix products: 58.5 us -> 0 us
  starting transfers between devices: 7.25 us -> 57.3 us
  Pallas kernels: 0 us -> 28 us
  between operations: 16.3 us -> 3.55 us
  other arithmetic: 6.39 us -> 0.61 us
    all_gather x4 -> x0, waiting for transfers between devices: 178 us -> none  [the longest x1 68.8 us: shards(): lax.all_gather(w_in, 'shard', axis=0, tiled=True)]
    reduce_scatter x4 -> x0, waiting for transfers between devices: 140 us -> none  [the longest x1 69.1 us: shards(): lax.psum_scatter(grad_qkv.astype(jnp.bfloat16), 'shard', scatter_dimensio...]
    psum x1 -> x0, blocking collectives: 105 us -> none  [shards(): lax.psum((owned[0], owned[1], owned[2], owned[3], owned[4], owned[5]), 's...]
    ppermute x4 -> x44, waiting for transfers between devices: 3.21 us -> 91 us  [the longest x32 60.1 us: swap_seq(): return lax.ppermute(value, 'seq', [(i, i ^ bits) for i in range(count)])]
    dot_general x18 -> x0, matrix products: 58.5 us -> none  [the longest x1 11.2 us: shards(): jnp.einsum('hqk,khd->qhd', grad_scores, keys_ext, preferred_element_type=...]
    ppermute x4 -> x44, starting transfers between devices: 6.76 us -> 57.3 us  [the longest x32 31.1 us: swap_seq(): return lax.ppermute(value, 'seq', [(i, i ^ bits) for i in range(count)])]
    pallas_call x0 -> x21, Pallas kernels: none -> 28 us  [call(): pl.pallas_call(body, out_shape=outs, in_specs=specs, out_specs=jax.tree.m...]
    unnamed x2 -> x0, blocking collectives: 24.4 us -> none
  transfers between devices with their start and end apart: 12 -> 44, of which waited for: 8 -> 20; matrix products, arithmetic and copies ran while one was open for 11% -> 2% of each run, Pallas kernels for 0% -> 5%
where the time goes in v2:
time: 190 us; the launch traced here: 189 us
  waiting for transfers between devices  91 us (48%)
  starting transfers between devices  57.3 us (30%)
  Pallas kernels  28 us (15%)
  local copies, waits for them, and re-layouts  8.87 us (5%)
  between operations  3.55 us (2%)
    ppermute x32, waiting for transfers between devices, swap_seq(): return lax.ppermute(value, 'seq', [(i, i ^ bits) for i in range(count)])  60.1 us
    ppermute x32, starting transfers between devices, swap_seq(): return lax.ppermute(value, 'seq', [(i, i ^ bits) for i in range(count)])  31.1 us
    ppermute x12, waiting for transfers between devices, swap_shard(): return lax.ppermute(value, 'shard', [(i, i ^ bits) for i in range(count)])  30.9 us
    pallas_call x21, Pallas kernels, call(): pl.pallas_call(body, out_shape=outs, in_specs=specs, out_specs=jax.tree.m...  28 us
    ppermute x12, starting transfers between devices, swap_shard(): return lax.ppermute(value, 'shard', [(i, i ^ bits) for i in range(count)])  26.2 us
    unnamed x18, local copies, waits for them, and re-layouts  5.42 us
  transfers between devices with their start and end apart: 44, of which 20 were waited for; matrix products, arithmetic and copies ran while one was open for 2% of the time, Pallas kernels for 5%

profile of v2, /device:TPU:0, one launch (start us, length us, event | category | flops | bytes accessed | tf_op | source)
XLA Modules:
  0.0 189.3 jit_solution(17110419548750921855)
XLA Ops:
  3.3 5.1 %collective-permute-start.5 = (bf16[112,576]{1,0:T(8,128)(2,1)S(1)}, bf16[112,576]{1,0:T(8,128)(2,1)S(1)}, u32[]{:S(2)}, u32[]{:S(2)}) collective-permute-start(bf16[112,576]{1,0:T(8,128)(2,1)S(1)} %qkv_piece.1.refs_0_.refs_4_), channel_id=1, source_target_pairs={{0,3},{1,2},{2,1},{3,0},{4,7},{5,6},{6,5},{7,4},{8,11},{9,10},{10,... | collective-permute-start | bytes 387080 | tf_op jit(solution)/shard_map/ppermute | solution.py:44
  9.0 2.6 %collective-permute-start.2 = (bf16[128,768]{1,0:T(8,128)(2,1)}, bf16[128,768]{1,0:T(8,128)(2,1)S(1)}, u32[]{:S(2)}, u32[]{:S(2)}) collective-permute-start(bf16[128,768]{1,0:T(8,128)(2,1)} %bitcast.21), channel_id=1, source_target_pairs={{0,24},{4,28},{8,16},{12,20},{16,8},{20,12},{24,0},{28,4},{1,25},{... | collective-permute-start | bytes 589832 | tf_op jit(solution)/shard_map/ppermute | solution.py:39
  20.5 2.5 %collective-permute-start.16 = (bf16[96,1728]{1,0:T(8,128)(2,1)S(1)}, bf16[96,1728]{1,0:T(8,128)(2,1)S(1)}, u32[]{:S(2)}, u32[]{:S(2)}) collective-permute-start(bf16[96,1728]{1,0:T(8,128)(2,1)S(1)} %get-tuple-element.67.refs_0_), channel_id=1, source_target_pairs={{0,3},{1,2},{2,1},{3,0},{4,7},{5,6},{6,5},{7,4},{8,11},{9,10},{10,... | collective-permute-start | bytes 995336 | tf_op jit(solution)/shard_map/ppermute | solution.py:44
  34.9 15.8 %collective-permute-done.15.refs_2_ = bf16[96,1728]{1,0:T(8,128)(2,1)S(1)} collective-permute-done((bf16[96,1728]{1,0:T(8,128)(2,1)S(1)}, bf16[96,1728]{1,0:T(8,128)(2,1)S(1)}, u32[]{:S(2)}, u32[]{:S(2)}) %collective-permute-start.15) | collective-permute-done | bytes 331808 | tf_op jit(solution)/shard_map/ppermute | solution.py:44
  50.9 2.5 %collective-permute-start.13 = (bf16[128,768]{1,0:T(8,128)(2,1)S(1)}, bf16[128,768]{1,0:T(8,128)(2,1)S(1)}, u32[]{:S(2)}, u32[]{:S(2)}) collective-permute-start(bf16[128,768]{1,0:T(8,128)(2,1)S(1)} %get-tuple-element.66.refs_8_.refs_3_.refs_4_), channel_id=1, source_target_pairs={{0,24},{4,28},{8,16},{12,20},{16,8},{20,12},{24,0},{28,4},{1,25},{... | collective-permute-start | bytes 589832 | tf_op jit(solution)/shard_map/ppermute | solution.py:39
  54.4 2.5 %collective-permute-start.10 = (bf16[4,128,192]{2,1,0:T(8,128)(2,1)S(1)}, bf16[4,128,192]{2,1,0:T(8,128)(2,1)S(1)}, u32[]{:S(2)}, u32[]{:S(2)}) collective-permute-start(bf16[4,128,192]{2,1,0:T(8,128)(2,1)S(1)} %attend.1.refs_0_.refs_6_), channel_id=1, source_target_pairs={{0,24},{4,28},{8,16},{12,20},{16,8},{20,12},{24,0},{28,4},{1,25},{... | collective-permute-start | bytes 589832 | tf_op jit(solution)/shard_map/ppermute | solution.py:39
  56.9 2.7 %collective-permute-done.13.refs_11_.refs_6_ = bf16[128,768]{1,0:T(8,128)(2,1)S(1)} collective-permute-done((bf16[128,768]{1,0:T(8,128)(2,1)S(1)}, bf16[128,768]{1,0:T(8,128)(2,1)S(1)}, u32[]{:S(2)}, u32[]{:S(2)}) %collective-permute-start.13) | collective-permute-done | bytes 196640 | tf_op jit(solution)/shard_map/ppermute | solution.py:39
  61.1 2.7 %collective-permute-done.12.refs_10_.refs_5_ = bf16[128,768]{1,0:T(8,128)(2,1)S(1)} collective-permute-done((bf16[128,768]{1,0:T(8,128)(2,1)S(1)}, bf16[128,768]{1,0:T(8,128)(2,1)S(1)}, u32[]{:S(2)}, u32[]{:S(2)}) %collective-permute-start.12) | collective-permute-done | bytes 196640 | tf_op jit(solution)/shard_map/ppermute | solution.py:39
  63.9 5.2 %collective-permute-done.10.refs_3_.refs_9_ = bf16[4,128,192]{2,1,0:T(8,128)(2,1)S(1)} collective-permute-done((bf16[4,128,192]{2,1,0:T(8,128)(2,1)S(1)}, bf16[4,128,192]{2,1,0:T(8,128)(2,1)S(1)}, u32[]{:S(2)}, u32[]{:S(2)}) %collective-permute-start.10) | collective-permute-done | bytes 196640 | tf_op jit(solution)/shard_map/ppermute | solution.py:39
  69.1 5.5 %collective-permute-done.9.refs_2_.refs_8_ = bf16[4,128,192]{2,1,0:T(8,128)(2,1)S(1)} collective-permute-done((bf16[4,128,192]{2,1,0:T(8,128)(2,1)S(1)}, bf16[4,128,192]{2,1,0:T(8,128)(2,1)S(1)}, u32[]{:S(2)}, u32[]{:S(2)}) %collective-permute-start.9) | collective-permute-done | bytes 196640 | tf_op jit(solution)/shard_map/ppermute | solution.py:39
  74.5 4.8 %ffn.1 = (f32[128,768]{1,0:T(8,128)S(1)}, bf16[128,768]{1,0:T(8,128)(2,1)S(1)}, bf16[128,768]{1,0:T(8,128)(2,1)S(1)}, bf16[128,768]{1,0:T(8,128)(2,1)S(1)}, f32[...) custom-call(bf16[4,128,192]{2,1,0:T(8,128)(2,1)S(1)} %attend.1.refs_, ...), custom_call_target="tpu_custom_call" | custom-call | flops 1736441856 | bytes 5038080 | tf_op jit(solution)/shard_map/ffn/pallas_call | solution.py:77
  84.8 4.2 %collective-permute-done.18.refs_1_ = bf16[128,768]{1,0:T(8,128)(2,1)S(1)} collective-permute-done((bf16[128,768]{1,0:T(8,128)(2,1)S(1)}, bf16[128,768]{1,0:T(8,128)(2,1)S(1)}, u32[]{:S(2)}, u32[]{:S(2)}) %collective-permute-start.18) | collective-permute-done | bytes 196640 | tf_op jit(solution)/shard_map/ppermute | solution.py:39
  89.0 5.0 %collective-permute-done.19.refs_2_ = bf16[128,768]{1,0:T(8,128)(2,1)S(1)} collective-permute-done((bf16[128,768]{1,0:T(8,128)(2,1)S(1)}, bf16[128,768]{1,0:T(8,128)(2,1)S(1)}, u32[]{:S(2)}, u32[]{:S(2)}) %collective-permute-start.19) | collective-permute-done | bytes 196640 | tf_op jit(solution)/shard_map/ppermute | solution.py:39
  98.1 5.2 %collective-permute-done.23.refs_7_.refs_13_ = bf16[128,768]{1,0:T(8,128)(2,1)S(1)} collective-permute-done((bf16[128,768]{1,0:T(8,128)(2,1)S(1)}, bf16[128,768]{1,0:T(8,128)(2,1)S(1)}, u32[]{:S(2)}, u32[]{:S(2)}) %collective-permute-start.23) | collective-permute-done | bytes 196640 | tf_op jit(solution)/shard_map/ppermute | solution.py:39
  103.3 2.6 %collective-permute-done.22.refs_6_.refs_12_ = bf16[128,768]{1,0:T(8,128)(2,1)S(1)} collective-permute-done((bf16[128,768]{1,0:T(8,128)(2,1)S(1)}, bf16[128,768]{1,0:T(8,128)(2,1)S(1)}, u32[]{:S(2)}, u32[]{:S(2)}) %collective-permute-start.22) | collective-permute-done | bytes 196640 | tf_op jit(solution)/shard_map/ppermute | solution.py:39
  105.8 6.9 %attend_back.1 = (f32[4,128,192]{2,1,0:T(8,128)S(1)}, f32[4,128,384]{2,1,0:T(8,128)S(1)}, bf16[4,128,384]{2,1,0:T(8,128)(2,1)S(1)}) custom-call(bf16[4,128,192]{2,1,0:T(8,128)(2,1)S(1)} %get-tuple-element.64.refs_0_, bf16[4,128,384]{2,1,0:T(8,128)(2,1)S(1)} %get-tuple-element.65.refs_1_, bf16[4,128,384]{2,1,0:T(8,128)(2,1)S(1)} %collective-permute-done.7.refs_2_, ...), custom_call_target="tpu_custom_call" | custom-call | flops 251658240 | bytes 2588672 | tf_op jit(solution)/shard_map/attend_back/pallas_call | solution.py:77
  114.6 2.3 %qkv_grads.1 = (f32[4,96,768]{2,1,0:T(8,128)S(1)}, bf16[4,96,768]{2,1,0:T(8,128)(2,1)S(1)}, bf16[512,576]{1,0:T(8,128)(2,1)S(1)}) custom-call(f32[4,128,192]{2,1,0:T(8,128)S(1)} %get-tuple-element.83.refs_0_.refs_4_, f32[4,128,384]{2,1,0:T(8,128)S(1)} %get-tuple-element.84.refs_1_, bf16[4,128,384]{2,1,0:T(8,128)(2,1)S(1)} %collective-permute-done.25.refs_2_, ...), custom_call_target="tpu_custom_call" | custom-call | flops 603979776 | bytes 4456448 | tf_op jit(solution)/shard_map/qkv_grads/pallas_call | solution.py:77
  117.1 2.3 %collective-permute-start.39 = (bf16[96,960]{1,0:T(8,128)(2,1)S(1)}, bf16[96,960]{1,0:T(8,128)(2,1)S(1)}, u32[]{:S(2)}, u32[]{:S(2)}) collective-permute-start(bf16[96,960]{1,0:T(8,128)(2,1)S(1)} %get-tuple-element.113), channel_id=1, source_target_pairs={{0,3},{1,2},{2,1},{3,0},{4,7},{5,6},{6,5},{7,4},{8,11},{9,10},{10,... | collective-permute-start | bytes 552968 | tf_op jit(solution)/shard_map/ppermute | solution.py:44
  123.2 10.5 %collective-permute-done.38.refs_2_ = bf16[96,960]{1,0:T(8,128)(2,1)S(1)} collective-permute-done((bf16[96,960]{1,0:T(8,128)(2,1)S(1)}, bf16[96,960]{1,0:T(8,128)(2,1)S(1)}, u32[]{:S(2)}, u32[]{:S(2)}) %collective-permute-start.38) | collective-permute-done | bytes 184352 | tf_op jit(solution)/shard_map/ppermute | solution.py:44
  138.0 9.9 %collective-permute-start.30 = (bf16[112,768]{1,0:T(8,128)(2,1)S(1)}, bf16[112,768]{1,0:T(8,128)(2,1)S(1)}, u32[]{:S(2)}, u32[]{:S(2)}) collective-permute-start(bf16[112,768]{1,0:T(8,128)(2,1)S(1)} %get-tuple-element.102.refs_8_.refs_4_), channel_id=1, source_target_pairs={{0,1},{1,0},{2,3},{3,2},{4,5},{5,4},{6,7},{7,6},{8,9},{9,8},{10,11... | collective-permute-start | bytes 516104 | tf_op jit(solution)/shard_map/ppermute | solution.py:44
  149.8 2.5 %collective-permute-done.30.refs_1_ = bf16[112,768]{1,0:T(8,128)(2,1)S(1)} collective-permute-done((bf16[112,768]{1,0:T(8,128)(2,1)S(1)}, bf16[112,768]{1,0:T(8,128)(2,1)S(1)}, u32[]{:S(2)}, u32[]{:S(2)}) %collective-permute-start.30) | collective-permute-done | bytes 172064 | tf_op jit(solution)/shard_map/ppermute | solution.py:44
  156.6 4.1 %collective-permute-done.35.refs_3_ = bf16[112,768]{1,0:T(8,128)(2,1)S(1)} collective-permute-done((bf16[112,768]{1,0:T(8,128)(2,1)S(1)}, bf16[112,768]{1,0:T(8,128)(2,1)S(1)}, u32[]{:S(2)}, u32[]{:S(2)}) %collective-permute-start.35) | collective-permute-done | bytes 172064 | tf_op jit(solution)/shard_map/ppermute | solution.py:39
  166.6 8.4 %collective-permute-done.26.refs_1_ = bf16[256,768]{1,0:T(8,128)(2,1)S(1)} collective-permute-done((bf16[256,768]{1,0:T(8,128)(2,1)S(1)}, bf16[256,768]{1,0:T(8,128)(2,1)S(1)}, u32[]{:S(2)}, u32[]{:S(2)}) %collective-permute-start.26) | collective-permute-done | bytes 393248 | tf_op jit(solution)/shard_map/ppermute | solution.py:39
  175.0 8.6 %collective-permute-done.27.refs_2_ = bf16[256,768]{1,0:T(8,128)(2,1)S(1)} collective-permute-done((bf16[256,768]{1,0:T(8,128)(2,1)S(1)}, bf16[256,768]{1,0:T(8,128)(2,1)S(1)}, u32[]{:S(2)}, u32[]{:S(2)}) %collective-permute-start.27) | collective-permute-done | bytes 393248 | tf_op jit(solution)/shard_map/ppermute | solution.py:39
  (121 shorter events, 61.4 us)
Async XLA Ops:
  3.3 15.6 %collective-permute-start.5 = (bf16[112,576]{1,0:T(8,128)(2,1)S(1)}, bf16[112,576]{1,0:T(8,128)(2,1)S(1)}, u32[]{:S(2)}, u32[]{:S(2)}) collective-permute-start(bf16[112,576]{1,0:T(8,128)(2,1)S(1)} %qkv_piece.1.refs_0_.refs_4_), channel_id=1, source_target_pairs={{0,3},{1,2},{2,1},{3,0},{4,7},{5,6},{6,5},{7,4},{8,11},{9,10},{10,... | collective-permute-start | bytes 387080 | tf_op jit(solution)/shard_map/ppermute | solution.py:44
  8.4 12.1 %collective-permute-start.4 = (bf16[112,576]{1,0:T(8,128)(2,1)S(1)}, bf16[112,576]{1,0:T(8,128)(2,1)S(1)}, u32[]{:S(2)}, u32[]{:S(2)}) collective-permute-start(bf16[112,576]{1,0:T(8,128)(2,1)S(1)} %qkv_piece.1.refs_0_.refs_4_), channel_id=1, source_target_pairs={{0,2},{1,3},{2,0},{3,1},{4,6},{5,7},{6,4},{7,5},{8,10},{9,11},{10,... | collective-permute-start | bytes 387080 | tf_op jit(solution)/shard_map/ppermute | solution.py:44
  8.4 14.6 %collective-permute-start.3 = (bf16[112,576]{1,0:T(8,128)(2,1)S(1)}, bf16[112,576]{1,0:T(8,128)(2,1)S(1)}, u32[]{:S(2)}, u32[]{:S(2)}) collective-permute-start(bf16[112,576]{1,0:T(8,128)(2,1)S(1)} %qkv_piece.1.refs_0_.refs_4_), channel_id=1, source_target_pairs={{0,1},{1,0},{2,3},{3,2},{4,5},{5,4},{6,7},{7,6},{8,9},{9,8},{10,11... | collective-permute-start | bytes 387080 | tf_op jit(solution)/shard_map/ppermute | solution.py:44
  9.0 16.7 %collective-permute-start.2 = (bf16[128,768]{1,0:T(8,128)(2,1)}, bf16[128,768]{1,0:T(8,128)(2,1)S(1)}, u32[]{:S(2)}, u32[]{:S(2)}) collective-permute-start(bf16[128,768]{1,0:T(8,128)(2,1)} %bitcast.21), channel_id=1, source_target_pairs={{0,24},{4,28},{8,16},{12,20},{16,8},{20,12},{24,0},{28,4},{1,25},{... | collective-permute-start | bytes 589832 | tf_op jit(solution)/shard_map/ppermute | solution.py:39
  11.6 14.2 %collective-permute-start.1 = (bf16[128,768]{1,0:T(8,128)(2,1)}, bf16[128,768]{1,0:T(8,128)(2,1)S(1)}, u32[]{:S(2)}, u32[]{:S(2)}) collective-permute-start(bf16[128,768]{1,0:T(8,128)(2,1)} %bitcast.22), channel_id=1, source_target_pairs={{0,16},{4,20},{8,24},{12,28},{16,0},{20,4},{24,8},{28,12},{1,17},{... | collective-permute-start | bytes 589832 | tf_op jit(solution)/shard_map/ppermute | solution.py:39
  20.5 14.4 %collective-permute-start.16 = (bf16[96,1728]{1,0:T(8,128)(2,1)S(1)}, bf16[96,1728]{1,0:T(8,128)(2,1)S(1)}, u32[]{:S(2)}, u32[]{:S(2)}) collective-permute-start(bf16[96,1728]{1,0:T(8,128)(2,1)S(1)} %get-tuple-element.67.refs_0_), channel_id=1, source_target_pairs={{0,3},{1,2},{2,1},{3,0},{4,7},{5,6},{6,5},{7,4},{8,11},{9,10},{10,... | collective-permute-start | bytes 995336 | tf_op jit(solution)/shard_map/ppermute | solution.py:44
  25.7 25.0 %collective-permute-start.15 = (bf16[96,1728]{1,0:T(8,128)(2,1)S(1)}, bf16[96,1728]{1,0:T(8,128)(2,1)S(1)}, u32[]{:S(2)}, u32[]{:S(2)}) collective-permute-start(bf16[96,1728]{1,0:T(8,128)(2,1)S(1)} %get-tuple-element.67.refs_0_), channel_id=1, source_target_pairs={{0,2},{1,3},{2,0},{3,1},{4,6},{5,7},{6,4},{7,5},{8,10},{9,11},{10,... | collective-permute-start | bytes 995336 | tf_op jit(solution)/shard_map/ppermute | solution.py:44
  25.8 24.9 %collective-permute-start.14 = (bf16[96,1728]{1,0:T(8,128)(2,1)S(1)}, bf16[96,1728]{1,0:T(8,128)(2,1)S(1)}, u32[]{:S(2)}, u32[]{:S(2)}) collective-permute-start(bf16[96,1728]{1,0:T(8,128)(2,1)S(1)} %get-tuple-element.67.refs_0_), channel_id=1, source_target_pairs={{0,1},{1,0},{2,3},{3,2},{4,5},{5,4},{6,7},{7,6},{8,9},{9,8},{10,11... | collective-permute-start | bytes 995336 | tf_op jit(solution)/shard_map/ppermute | solution.py:44
  33.3 17.4 %collective-permute-start.8 = (bf16[4,128,192]{2,1,0:T(8,128)(2,1)S(1)}, bf16[4,128,192]{2,1,0:T(8,128)(2,1)S(1)}, u32[]{:S(2)}, u32[]{:S(2)}) collective-permute-start(bf16[4,128,192]{2,1,0:T(8,128)(2,1)S(1)} %attend.1.refs_0_.refs_6_), channel_id=1, source_target_pairs={{0,8},{4,12},{8,0},{12,4},{16,24},{20,28},{24,16},{28,20},{1,9},{5... | collective-permute-start | bytes 589832 | tf_op jit(solution)/shard_map/ppermute | solution.py:39
  50.8 23.7 %collective-permute-start.17 = (bf16[4,96,1728]{2,1,0:T(8,128)(2,1)S(1)}, bf16[4,96,1728]{2,1,0:T(8,128)(2,1)S(1)}, u32[]{:S(2)}, u32[]{:S(2)}) collective-permute-start(bf16[4,96,1728]{2,1,0:T(8,128)(2,1)S(1)} %ffn_place.1.refs_12_), channel_id=1, source_target_pairs={{0,4},{4,0},{8,12},{12,8},{16,20},{20,16},{24,28},{28,24},{1,5},{5... | collective-permute-start | bytes 3981320 | tf_op jit(solution)/shard_map/ppermute | solution.py:39
  54.4 14.6 %collective-permute-start.10 = (bf16[4,128,192]{2,1,0:T(8,128)(2,1)S(1)}, bf16[4,128,192]{2,1,0:T(8,128)(2,1)S(1)}, u32[]{:S(2)}, u32[]{:S(2)}) collective-permute-start(bf16[4,128,192]{2,1,0:T(8,128)(2,1)S(1)} %attend.1.refs_0_.refs_6_), channel_id=1, source_target_pairs={{0,24},{4,28},{8,16},{12,20},{16,8},{20,12},{24,0},{28,4},{1,25},{... | collective-permute-start | bytes 589832 | tf_op jit(solution)/shard_map/ppermute | solution.py:39
  59.6 15.0 %collective-permute-start.9 = (bf16[4,128,192]{2,1,0:T(8,128)(2,1)S(1)}, bf16[4,128,192]{2,1,0:T(8,128)(2,1)S(1)}, u32[]{:S(2)}, u32[]{:S(2)}) collective-permute-start(bf16[4,128,192]{2,1,0:T(8,128)(2,1)S(1)} %attend.1.refs_0_.refs_6_), channel_id=1, source_target_pairs={{0,16},{4,20},{8,24},{12,28},{16,0},{20,4},{24,8},{28,12},{1,17},{... | collective-permute-start | bytes 589832 | tf_op jit(solution)/shard_map/ppermute | solution.py:39
  81.2 16.8 %collective-permute-start.24 = (bf16[4,96,960]{2,1,0:T(8,128)(2,1)S(1)}, bf16[4,96,960]{2,1,0:T(8,128)(2,1)S(1)}, u32[]{:S(2)}, u32[]{:S(2)}) collective-permute-start(bf16[4,96,960]{2,1,0:T(8,128)(2,1)S(1)} %get-tuple-element.78.refs_7_), channel_id=1, source_target_pairs={{0,4},{4,0},{8,12},{12,8},{16,20},{20,16},{24,28},{28,24},{1,5},{5... | collective-permute-start | bytes 2211848 | tf_op jit(solution)/shard_map/ppermute | solution.py:39
  117.1 16.6 %collective-permute-start.38 = (bf16[96,960]{1,0:T(8,128)(2,1)S(1)}, bf16[96,960]{1,0:T(8,128)(2,1)S(1)}, u32[]{:S(2)}, u32[]{:S(2)}) collective-permute-start(bf16[96,960]{1,0:T(8,128)(2,1)S(1)} %get-tuple-element.112), channel_id=1, source_target_pairs={{0,2},{1,3},{2,0},{3,1},{4,6},{5,7},{6,4},{7,5},{8,10},{9,11},{10,... | collective-permute-start | bytes 552968 | tf_op jit(solution)/shard_map/ppermute | solution.py:44
  117.1 16.6 %collective-permute-start.39 = (bf16[96,960]{1,0:T(8,128)(2,1)S(1)}, bf16[96,960]{1,0:T(8,128)(2,1)S(1)}, u32[]{:S(2)}, u32[]{:S(2)}) collective-permute-start(bf16[96,960]{1,0:T(8,128)(2,1)S(1)} %get-tuple-element.113), channel_id=1, source_target_pairs={{0,3},{1,2},{2,1},{3,0},{4,7},{5,6},{6,5},{7,4},{8,11},{9,10},{10,... | collective-permute-start | bytes 552968 | tf_op jit(solution)/shard_map/ppermute | solution.py:44
  119.4 15.2 %collective-permute-start.37 = (bf16[96,960]{1,0:T(8,128)(2,1)S(1)}, bf16[96,960]{1,0:T(8,128)(2,1)S(1)}, u32[]{:S(2)}, u32[]{:S(2)}) collective-permute-start(bf16[96,960]{1,0:T(8,128)(2,1)S(1)} %get-tuple-element.82.refs_9_), channel_id=1, source_target_pairs={{0,1},{1,0},{2,3},{3,2},{4,5},{5,4},{6,7},{7,6},{8,9},{9,8},{10,11... | collective-permute-start | bytes 552968 | tf_op jit(solution)/shard_map/ppermute | solution.py:44
  122.2 26.4 %collective-permute-start.31 = (bf16[112,768]{1,0:T(8,128)(2,1)S(1)}, bf16[112,768]{1,0:T(8,128)(2,1)S(1)}, u32[]{:S(2)}, u32[]{:S(2)}) collective-permute-start(bf16[112,768]{1,0:T(8,128)(2,1)S(1)} %get-tuple-element.106), channel_id=1, source_target_pairs={{0,2},{1,3},{2,0},{3,1},{4,6},{5,7},{6,4},{7,5},{8,10},{9,11},{10,... | collective-permute-start | bytes 516104 | tf_op jit(solution)/shard_map/ppermute | solution.py:44
  134.7 20.0 %collective-permute-start.42 = (bf16[96,960]{1,0:T(8,128)(2,1)S(1)}, bf16[96,960]{1,0:T(8,128)(2,1)S(1)}, u32[]{:S(2)}, u32[]{:S(2)}) collective-permute-start(bf16[96,960]{1,0:T(8,128)(2,1)S(1)} %ffn_sum.1.refs_0_), channel_id=1, source_target_pairs={{0,24},{4,28},{8,16},{12,20},{16,8},{20,12},{24,0},{28,4},{1,25},{... | collective-permute-start | bytes 552968 | tf_op jit(solution)/shard_map/ppermute | solution.py:39
  136.4 13.4 %collective-permute-start.32 = (bf16[112,768]{1,0:T(8,128)(2,1)S(1)}, bf16[112,768]{1,0:T(8,128)(2,1)S(1)}, u32[]{:S(2)}, u32[]{:S(2)}) collective-permute-start(bf16[112,768]{1,0:T(8,128)(2,1)S(1)} %get-tuple-element.107), channel_id=1, source_target_pairs={{0,3},{1,2},{2,1},{3,0},{4,7},{5,6},{6,5},{7,4},{8,11},{9,10},{10,... | collective-permute-start | bytes 516104 | tf_op jit(solution)/shard_map/ppermute | solution.py:44
  138.0 14.3 %collective-permute-start.30 = (bf16[112,768]{1,0:T(8,128)(2,1)S(1)}, bf16[112,768]{1,0:T(8,128)(2,1)S(1)}, u32[]{:S(2)}, u32[]{:S(2)}) collective-permute-start(bf16[112,768]{1,0:T(8,128)(2,1)S(1)} %get-tuple-element.102.refs_8_.refs_4_), channel_id=1, source_target_pairs={{0,1},{1,0},{2,3},{3,2},{4,5},{5,4},{6,7},{7,6},{8,9},{9,8},{10,11... | collective-permute-start | bytes 516104 | tf_op jit(solution)/shard_map/ppermute | solution.py:44
  156.5 28.3 %collective-permute-start.43 = (bf16[4,96,960]{2,1,0:T(8,128)(2,1)S(1)}, bf16[4,96,960]{2,1,0:T(8,128)(2,1)S(1)}, u32[]{:S(2)}, u32[]{:S(2)}) collective-permute-start(bf16[4,96,960]{2,1,0:T(8,128)(2,1)S(1)} %ffn_gather.1.refs_0_), channel_id=1, source_target_pairs={{0,4},{4,0},{8,12},{12,8},{16,20},{20,16},{24,28},{28,24},{1,5},{5... | collective-permute-start | bytes 2211848 | tf_op jit(solution)/shard_map/ppermute | solution.py:39
  162.9 24.1 %collective-permute-start.36 = (bf16[4,112,768]{2,1,0:T(8,128)(2,1)S(1)}, bf16[4,112,768]{2,1,0:T(8,128)(2,1)S(1)}, u32[]{:S(2)}, u32[]{:S(2)}) collective-permute-start(bf16[4,112,768]{2,1,0:T(8,128)(2,1)S(1)} %qkv_gather.1.refs_0_), channel_id=1, source_target_pairs={{0,4},{4,0},{8,12},{12,8},{16,20},{20,16},{24,28},{28,24},{1,5},{5... | collective-permute-start | bytes 2064392 | tf_op jit(solution)/shard_map/ppermute | solution.py:39
  163.9 19.6 %collective-permute-start.27 = (bf16[256,768]{1,0:T(8,128)(2,1)S(1)}, bf16[256,768]{1,0:T(8,128)(2,1)S(1)}, u32[]{:S(2)}, u32[]{:S(2)}) collective-permute-start(bf16[256,768]{1,0:T(8,128)(2,1)S(1)} %get-tuple-element.96), channel_id=1, source_target_pairs={{0,16},{4,20},{8,24},{12,28},{16,0},{20,4},{24,8},{28,12},{1,17},{... | collective-permute-start | bytes 1179656 | tf_op jit(solution)/shard_map/ppermute | solution.py:39
  165.2 18.3 %collective-permute-start.28 = (bf16[256,768]{1,0:T(8,128)(2,1)S(1)}, bf16[256,768]{1,0:T(8,128)(2,1)S(1)}, u32[]{:S(2)}, u32[]{:S(2)}) collective-permute-start(bf16[256,768]{1,0:T(8,128)(2,1)S(1)} %get-tuple-element.97), channel_id=1, source_target_pairs={{0,24},{4,28},{8,16},{12,20},{16,8},{20,12},{24,0},{28,4},{1,25},{... | collective-permute-start | bytes 1179656 | tf_op jit(solution)/shard_map/ppermute | solution.py:39
  (29 other events, 213.3 us)

commit v3 on v2

--- a/solution.py
+++ b/solution.py
@@ -1,4 +1,5 @@
 import functools
+import math
 
 import jax
 import jax.numpy as jnp
@@ -19,7 +20,31 @@
 f32 = jnp.float32
 bf16 = jnp.bfloat16
 SCALE = HEAD_DIM ** (-0.5)
-VMEM = 20 * 1024 * 1024
+ROOM = 6 * 1024 * 1024
+
+
+TIMES = {
+    "qkv_piece": 0.5,
+    "ffn_piece": 1,
+    "qkv_place": 0.8,
+    "qkv": 1.6,
+    "attend": 2.3,
+    "ffn_place": 1.2,
+    "ffn": 4.5,
+    "ffn_grads": 1.6,
+    "dh": 0.4,
+    "mixed": 0.6,
+    "ffn_split": 1,
+    "mixed_sum": 0.4,
+    "attend_back": 6.9,
+    "qkv_grads": 2.4,
+    "da": 1.5,
+    "qkv_to_planes": 0.8,
+    "qkv_gather": 0.6,
+    "last": 0.6,
+    "ffn_owned": 2.2,
+    "qkv_owned": 1.7,
+}
 
 
 def dot(left, right):
@@ -65,15 +90,22 @@
     return (me % MEMBERS) // CORES, me % CORES, lax.axis_index("shard")
 
 
-def call(kernel, name, outs, *operands, after=(), scratch=(), flops=1e6):
+def size_of(value):
+    return math.prod(value.shape) * jnp.dtype(value.dtype).itemsize
+
+
+def call(kernel, name, outs, *operands, after=(), scratch=(), held=0):
     taken = len(operands)
-    specs = [pl.BlockSpec(memory_space=pltpu.VMEM)] * taken
+    specs = [pl.BlockSpec(memory_space=pltpu.HBM)] * held
+    specs += [pl.BlockSpec(memory_space=pltpu.VMEM)] * (taken - held)
     specs += [pl.BlockSpec(memory_space=pl.ANY)] * len(after)
+    us = TIMES.get(name, 0.5)
+    held_size = sum(size_of(o) for o in operands[held:])
+    held_size += sum(size_of(o) for o in jax.tree.leaves(outs))
 
     def body(*refs):
         kernel(places(), *refs[:taken], *refs[taken + len(after) :])
 
-    moved = sum(o.size * o.dtype.itemsize for o in operands)
     return pl.pallas_call(
         body,
         out_shape=outs,
@@ -81,9 +113,9 @@
         out_specs=jax.tree.map(lambda _: pl.BlockSpec(memory_space=pltpu.VMEM), outs),
         scratch_shapes=list(scratch),
         cost_estimate=pl.CostEstimate(
-            flops=int(flops), bytes_accessed=int(moved), transcendentals=0
-        ),
-        compiler_params=pltpu.CompilerParams(vmem_limit_bytes=VMEM),
+            flops=int(us * 2e10), bytes_accessed=int(us * 10), transcendentals=0
+        ),
+        compiler_params=pltpu.CompilerParams(vmem_limit_bytes=2 * held_size + ROOM),
         name=name,
     )(*operands, *after)
 
@@ -115,6 +147,10 @@
     return pl.ds(pl.multiple_of(start, 16), size)
 
 
+def lanes_at(start, size):
+    return pl.ds(pl.multiple_of(start, 128), size)
+
+
 def extra_rows(first, second, lanes):
     row = lax.broadcasted_iota(jnp.int32, (EXTRA, lanes), 0)
     pad = jnp.zeros((1, lanes - first.shape[1]), f32)
@@ -123,54 +159,116 @@
     return jnp.where(row == 0, first, jnp.where(row == 1, second, 0.0))
 
 
-def qkv_piece_kernel(where, w_qkv, gain_one, gain_two, out):
+def copied(pairs, sems):
+    copies = [pltpu.make_async_copy(src, dst, sems.at[i]) for i, (src, dst) in enumerate(pairs)]
+    for copy in copies:
+        copy.start()
+    for copy in copies:
+        copy.wait()
+
+
+def qkv_piece_kernel(where, w_qkv, w_out, gain_one, gain_two, out, rows, part, sems):
+    chip, core = where[0], where[1]
     half = w_qkv.shape[0] // CORES
     width = w_qkv.shape[1] // 3
     local = width // CHIPS
-    rows = rows_at(where[1] * half, half)
+    size, lanes = part.shape
+    copied(
+        (
+            (w_qkv.at[rows_at(core * half, half), :], rows),
+            (w_out.at[rows_at(chip * size, size), lanes_at(core * lanes, lanes)], part),
+        ),
+        sems,
+    )
     for b in range(CHIPS):
 
-        @pl.when(where[0] == b)
+        @pl.when(chip == b)
         def _():
             for p in range(3):
                 at = p * width + b * local
-                out[:half, p * local : (p + 1) * local] = w_qkv[rows, at : at + local]
-
-    out[half:, :] = extra_rows(
+                out[:half, p * local : (p + 1) * local] = rows[:, at : at + local]
+
+    out[half : half + EXTRA, :] = extra_rows(
         gain_one[...].astype(f32)[None], gain_two[...].astype(f32)[None], 3 * local
     ).astype(bf16)
-
-
-def ffn_piece_kernel(where, w_in, w_out, w_back, cotangent, out, upward):
-    upward[...] = cotangent[...]
+    at = half + EXTRA
+    out[at : at + 16, :lanes] = part[:16, :]
+    out[at + 16 :, :lanes] = part[16:32, :]
+    out[at : at + 16, lanes:] = part[32:, :local]
+    out[at + 16 :, lanes:] = part[32:, local:]
+
+
+def ffn_piece_kernel(where, w_in, w_back, out, rows, back, sems):
+    chip, core = where[0], where[1]
     half = w_in.shape[0] // CORES
-    width = w_out.shape[1]
     units = FF // PLANES // CHIPS
-    rows = rows_at(where[1] * half, half)
-    lanes = width // CORES
-    at_out = 2 * PLANES * units
-    at_back = at_out + width
-    out[:, at_out:at_back] = w_out[rows, :]
-    out[units:, at_back:] = jnp.zeros((half - units, lanes), bf16)
+    lanes = back.shape[1]
+    copied(
+        (
+            (w_in.at[rows_at(core * half, half), :], rows),
+            (w_back.at[:, lanes_at(core * lanes, lanes)], back),
+        ),
+        sems,
+    )
+    out[units:, :lanes] = jnp.zeros((half - units, lanes), bf16)
     for b in range(CHIPS):
 
-        @pl.when(where[0] == b)
+        @pl.when(chip == b)
         def _():
             for p in range(2):
                 for z in range(PLANES):
                     at = p * FF + z * units * CHIPS + b * units
-                    to = (p * PLANES + z) * units
-                    out[:, to : to + units] = w_in[rows, at : at + units]
-            for k in range(CORES):
-
-                @pl.when(where[1] == k)
-                def _():
-                    out[:units, at_back:] = w_back[b * units : (b + 1) * units, k * lanes : (k + 1) * lanes]
+                    to = lanes + (p * PLANES + z) * units
+                    out[:, to : to + units] = rows[:, at : at + units]
+            out[:units, :lanes] = back[b * units : (b + 1) * units, :]
 
 
 def place_kernel(slot, where, p0, p1, p2, p3, out):
     for i, ref in enumerate((p0, p1, p2, p3)):
         out[where[slot] ^ i] = ref[...]
+
+
+def qkv_place_kernel(where, p0, p1, p2, p3, out, packet):
+    kept = out.shape[1]
+    lanes = packet.shape[2]
+    for i, ref in enumerate((p0, p1, p2, p3)):
+        z = where[2] ^ i
+        out[z] = ref[:kept, :]
+        packet[z, :16, :] = ref[kept : kept + 16, :lanes]
+        packet[z, 16:32, :] = ref[kept + 16 :, :lanes]
+        packet[z, 32:, :] = jnp.concatenate(
+            [ref[kept : kept + 16, lanes:], ref[kept + 16 :, lanes:]], axis=1
+        )
+
+
+def up_pair_kernel(where, own, both, out):
+    out[0] = own[...]
+    out[1] = both[own.shape[0] :, :]
+
+
+def pair_kernel(where, first, second, out):
+    out[0] = first[...]
+    out[1] = second[...]
+
+
+def ffn_place_kernel(where, near, far, p01, p23, out):
+    half = near.shape[1]
+    p0, p1, p2, p3 = p01.at[0], p01.at[1], p23.at[0], p23.at[1]
+    size, lanes = p0.shape[1:]
+    for i, ref in enumerate((near.at[0], near.at[1], far.at[0], far.at[1])):
+        z = where[2] ^ i
+        out[z, :, :lanes] = ref[:, :lanes]
+        out[z, :, 3 * lanes :] = ref[:, lanes:]
+    for i, ref in enumerate((p0, p1, p2, p3)):
+        b = where[0] ^ i
+        at = rows_at((b % 2) * size, size)
+
+        for half_at in range(2):
+
+            @pl.when(b // 2 == half_at)
+            def _():
+                for z in range(PLANES):
+                    out[z, at, (half_at + 1) * lanes : (half_at + 2) * lanes] = ref[z]
 
 
 def qkv_kernel(where, x0, x1, x2, x3, mine, other, cos, sin, a_out, q_out, kv_out, w_out, g_out):
@@ -186,7 +284,7 @@
         g_out[:, z * share : (z + 1) * share] = tail[:8]
     gain = g_out[0:1, :]
     for j, ref in enumerate((x0, x1, x2, x3)):
-        normed, _ = norm_parts(ref[...].astype(f32))
+        normed, _ = norm_parts(ref[:rows, :].astype(f32))
         a_out[j * rows : (j + 1) * rows, :] = (normed * gain).astype(bf16)
     out = dot(a_out[...], w_out[...])
     front = first_half((CHIPS * rows, 128))
@@ -239,7 +337,7 @@
 
 
 def ffn_kernel(
-    where, t0, t1, t2, t3, x0, x1, x2, x3, y0, y1, y2, y3, mine, other, gains,
+    where, t0, t1, t2, t3, x0, x1, x2, x3, y02, y13, mine, other, gains,
     own_out, d1_out, d2_out, d3_out, hid_out, a_out, m_out, dgu_out, gain_out, wb_out, wc_out,
     wi, wo,
 ):
@@ -252,13 +350,14 @@
     part = units // PLANES
     lanes = width // CORES
     local = width // CHIPS
-    at_out, at_back = 2 * units, 2 * units + width
     for z in range(PLANES):
         for k, ref in ((core, mine), (1 - core, other)):
-            wi[rows_at(z * share + k * half, half), :] = ref[z, :, :at_out]
-            wo[rows_at(z * share + k * half, half), :] = ref[z, :, at_out:at_back]
-    own_back = jnp.concatenate([mine[z, :part, at_back:] for z in range(PLANES)], axis=0)
-    other_back = jnp.concatenate([other[z, :part, at_back:] for z in range(PLANES)], axis=0)
+            wi[rows_at(z * share + k * half, half), :] = ref[z, :, 3 * lanes :]
+            for p in range(CORES):
+                at = slice(z * share + p * half, z * share + (p + 1) * half)
+                wo[at, lanes_at(k * lanes, lanes)] = ref[z, :, (p + 1) * lanes : (p + 2) * lanes]
+    own_back = jnp.concatenate([mine[z, :part, :lanes] for z in range(PLANES)], axis=0)
+    other_back = jnp.concatenate([other[z, :part, :lanes] for z in range(PLANES)], axis=0)
     wb_out[:, :lanes] = jnp.where(core == 0, own_back, other_back)
     wb_out[:, lanes:] = jnp.where(core == 0, other_back, own_back)
     wc_out[...] = wo[rows_at(chip * local, local), :]
@@ -269,7 +368,7 @@
     ]
     normed = []
     for j in range(CHIPS):
-        hidden = xs[j][...].astype(f32)
+        hidden = xs[j][:rows, :].astype(f32)
         for i, (ref, weight) in enumerate(outward):
             hidden = hidden + dot(ref[j ^ i], weight)
         if j == 0:
@@ -286,7 +385,7 @@
         slope = rise + entering * jnp.exp(-0.5 * entering * entering) * 0.3989422804014327
         act = entering * rise
         m_out[at, :] = (act * gating).astype(bf16)
-        dm = dot_t((y0, y1, y2, y3)[j][...], wb_out[...])
+        dm = dot_t((y02, y13)[j % 2][j // 2], wb_out[...])
         dgu = jnp.concatenate([dm * gating * slope, dm * act], axis=1).astype(bf16)
         dgu_out[at, :] = dgu
         da = dot_t(dgu, wi[...])
@@ -298,16 +397,27 @@
     gain_out[...] = jnp.broadcast_to(total, gain_out.shape)
 
 
-def ffn_grads_kernel(where, a, m, dgu, y0, y1, y2, y3, wb, keep, away, mixed_own, m1, m2, m3, gin, gb):
+def mixed_kernel(where, m, wb, own, m1, m2, m3):
+    rows = own.shape[0]
+    own[...] = dot(m[:rows, :], wb[...])
+    for j, ref in enumerate((m1, m2, m3)):
+        ref[...] = dot(m[(j + 1) * rows : (j + 2) * rows, :], wb[...]).astype(bf16)
+
+
+def mixed_sum_kernel(where, own, r1, r2, r3, hidden, out):
+    total = own[...] + r1[...].astype(f32) + r2[...].astype(f32) + r3[...].astype(f32)
+    out[0] = (hidden[...] + total).astype(bf16)
+
+
+def ffn_grads_kernel(where, a, m, dgu, y02, y13, keep, away, gin, gb):
     core = where[1]
-    rows = y0.shape[0]
     half = keep.shape[1]
     share = CORES * half
     units = m.shape[1]
     part = units // PLANES
-    lanes = y0.shape[1] // CORES
+    lanes = y02.shape[2] // CORES
     gin[...] = t_dot(a[...], dgu[...])
-    upward = jnp.concatenate([ref[...] for ref in (y0, y1, y2, y3)], axis=0)
+    upward = jnp.concatenate([y02[0], y13[0], y02[1], y13[1]], axis=0)
     back = t_dot(m[...], upward)
     first, second = back[:, :lanes], back[:, lanes:]
     gb[0] = jnp.where(core == 0, first, second)
@@ -319,15 +429,12 @@
         keep[z, :, 2 * units :] = jnp.concatenate([gb[0, at, :], blank], axis=0)
         away[z, :, : 2 * units] = gin[rows_at(z * share + (1 - core) * half, half), :].astype(bf16)
         away[z, :, 2 * units :] = jnp.concatenate([gb[1, at, :], blank], axis=0).astype(bf16)
-    mixed_own[...] = dot(m[:rows, :], wb[...])
-    for j, ref in enumerate((m1, m2, m3)):
-        ref[...] = dot(m[(j + 1) * rows : (j + 2) * rows, :], wb[...]).astype(bf16)
-
-
-def dh_kernel(where, own, r1, r2, r3, y0, hidden, gains, dh_out, low_out):
+
+
+def dh_kernel(where, own, r1, r2, r3, y02, hidden, gains, dh_out, low_out):
     total = own[...] + r1[...].astype(f32) + r2[...].astype(f32) + r3[...].astype(f32)
     normed, factor = norm_parts(hidden[...])
-    dh = y0[...].astype(f32) + norm_inward(total, gains[1:2, :], normed, factor)
+    dh = y02[0].astype(f32) + norm_inward(total, gains[1:2, :], normed, factor)
     dh_out[...] = dh
     low_out[...] = dh.astype(bf16)
 
@@ -402,10 +509,10 @@
             value = rim[...].astype(f32)
             gkv = gkv + jnp.where(
                 (core == 0) & (b == 0), jnp.concatenate([value, blank], axis=0), 0.0
-            )
+    )
             gkv = gkv + jnp.where(
                 (core == 1) & (b == CHIPS - 1), jnp.concatenate([blank, value], axis=0), 0.0
-            )
+    )
         g = jnp.concatenate([dq[j], gkv[:, :local]], axis=1)
         for lane in range(0, 2 * local, 128):
             u = g[:, lane : lane + 128]
@@ -432,35 +539,49 @@
         away[z] = acc[rows_at(z * share + (1 - core) * half, half), :].astype(bf16)
 
 
-def da_kernel(where, d, w, x0, x1, x2, x3, own_mixed, m1, m2, m3, gain_two, own_out, o1, o2, o3, gain_out):
+def da_kernel(where, d, w, x0, x1, x2, x3, gain_two, own_out, o1, o2, o3, gain_out):
     rows = x0.shape[0]
     total = jnp.zeros((1, w.shape[0]), f32)
     for j, ref in enumerate((x0, x1, x2, x3)):
         da = dot_t(d[j * rows : (j + 1) * rows, :], w[...])
-        normed, _ = norm_parts(ref[...].astype(f32))
+        normed, _ = norm_parts(ref[:rows, :].astype(f32))
         total = total + jnp.sum(da * normed, axis=0, keepdims=True)
         if j == 0:
-            own_out[:rows, :] = da
-            own_out[rows:, :] = own_mixed[...]
+            own_out[...] = da
         else:
-            out = (o1, o2, o3)[j - 1]
-            out[:rows, :] = da.astype(bf16)
-            out[rows:, :] = (m1, m2, m3)[j - 1][...]
+            (o1, o2, o3)[j - 1][...] = da.astype(bf16)
     share = w.shape[0] // PLANES
     for z in range(PLANES):
         at = slice(z * share, (z + 1) * share)
         gain_out[z] = extra_rows(total[:, at], gain_two[0:1, at], gain_out.shape[2])
 
 
-def to_planes_kernel(where, keep, got, own, o1, o2, o3):
-    plane = where[2]
-    own[...] = keep[plane] + got[plane].astype(f32)
-    for i, ref in enumerate((o1, o2, o3)):
-        at = plane ^ (i + 1)
-        ref[...] = (keep[at] + got[at].astype(f32)).astype(bf16)
-
-
-def to_planes_gains_kernel(where, keep, got, gains, own, o1, o2, o3):
+def copy_kernel(where, value, out):
+    out[...] = value[...]
+
+
+def ffn_split_kernel(where, keep, got, near, far):
+    for i in range(PLANES):
+        at = where[2] ^ i
+        total = keep[at] + got[at].astype(f32)
+        if i < 2:
+            near[i] = total
+        else:
+            far[i - 2] = total.astype(bf16)
+
+
+def ffn_near_kernel(where, near, got, own, sent):
+    own[...] = near[0] + got[0].astype(f32)
+    sent[...] = (near[1] + got[1].astype(f32)).astype(bf16)
+
+
+def ffn_total_kernel(where, own, got, out):
+    out[...] = (own[...] + got[...].astype(f32)).astype(out.dtype)
+
+
+def to_planes_gains_kernel(where, keep, got, gains, d1, d2, d3, own, o1, o2, o3, e1, e2, e3):
+    for ref, out in ((d1, e1), (d2, e2), (d3, e3)):
+        out[...] = ref[...]
     plane = where[2]
     half = keep.shape[1]
     own[:half, :] = keep[plane] + got[plane].astype(f32)
@@ -476,12 +597,10 @@
     out[...] = total.astype(out.dtype)
 
 
-def last_kernel(where, own, r1, r2, r3, x0, dh, hidden, gains, mixed_out, grad_out):
-    rows = dh.shape[0]
+def last_kernel(where, own, r1, r2, r3, x0, dh, gains, grad_out):
     total = own[...] + r1[...].astype(f32) + r2[...].astype(f32) + r3[...].astype(f32)
-    mixed_out[0] = (hidden[...] + total[rows:, :]).astype(bf16)
     normed, factor = norm_parts(x0[...].astype(f32))
-    grad = dh[...] + norm_inward(total[:rows, :], gains[0:1, :], normed, factor)
+    grad = dh[...] + norm_inward(total, gains[0:1, :], normed, factor)
     grad_out[0] = grad.astype(bf16)
 
 
@@ -506,7 +625,7 @@
         back_out[b * part : (b + 1) * part, lanes:] = jnp.where(core == 0, got, own)
 
 
-def qkv_owned_kernel(where, mine, other, qkv_out, w_out, gain_out):
+def qkv_owned_kernel(where, mine, other, qkv_out, w_out, one_out, two_out):
     core = where[1]
     half = mine.shape[1] - EXTRA
     local = w_out.shape[1] // CHIPS
@@ -519,7 +638,8 @@
                 qkv_out[rows, to : to + local] = ref[b, :half, p * local : (p + 1) * local].astype(f32)
             w_out[rows, b * local : (b + 1) * local] = ref[b, :half, 3 * local :].astype(f32)
             total = total + ref[b, half:, :local].astype(f32)
-    gain_out[...] = total
+    one_out[...] = total[0]
+    two_out[...] = total[1]
 
 
 def shards(tokens, norm_gain, w_qkv, w_out, ffn_gain, w_in, w_back, seq_ids, cotangent):
@@ -538,38 +658,62 @@
     extent = length + 2 * HALF
     kept = half + EXTRA
     in_lanes = 2 * units + width + lanes
+    in_sent = lanes + 2 * units
     ffn_lanes = 2 * units + lanes
     qkv_lanes = 4 * local
 
+    out_rows = w_out.shape[0] // CHIPS
     piece = call(
-        qkv_piece_kernel, "qkv_piece", shape(kept, 3 * local), w_qkv, norm_gain, ffn_gain
+        qkv_piece_kernel,
+        "qkv_piece",
+        shape(kept + 32, 3 * local),
+        w_qkv,
+        w_out,
+        norm_gain,
+        ffn_gain,
+        held=2,
+        scratch=(
+            pltpu.VMEM((half, 3 * width), bf16),
+            pltpu.VMEM((out_rows, lanes), bf16),
+            pltpu.SemaphoreType.DMA((2,)),
+        ),
     )
     pieces = over_planes(piece)
-    xs = over_chips(tokens[0])
-    piece, upward = call(
+    both = jnp.concatenate([tokens[0], cotangent[0]], axis=0)
+    both_near = swap_seq(both, 2 * CORES)
+    xs = [tokens[0], swap_seq(tokens[0], CORES), both_near, swap_seq(tokens[0], 3 * CORES)]
+    piece = call(
         ffn_piece_kernel,
         "ffn_piece",
-        (shape(half, in_lanes), shape(length, width)),
+        shape(half, in_sent),
         w_in,
-        w_out,
         w_back,
-        cotangent[0],
+        held=2,
+        scratch=(
+            pltpu.VMEM((half, 2 * FF), bf16),
+            pltpu.VMEM((w_back.shape[0], lanes), bf16),
+            pltpu.SemaphoreType.DMA((2,)),
+        ),
         after=(piece,),
     )
-    in_pieces = over_planes(piece)
-    gys = over_chips(upward)
-    mine = call(
-        functools.partial(place_kernel, 2), "qkv_place", shape(PLANES, kept, 3 * local), *pieces
-    )
+    in_near = swap_shard(piece, 1)
+    mine, out_own = call(
+        qkv_place_kernel,
+        "qkv_place",
+        (
+            shape(PLANES, kept, 3 * local),
+            shape(PLANES, out_rows, lanes),
+        ),
+        *pieces,
+    )
+    out_near = swap_seq(out_own, CORES)
     other = swap_core(mine)
 
     block = (group * CHIPS + (chip ^ jnp.arange(CHIPS))) * CORES + core
     position = (block[:, None] * length + jnp.arange(length)[None]).astype(f32).reshape(many)
     frequency = 10000.0 ** (-jnp.arange(0, HEAD_DIM, 2).astype(f32) / HEAD_DIM)
-    angles = position[:, None] * frequency[None]
-    cosine, sine = lax.optimization_barrier((jnp.cos(angles), jnp.sin(angles)))
-    cosine = jnp.tile(cosine, (1, 4))
-    sine = jnp.tile(sine, (1, 4))
+    angles = position[:, None] * jnp.tile(frequency, 4)[None]
+    cosine, sine = jnp.cos(angles), jnp.sin(angles)
     spans = length // HALF
     ids = jnp.pad(seq_ids[0], (1, 1), constant_values=-1)
     key_ids = jnp.stack(
@@ -596,9 +740,12 @@
         other,
         cosine,
         sine,
-                flops=2 * many * width * 3 * local,
     )
     kv_other = swap_core(kv)
+    in_pair = call(
+        pair_kernel, "in_pair", shape(2, half, in_sent), piece, in_near, after=(gains,)
+    )
+    in_far = swap_shard(in_pair, 2)
 
     def beyond(value):
         pairs = []
@@ -614,6 +761,10 @@
         last = lax.dynamic_index_in_dim(kv, chip ^ (CHIPS - 1), 0, False)[length - HALF :]
         rim = (beyond(jnp.where(core == 0, first, last)),)
 
+    out_pair = call(pair_kernel, "out_pair", shape(2, *out_own.shape), out_own, out_near, after=(in_pair,))
+    out_far = swap_seq(out_pair, 2 * CORES)
+    up_pair = call(up_pair_kernel, "up_pair", shape(2, length, width), cotangent[0], both_near, after=(gains,))
+    gys = (up_pair, swap_seq(up_pair, CORES))
     attn = call(
         functools.partial(attend_kernel, edges),
         "attend",
@@ -623,13 +774,20 @@
         kv_other,
         bias,
         *rim,
-                flops=4 * many * extent * local,
+        after=(gys[1],),
     )
     attns = over_chips(attn)
-    mine = call(
-        functools.partial(place_kernel, 2), "ffn_place", shape(PLANES, half, in_lanes), *in_pieces, after=(attns[1],)
-    )
-    other = swap_core(mine)
+    in_mine = call(
+        ffn_place_kernel,
+        "ffn_place",
+        shape(PLANES, half, in_lanes),
+        in_pair,
+        in_far,
+        out_pair,
+        out_far,
+        after=tuple(attns[1:]),
+    )
+    in_other = swap_core(in_mine)
     own, d1, d2, d3, hidden, low_two, hidden_low, grad_expanded, gain_two, wb, wo = call(
         ffn_kernel,
         "ffn",
@@ -647,41 +805,44 @@
         *attns,
         *xs,
         *gys,
-        mine,
-        other,
+        in_mine,
+        in_other,
         gains,
-                scratch=(pltpu.VMEM((width, 2 * units), bf16), pltpu.VMEM((width, width), bf16)),
-        flops=2 * many * width * (width + 5 * units),
+        scratch=(pltpu.VMEM((width, 2 * units), bf16), pltpu.VMEM((width, width), bf16)),
     )
     received = [swap_seq(d, CORES * (j + 1)) for j, d in enumerate((d1, d2, d3))]
-    keep_ffn, away, mixed_own, mixed1, mixed2, mixed3 = call(
+    keep_ffn, away = call(
         ffn_grads_kernel,
         "ffn_grads",
-        (shape(PLANES, half, ffn_lanes, dtype=f32), shape(PLANES, half, ffn_lanes))
-        + (shape(length, width, dtype=f32),)
-        + (shape(length, width),) * 3,
+        (shape(PLANES, half, ffn_lanes, dtype=f32), shape(PLANES, half, ffn_lanes)),
         low_two,
         hidden_low,
         grad_expanded,
         *gys,
-        wb,
-                scratch=(pltpu.VMEM((width, 2 * units), f32), pltpu.VMEM((CORES, units, lanes), f32)),
-        flops=2 * many * width * 4 * units,
+        scratch=(pltpu.VMEM((width, 2 * units), f32), pltpu.VMEM((CORES, units, lanes), f32)),
     )
     got_ffn = swap_core(away)
-    dh, dh_low = call(
-        dh_kernel, "dh", (shape(length, width, dtype=f32), shape(length, width)), own, *received, gys[0], hidden, gains, after=(away,)
-    )
-    dhs = over_chips(dh_low)
-    sent_ffn = call(
-        to_planes_kernel,
-        "ffn_to_planes",
-        (shape(half, ffn_lanes, dtype=f32),) + (shape(half, ffn_lanes),) * 3,
+    near, far = call(
+        ffn_split_kernel,
+        "ffn_split",
+        (shape(2, half, ffn_lanes, dtype=f32), shape(2, half, ffn_lanes)),
         keep_ffn,
         got_ffn,
+    )
+    got_far = swap_shard(far, 2)
+    dh, dh_low = call(
+        dh_kernel, "dh", (shape(length, width, dtype=f32), shape(length, width)), own, *received, gys[0], hidden, gains, after=(far,)
+    )
+    dhs = over_chips(dh_low)
+    partial_mixed = call(
+        mixed_kernel,
+        "mixed",
+        (shape(length, width, dtype=f32),) + (shape(length, width),) * 3,
+        hidden_low,
+        wb,
         after=(dh_low,),
-            )
-    got_ffn = [swap_shard(s, i + 1) for i, s in enumerate(sent_ffn[1:])]
+    )
+    got_mixed = [swap_seq(o, CORES * (j + 1)) for j, o in enumerate(partial_mixed[1:])]
 
     backs = call(
         functools.partial(attend_back_kernel, edges),
@@ -699,8 +860,7 @@
         *dhs,
         wo,
         *rim,
-        after=(sent_ffn[1],),
-                flops=10 * many * extent * local,
+        after=(far,),
     )
     dq, dkv, back = backs[:3]
     back = swap_core(back)
@@ -720,7 +880,9 @@
         )
         return over_groups(out, bf16)
 
-    pieces_ffn = over_chips(summed(sent_ffn[0], got_ffn, "ffn_sum", (dq,)))
+    mixed = call(
+        mixed_sum_kernel, "mixed_sum", shape(1, length, width), partial_mixed[0], *got_mixed, hidden, after=(dq,)
+    )
 
     keep, away, dqkv = call(
         functools.partial(qkv_grads_kernel, edges),
@@ -739,36 +901,53 @@
         *attns,
         *dhs,
         *rim,
-                scratch=(pltpu.VMEM((width, qkv_lanes), f32), pltpu.VMEM((many, local), bf16)),
-        flops=2 * many * width * 4 * local,
-    )
+        scratch=(pltpu.VMEM((width, qkv_lanes), f32), pltpu.VMEM((many, local), bf16)),
+    )
+    own_ffn, sent_near = call(
+        ffn_near_kernel,
+        "ffn_near",
+        (shape(half, ffn_lanes, dtype=f32), shape(half, ffn_lanes)),
+        near,
+        got_far,
+        after=(dq,),
+    )
+    total = call(
+        ffn_total_kernel,
+        "ffn_total",
+        shape(half, ffn_lanes, dtype=f32 if edges else bf16),
+        own_ffn,
+        swap_shard(sent_near, 1),
+        after=(away,),
+    )
+    pieces_ffn = over_chips(over_groups(total, bf16))
     got = swap_core(away)
     last_own, o1, o2, o3, gain_sums = call(
         da_kernel,
         "da",
-        (shape(2 * length, width, dtype=f32),)
-        + (shape(2 * length, width),) * 3
+        (shape(length, width, dtype=f32),)
+        + (shape(length, width),) * 3
         + (shape(PLANES, EXTRA, qkv_lanes, dtype=f32),),
         dqkv,
         wq,
         *xs,
-        mixed_own,
-        mixed1,
-        mixed2,
-        mixed3,
         gain_two,
-        flops=2 * many * width * 3 * local,
-    )
-    received = [swap_seq(o, CORES * (j + 1)) for j, o in enumerate((o1, o2, o3))]
+        after=(mixed,),
+    )
     sent = call(
         to_planes_gains_kernel,
         "qkv_to_planes",
-        (shape(kept, qkv_lanes, dtype=f32),) + (shape(kept, qkv_lanes),) * 3,
+        (shape(kept, qkv_lanes, dtype=f32),)
+        + (shape(kept, qkv_lanes),) * 3
+        + (shape(length, width),) * 3,
         keep,
         got,
         gain_sums,
-            )
-    got = [swap_shard(s, i + 1) for i, s in enumerate(sent[1:])]
+        o1,
+        o2,
+        o3,
+    )
+    got = [swap_shard(s, i + 1) for i, s in enumerate(sent[1:4])]
+    received = [swap_seq(o, CORES * (j + 1)) for j, o in enumerate(sent[4:])]
 
     mine = call(
         functools.partial(place_kernel, 0),
@@ -776,23 +955,22 @@
         shape(CHIPS, half, ffn_lanes),
         *pieces_ffn,
         after=(sent[1],),
-            )
+    )
     owned_in, owned_back = call(
         ffn_owned_kernel,
         "ffn_owned",
         (shape(*w_in.shape, dtype=f32), shape(*w_back.shape, dtype=f32)),
         mine,
         swap_core(mine),
-            )
-    mixed, grad_tokens = call(
+    )
+    grad_tokens = call(
         last_kernel,
         "last",
-        (shape(1, length, width), shape(1, length, width)),
+        shape(1, length, width),
         last_own,
         *received,
         xs[0],
         dh,
-        hidden,
         gains,
         after=(sent[1],),
     )
@@ -801,19 +979,21 @@
         "qkv_gather",
         shape(CHIPS, kept, qkv_lanes),
         *over_chips(summed(sent[0], got, "qkv_sum")),
-            )
-    owned_qkv, owned_out, gain_sums = call(
+        after=(grad_tokens, owned_back),
+    )
+    owned_qkv, owned_out, grad_gain_one, grad_gain_two = call(
         qkv_owned_kernel,
         "qkv_owned",
         (
             shape(*w_qkv.shape, dtype=f32),
             shape(*w_out.shape, dtype=f32),
-            shape(EXTRA, local, dtype=f32),
+            shape(local, dtype=f32),
+            shape(local, dtype=f32),
         ),
         mine,
         swap_core(mine),
-            )
-    return (mixed, grad_tokens, gain_sums[0], owned_qkv, owned_out, gain_sums[1], owned_in, owned_back)
+    )
+    return (mixed, grad_tokens, grad_gain_one, owned_qkv, owned_out, grad_gain_two, owned_in, owned_back)
 
 
 def solution(mesh):

time: 190 us -> 156 us (0.82)
  waiting for transfers between devices: 91 us -> 58.6 us
  starting transfers between devices: 57.3 us -> 49.2 us
  Pallas kernels: 28 us -> 32.5 us
    ppermute x32 -> x35, waiting for transfers between devices: 60.1 us -> 35.7 us  [swap_seq(): return lax.ppermute(value, 'seq', [(i, i ^ bits) for i in range(count)])]
    ppermute x12 -> x10, starting transfers between devices: 26.2 us -> 14.8 us  [swap_shard(): return lax.ppermute(value, 'shard', [(i, i ^ bits) for i in range(count)])]
    ppermute x12 -> x10, waiting for transfers between devices: 30.9 us -> 22.9 us  [swap_shard(): return lax.ppermute(value, 'shard', [(i, i ^ bits) for i in range(count)])]
    pallas_call x21 -> x27, Pallas kernels: 28 us -> 32.5 us  [call(): pl.pallas_call(body, out_shape=outs, in_specs=specs, out_specs=jax.tree.m...]
    ppermute x32 -> x35, starting transfers between devices: 31.1 us -> 34.5 us  [swap_seq(): return lax.ppermute(value, 'seq', [(i, i ^ bits) for i in range(count)])]
    unnamed x18 -> x68, local copies, waits for them, and re-layouts: 5.42 us -> 8.15 us
    another operation x4 -> x1, local copies, waits for them, and re-layouts: 1.95 us -> 0.01 us  [shards(): angles = position[:, None] * jnp.tile(frequency, 4)[None]]
  transfers between devices with their start and end apart: 44 -> 45, of which waited for: 20 -> 20; matrix products, arithmetic and copies ran while one was open for 2% -> 2% of each run, Pallas kernels for 5% -> 15%
where the time goes in v3:
time: 156 us; the launch traced here: 155 us
  waiting for transfers between devices  58.6 us (38%)
  starting transfers between devices  49.2 us (32%)
  Pallas kernels  32.5 us (21%)
  local copies, waits for them, and re-layouts  9.17 us (6%)
  between operations  3.75 us (2%)
  other arithmetic  2.05 us (1%)
    ppermute x35, waiting for transfers between devices, swap_seq(): return lax.ppermute(value, 'seq', [(i, i ^ bits) for i in range(count)])  35.7 us
    ppermute x35, starting transfers between devices, swap_seq(): return lax.ppermute(value, 'seq', [(i, i ^ bits) for i in range(count)])  34.5 us
    pallas_call x27, Pallas kernels, call(): pl.pallas_call(body, out_shape=outs, in_specs=specs, out_specs=jax.tree.m...  32.5 us
    ppermute x10, waiting for transfers between devices, swap_shard(): return lax.ppermute(value, 'shard', [(i, i ^ bits) for i in range(count)])  22.9 us
    ppermute x10, starting transfers between devices, swap_shard(): return lax.ppermute(value, 'shard', [(i, i ^ bits) for i in range(count)])  14.8 us
    unnamed x68, local copies, waits for them, and re-layouts  8.15 us
  transfers between devices with their start and end apart: 45, of which 20 were waited for; matrix products, arithmetic and copies ran while one was open for 2% of the time, Pallas kernels for 15%

profile of v3, /device:TPU:0, one launch (start us, length us, event | category | flops | bytes accessed | tf_op | source)
XLA Modules:
  0.0 155.3 jit_solution(7444368890565393496)
XLA Ops:
  4.6 5.1 %collective-permute-start.5 = (bf16[144,576]{1,0:T(8,128)(2,1)S(1)}, bf16[144,576]{1,0:T(8,128)(2,1)S(1)}, u32[]{:S(2)}, u32[]{:S(2)}) collective-permute-start(bf16[144,576]{1,0:T(8,128)(2,1)S(1)} %qkv_piece.1.refs_0_.refs_2_), channel_id=1, source_target_pairs={{0,3},{1,2},{2,1},{3,0},{4,7},{5,6},{6,5},{7,4},{8,11},{9,10},{10,... | collective-permute-start | bytes 497672 | tf_op jit(solution)/shard_map/ppermute | solution.py:69
  10.3 2.6 %collective-permute-start.2 = (bf16[128,768]{1,0:T(8,128)(2,1)S(1)}, bf16[128,768]{1,0:T(8,128)(2,1)S(1)}, u32[]{:S(2)}, u32[]{:S(2)}) collective-permute-start(bf16[128,768]{1,0:T(8,128)(2,1)S(1)} %bitcast.19), channel_id=1, source_target_pairs={{0,24},{4,28},{8,16},{12,20},{16,8},{20,12},{24,0},{28,4},{1,25},{... | collective-permute-start | bytes 589832 | tf_op jit(solution)/shard_map/ppermute | solution.py:64
  18.8 4.1 %collective-permute-start.12 = (bf16[96,960]{1,0:T(8,128)(2,1)S(1)}, bf16[96,960]{1,0:T(8,128)(2,1)S(1)}, u32[]{:S(2)}, u32[]{:S(2)}) collective-permute-start(bf16[96,960]{1,0:T(8,128)(2,1)S(1)} %ffn_piece.1.refs_0_), channel_id=1, source_target_pairs={{0,1},{1,0},{2,3},{3,2},{4,5},{5,4},{6,7},{7,6},{8,9},{9,8},{10,11... | collective-permute-start | bytes 552968 | tf_op jit(solution)/shard_map/ppermute | solution.py:69
  22.9 2.5 %collective-permute-done.4.refs_2_ = bf16[144,576]{1,0:T(8,128)(2,1)S(1)} collective-permute-done((bf16[144,576]{1,0:T(8,128)(2,1)S(1)}, bf16[144,576]{1,0:T(8,128)(2,1)S(1)}, u32[]{:S(2)}, u32[]{:S(2)}) %collective-permute-start.4) | collective-permute-done | bytes 165920 | tf_op jit(solution)/shard_map/ppermute | solution.py:69
  33.0 3.4 %collective-permute-done.1.refs_2_.refs_1_.refs_6_.refs_4_ = bf16[256,768]{1,0:T(8,128)(2,1)S(1)} collective-permute-done((bf16[256,768]{1,0:T(8,128)(2,1)}, bf16[256,768]{1,0:T(8,128)(2,1)S(1)}, u32[]{:S(2)}, u32[]{:S(2)}) %collective-permute-start.1) | collective-permute-done | bytes 393248 | tf_op jit(solution)/shard_map/ppermute | solution.py:64
  42.2 5.1 %collective-permute-done.8.refs_4_.refs_9_ = bf16[2,128,768]{2,1,0:T(8,128)(2,1)S(1)} collective-permute-done((bf16[2,128,768]{2,1,0:T(8,128)(2,1)S(1)}, bf16[2,128,768]{2,1,0:T(8,128)(2,1)S(1)}, u32[]{:S(2)}, u32[]{:S(2)}) %collective-permute-start.8) | collective-permute-done | bytes 393248 | tf_op jit(solution)/shard_map/ppermute | solution.py:64
  47.3 2.3 %attend.1.refs_0_.refs_6_ = bf16[4,128,192]{2,1,0:T(8,128)(2,1)S(1)} custom-call(bf16[4,128,192]{2,1,0:T(8,128)(2,1)S(1)} %get-tuple-element.63.refs_0_, bf16[4,128,384]{2,1,0:T(8,128)(2,1)S(1)} %get-tuple-element.64.refs_1_, bf16[4,128,384]{2,1,0:T(8,128)(2,1)S(1)} %collective-permute-done.7.refs_2_, f32[4,128,256]{2,1,0:T(8,128)S(1)} %and_select_fusion.refs_3_, ...), custom_call_target="tpu_custom_call" | custom-call | flops 46000001024 | bytes 23 | tf_op jit(solution)/shard_map/attend/pallas_call | solution.py:109
  49.7 2.5 %collective-permute-start.11 = (bf16[4,128,192]{2,1,0:T(8,128)(2,1)S(1)}, bf16[4,128,192]{2,1,0:T(8,128)(2,1)S(1)}, u32[]{:S(2)}, u32[]{:S(2)}) collective-permute-start(bf16[4,128,192]{2,1,0:T(8,128)(2,1)S(1)} %attend.1.refs_0_.refs_6_), channel_id=1, source_target_pairs={{0,24},{4,28},{8,16},{12,20},{16,8},{20,12},{24,0},{28,4},{1,25},{... | collective-permute-start | bytes 589832 | tf_op jit(solution)/shard_map/ppermute | solution.py:64
  53.2 7.0 %collective-permute-done.13.refs_1_ = bf16[2,96,960]{2,1,0:T(8,128)(2,1)S(1)} collective-permute-done((bf16[2,96,960]{2,1,0:T(8,128)(2,1)S(1)}, bf16[2,96,960]{2,1,0:T(8,128)(2,1)S(1)}, u32[]{:S(2)}, u32[]{:S(2)}) %collective-permute-start.13) | collective-permute-done | bytes 368672 | tf_op jit(solution)/shard_map/ppermute | solution.py:69
  62.2 3.1 %collective-permute-done.16.refs_11_ = bf16[4,96,1728]{2,1,0:T(8,128)(2,1)S(1)} collective-permute-done((bf16[4,96,1728]{2,1,0:T(8,128)(2,1)S(1)}, bf16[4,96,1728]{2,1,0:T(8,128)(2,1)S(1)}, u32[]{:S(2)}, u32[]{:S(2)}) %collective-permute-start.16) | collective-permute-done | bytes 1327136 | tf_op jit(solution)/shard_map/ppermute | solution.py:64
  65.4 4.5 %ffn.1 = (f32[128,768]{1,0:T(8,128)S(1)}, bf16[128,768]{1,0:T(8,128)(2,1)S(1)}, bf16[128,768]{1,0:T(8,128)(2,1)S(1)}, bf16[128,768]{1,0:T(8,128)(2,1)S(1)}, f32[...) custom-call(bf16[4,128,192]{2,1,0:T(8,128)(2,1)S(1)} %attend.1.refs_, ...), custom_call_target="tpu_custom_call" | custom-call | flops 89999998976 | bytes 45 | tf_op jit(solution)/shard_map/ffn/pallas_call | solution.py:109
  76.0 3.4 %collective-permute-done.17.refs_1_ = bf16[128,768]{1,0:T(8,128)(2,1)S(1)} collective-permute-done((bf16[128,768]{1,0:T(8,128)(2,1)S(1)}, bf16[128,768]{1,0:T(8,128)(2,1)S(1)}, u32[]{:S(2)}, u32[]{:S(2)}) %collective-permute-start.17) | collective-permute-done | bytes 196640 | tf_op jit(solution)/shard_map/ppermute | solution.py:64
  79.4 4.9 %collective-permute-done.18.refs_2_ = bf16[128,768]{1,0:T(8,128)(2,1)S(1)} collective-permute-done((bf16[128,768]{1,0:T(8,128)(2,1)S(1)}, bf16[128,768]{1,0:T(8,128)(2,1)S(1)}, u32[]{:S(2)}, u32[]{:S(2)}) %collective-permute-start.18) | collective-permute-done | bytes 196640 | tf_op jit(solution)/shard_map/ppermute | solution.py:64
  90.7 2.8 %collective-permute-done.26.refs_7_.refs_13_ = bf16[128,768]{1,0:T(8,128)(2,1)S(1)} collective-permute-done((bf16[128,768]{1,0:T(8,128)(2,1)S(1)}, bf16[128,768]{1,0:T(8,128)(2,1)S(1)}, u32[]{:S(2)}, u32[]{:S(2)}) %collective-permute-start.26) | collective-permute-done | bytes 196640 | tf_op jit(solution)/shard_map/ppermute | solution.py:64
  97.6 7.0 %attend_back.1 = (f32[4,128,192]{2,1,0:T(8,128)S(1)}, f32[4,128,384]{2,1,0:T(8,128)S(1)}, bf16[4,128,384]{2,1,0:T(8,128)(2,1)S(1)}) custom-call(bf16[4,128,192]{2,1,0:T(8,128)(2,1)S(1)} %copy-done.32, bf16[4,128,384]{2,1,0:T(8,128)(2,1)S(1)} %copy-done.10, bf16[4,128,384]{2,1,0:T(8,128)(2,1)S(1)} %copy-done.12, f32[4,128,256]{2,1,0:T(8,128)S(1)} %and_select_fusion.refs_3_, ...), custom_call_target="tpu_custom_call" | custom-call | flops 138000007168 | bytes 69 | tf_op jit(solution)/shard_map/attend_back/pallas_call | solution.py:109
  105.5 1.8 %collective-permute-done.38.refs_1_ = bf16[2,96,960]{2,1,0:T(8,128)(2,1)} collective-permute-done((bf16[2,96,960]{2,1,0:T(8,128)(2,1)}, bf16[2,96,960]{2,1,0:T(8,128)(2,1)}, u32[]{:S(2)}, u32[]{:S(2)}) %collective-permute-start.38) | collective-permute-done | bytes 368672 | tf_op jit(solution)/shard_map/ppermute | solution.py:69
  108.8 2.3 %qkv_grads.1 = (f32[4,96,768]{2,1,0:T(8,128)S(1)}, bf16[4,96,768]{2,1,0:T(8,128)(2,1)S(1)}, bf16[512,576]{1,0:T(8,128)(2,1)S(1)}) custom-call(f32[4,128,192]{2,1,0:T(8,128)S(1)} %get-tuple-element.85.refs_5_.refs_0_.refs_2_, f32[4,128,384]{2,1,0:T(8,128)S(1)} %get-tuple-element.86.refs_1_, bf16[4,128,384]{2,1,0:T(8,128)(2,1)S(1)} %collective-permute-done.27.refs_2_, ...), custom_call_target="tpu_custom_call" | custom-call | flops 48000000000 | bytes 24 | tf_op jit(solution)/shard_map/qkv_grads/pallas_call | solution.py:109
  111.1 3.5 %collective-permute-done.39.refs_1_ = bf16[96,960]{1,0:T(8,128)(2,1)S(1)} collective-permute-done((bf16[96,960]{1,0:T(8,128)(2,1)S(1)}, bf16[96,960]{1,0:T(8,128)(2,1)S(1)}, u32[]{:S(2)}, u32[]{:S(2)}) %collective-permute-start.39) | collective-permute-done | bytes 184352 | tf_op jit(solution)/shard_map/ppermute | solution.py:69
  121.5 1.9 %collective-permute-start.34 = (bf16[112,768]{1,0:T(8,128)(2,1)S(1)}, bf16[112,768]{1,0:T(8,128)(2,1)S(1)}, u32[]{:S(2)}, u32[]{:S(2)}) collective-permute-start(bf16[112,768]{1,0:T(8,128)(2,1)S(1)} %get-tuple-element.106), channel_id=1, source_target_pairs={{0,3},{1,2},{2,1},{3,0},{4,7},{5,6},{6,5},{7,4},{8,11},{9,10},{10,... | collective-permute-start | bytes 516104 | tf_op jit(solution)/shard_map/ppermute | solution.py:69
  127.3 8.1 %collective-permute-done.33.refs_2_ = bf16[112,768]{1,0:T(8,128)(2,1)S(1)} collective-permute-done((bf16[112,768]{1,0:T(8,128)(2,1)S(1)}, bf16[112,768]{1,0:T(8,128)(2,1)S(1)}, u32[]{:S(2)}, u32[]{:S(2)}) %collective-permute-start.33) | collective-permute-done | bytes 172064 | tf_op jit(solution)/shard_map/ppermute | solution.py:69
  140.5 3.7 %collective-permute-done.31.refs_3_ = bf16[128,768]{1,0:T(8,128)(2,1)S(1)} collective-permute-done((bf16[128,768]{1,0:T(8,128)(2,1)S(1)}, bf16[128,768]{1,0:T(8,128)(2,1)S(1)}, u32[]{:S(2)}, u32[]{:S(2)}) %collective-permute-start.31) | collective-permute-done | bytes 196640 | tf_op jit(solution)/shard_map/ppermute | solution.py:64
  145.2 2.3 %ffn_owned.1 = (f32[192,2304]{1,0:T(8,128)}, f32[288,768]{1,0:T(8,128)}) custom-call(bf16[4,96,960]{2,1,0:T(8,128)(2,1)S(1)} %ffn_gather.1.refs_0_, bf16[4,96,960]{2,1,0:T(8,128)(2,1)S(1)} %collective-permute-done.43.refs_1_), custom_call_target="tpu_custom_call" | custom-call | flops 44000002048 | bytes 22 | tf_op jit(solution)/shard_map/ffn_owned/pallas_call | solution.py:109
  147.8 2.4 %collective-permute-done.36.refs_2_ = bf16[112,768]{1,0:T(8,128)(2,1)S(1)} collective-permute-done((bf16[112,768]{1,0:T(8,128)(2,1)S(1)}, bf16[112,768]{1,0:T(8,128)(2,1)S(1)}, u32[]{:S(2)}, u32[]{:S(2)}) %collective-permute-start.36) | collective-permute-done | bytes 172064 | tf_op jit(solution)/shard_map/ppermute | solution.py:64
  151.5 2.1 %collective-permute-done.44.refs_1_ = bf16[4,112,768]{2,1,0:T(8,128)(2,1)S(1)} collective-permute-done((bf16[4,112,768]{2,1,0:T(8,128)(2,1)S(1)}, bf16[4,112,768]{2,1,0:T(8,128)(2,1)S(1)}, u32[]{:S(2)}, u32[]{:S(2)}) %collective-permute-start.44) | collective-permute-done | bytes 688160 | tf_op jit(solution)/shard_map/ppermute | solution.py:64
  (177 shorter events, 63.0 us)
Async XLA Ops:
  4.6 14.3 %collective-permute-start.5 = (bf16[144,576]{1,0:T(8,128)(2,1)S(1)}, bf16[144,576]{1,0:T(8,128)(2,1)S(1)}, u32[]{:S(2)}, u32[]{:S(2)}) collective-permute-start(bf16[144,576]{1,0:T(8,128)(2,1)S(1)} %qkv_piece.1.refs_0_.refs_2_), channel_id=1, source_target_pairs={{0,3},{1,2},{2,1},{3,0},{4,7},{5,6},{6,5},{7,4},{8,11},{9,10},{10,... | collective-permute-start | bytes 497672 | tf_op jit(solution)/shard_map/ppermute | solution.py:69
  9.7 15.7 %collective-permute-start.4 = (bf16[144,576]{1,0:T(8,128)(2,1)S(1)}, bf16[144,576]{1,0:T(8,128)(2,1)S(1)}, u32[]{:S(2)}, u32[]{:S(2)}) collective-permute-start(bf16[144,576]{1,0:T(8,128)(2,1)S(1)} %qkv_piece.1.refs_0_.refs_2_), channel_id=1, source_target_pairs={{0,2},{1,3},{2,0},{3,1},{4,6},{5,7},{6,4},{7,5},{8,10},{9,11},{10,... | collective-permute-start | bytes 497672 | tf_op jit(solution)/shard_map/ppermute | solution.py:69
  9.7 18.0 %collective-permute-start.3 = (bf16[144,576]{1,0:T(8,128)(2,1)S(1)}, bf16[144,576]{1,0:T(8,128)(2,1)}, u32[]{:S(2)}, u32[]{:S(2)}) collective-permute-start(bf16[144,576]{1,0:T(8,128)(2,1)S(1)} %qkv_piece.1.refs_0_.refs_2_), channel_id=1, source_target_pairs={{0,1},{1,0},{2,3},{3,2},{4,5},{5,4},{6,7},{7,6},{8,9},{9,8},{10,11... | collective-permute-start | bytes 497672 | tf_op jit(solution)/shard_map/ppermute | solution.py:69
  10.3 21.1 %collective-permute-start.2 = (bf16[128,768]{1,0:T(8,128)(2,1)S(1)}, bf16[128,768]{1,0:T(8,128)(2,1)S(1)}, u32[]{:S(2)}, u32[]{:S(2)}) collective-permute-start(bf16[128,768]{1,0:T(8,128)(2,1)S(1)} %bitcast.19), channel_id=1, source_target_pairs={{0,24},{4,28},{8,16},{12,20},{16,8},{20,12},{24,0},{28,4},{1,25},{... | collective-permute-start | bytes 589832 | tf_op jit(solution)/shard_map/ppermute | solution.py:64
  12.9 20.1 %collective-permute-start = (bf16[128,768]{1,0:T(8,128)(2,1)S(1)}, bf16[128,768]{1,0:T(8,128)(2,1)S(1)}, u32[]{:S(2)}, u32[]{:S(2)}) collective-permute-start(bf16[128,768]{1,0:T(8,128)(2,1)S(1)} %bitcast.20), channel_id=1, source_target_pairs={{0,8},{4,12},{8,0},{12,4},{16,24},{20,28},{24,16},{28,20},{1,9},{5... | collective-permute-start | bytes 589832 | tf_op jit(solution)/shard_map/ppermute | solution.py:64
  18.8 20.8 %collective-permute-start.12 = (bf16[96,960]{1,0:T(8,128)(2,1)S(1)}, bf16[96,960]{1,0:T(8,128)(2,1)S(1)}, u32[]{:S(2)}, u32[]{:S(2)}) collective-permute-start(bf16[96,960]{1,0:T(8,128)(2,1)S(1)} %ffn_piece.1.refs_0_), channel_id=1, source_target_pairs={{0,1},{1,0},{2,3},{3,2},{4,5},{5,4},{6,7},{7,6},{8,9},{9,8},{10,11... | collective-permute-start | bytes 552968 | tf_op jit(solution)/shard_map/ppermute | solution.py:69
  26.1 10.3 %collective-permute-start.1 = (bf16[256,768]{1,0:T(8,128)(2,1)}, bf16[256,768]{1,0:T(8,128)(2,1)S(1)}, u32[]{:S(2)}, u32[]{:S(2)}) collective-permute-start(bf16[256,768]{1,0:T(8,128)(2,1)} %pad_maximum_fusion), channel_id=1, source_target_pairs={{0,16},{4,20},{8,24},{12,28},{16,0},{20,4},{24,8},{28,12},{1,17},{... | collective-permute-start | bytes 1179656 | tf_op jit(solution)/shard_map/ppermute | solution.py:64
  39.7 20.6 %collective-permute-start.13 = (bf16[2,96,960]{2,1,0:T(8,128)(2,1)S(1)}, bf16[2,96,960]{2,1,0:T(8,128)(2,1)S(1)}, u32[]{:S(2)}, u32[]{:S(2)}) collective-permute-start(bf16[2,96,960]{2,1,0:T(8,128)(2,1)S(1)} %in_pair.1.refs_2_.refs_0_), channel_id=1, source_target_pairs={{0,2},{1,3},{2,0},{3,1},{4,6},{5,7},{6,4},{7,5},{8,10},{9,11},{10,... | collective-permute-start | bytes 1105928 | tf_op jit(solution)/shard_map/ppermute | solution.py:69
  40.6 12.6 %collective-permute-start.15 = (bf16[2,4,48,384]{3,2,1,0:T(8,128)(2,1)S(1)}, bf16[2,4,48,384]{3,2,1,0:T(8,128)(2,1)S(1)}, u32[]{:S(2)}, u32[]{:S(2)}) collective-permute-start(bf16[2,4,48,384]{3,2,1,0:T(8,128)(2,1)S(1)} %out_pair.1.refs_2_), channel_id=1, source_target_pairs={{0,16},{4,20},{8,24},{12,28},{16,0},{20,4},{24,8},{28,12},{1,17},{... | collective-permute-start | bytes 884744 | tf_op jit(solution)/shard_map/ppermute | solution.py:64
  49.7 10.6 %collective-permute-start.11 = (bf16[4,128,192]{2,1,0:T(8,128)(2,1)S(1)}, bf16[4,128,192]{2,1,0:T(8,128)(2,1)S(1)}, u32[]{:S(2)}, u32[]{:S(2)}) collective-permute-start(bf16[4,128,192]{2,1,0:T(8,128)(2,1)S(1)} %attend.1.refs_0_.refs_6_), channel_id=1, source_target_pairs={{0,24},{4,28},{8,16},{12,20},{16,8},{20,12},{24,0},{28,4},{1,25},{... | collective-permute-start | bytes 589832 | tf_op jit(solution)/shard_map/ppermute | solution.py:64
  73.2 11.1 %collective-permute-start.18 = (bf16[128,768]{1,0:T(8,128)(2,1)S(1)}, bf16[128,768]{1,0:T(8,128)(2,1)S(1)}, u32[]{:S(2)}, u32[]{:S(2)}) collective-permute-start(bf16[128,768]{1,0:T(8,128)(2,1)S(1)} %get-tuple-element.71), channel_id=1, source_target_pairs={{0,16},{4,20},{8,24},{12,28},{16,0},{20,4},{24,8},{28,12},{1,17},{... | collective-permute-start | bytes 589832 | tf_op jit(solution)/shard_map/ppermute | solution.py:64
  73.9 10.4 %collective-permute-start.19 = (bf16[128,768]{1,0:T(8,128)(2,1)S(1)}, bf16[128,768]{1,0:T(8,128)(2,1)S(1)}, u32[]{:S(2)}, u32[]{:S(2)}) collective-permute-start(bf16[128,768]{1,0:T(8,128)(2,1)S(1)} %get-tuple-element.72), channel_id=1, source_target_pairs={{0,24},{4,28},{8,16},{12,20},{16,8},{20,12},{24,0},{28,4},{1,25},{... | collective-permute-start | bytes 589832 | tf_op jit(solution)/shard_map/ppermute | solution.py:64
  86.7 10.8 %collective-permute-start.24 = (bf16[128,768]{1,0:T(8,128)(2,1)S(1)}, bf16[128,768]{1,0:T(8,128)(2,1)S(1)}, u32[]{:S(2)}, u32[]{:S(2)}) collective-permute-start(bf16[128,768]{1,0:T(8,128)(2,1)S(1)} %get-tuple-element.79.refs_2_.refs_4_.refs_10_), channel_id=1, source_target_pairs={{0,8},{4,12},{8,0},{12,4},{16,24},{20,28},{24,16},{28,20},{1,9},{5... | collective-permute-start | bytes 589832 | tf_op jit(solution)/shard_map/ppermute | solution.py:64
  88.2 19.0 %collective-permute-start.38 = (bf16[2,96,960]{2,1,0:T(8,128)(2,1)}, bf16[2,96,960]{2,1,0:T(8,128)(2,1)}, u32[]{:S(2)}, u32[]{:S(2)}) collective-permute-start(bf16[2,96,960]{2,1,0:T(8,128)(2,1)} %get-tuple-element.78.refs_7_.refs_9_), channel_id=1, source_target_pairs={{0,2},{1,3},{2,0},{3,1},{4,6},{5,7},{6,4},{7,5},{8,10},{9,11},{10,... | collective-permute-start | bytes 1105928 | tf_op jit(solution)/shard_map/ppermute | solution.py:69
  89.9 14.7 %collective-permute-start.21 = (bf16[128,768]{1,0:T(8,128)(2,1)S(1)}, bf16[128,768]{1,0:T(8,128)(2,1)S(1)}, u32[]{:S(2)}, u32[]{:S(2)}) collective-permute-start(bf16[128,768]{1,0:T(8,128)(2,1)S(1)} %get-tuple-element.81), channel_id=1, source_target_pairs={{0,8},{4,12},{8,0},{12,4},{16,24},{20,28},{24,16},{28,20},{1,9},{5... | collective-permute-start | bytes 589832 | tf_op jit(solution)/shard_map/ppermute | solution.py:64
  93.5 11.1 %collective-permute-start.22 = (bf16[128,768]{1,0:T(8,128)(2,1)S(1)}, bf16[128,768]{1,0:T(8,128)(2,1)S(1)}, u32[]{:S(2)}, u32[]{:S(2)}) collective-permute-start(bf16[128,768]{1,0:T(8,128)(2,1)S(1)} %get-tuple-element.82), channel_id=1, source_target_pairs={{0,16},{4,20},{8,24},{12,28},{16,0},{20,4},{24,8},{28,12},{1,17},{... | collective-permute-start | bytes 589832 | tf_op jit(solution)/shard_map/ppermute | solution.py:64
  120.4 15.0 %collective-permute-start.33 = (bf16[112,768]{1,0:T(8,128)(2,1)S(1)}, bf16[112,768]{1,0:T(8,128)(2,1)S(1)}, u32[]{:S(2)}, u32[]{:S(2)}) collective-permute-start(bf16[112,768]{1,0:T(8,128)(2,1)S(1)} %get-tuple-element.105), channel_id=1, source_target_pairs={{0,2},{1,3},{2,0},{3,1},{4,6},{5,7},{6,4},{7,5},{8,10},{9,11},{10,... | collective-permute-start | bytes 516104 | tf_op jit(solution)/shard_map/ppermute | solution.py:69
  121.5 15.3 %collective-permute-start.34 = (bf16[112,768]{1,0:T(8,128)(2,1)S(1)}, bf16[112,768]{1,0:T(8,128)(2,1)S(1)}, u32[]{:S(2)}, u32[]{:S(2)}) collective-permute-start(bf16[112,768]{1,0:T(8,128)(2,1)S(1)} %get-tuple-element.106), channel_id=1, source_target_pairs={{0,3},{1,2},{2,1},{3,0},{4,7},{5,6},{6,5},{7,4},{8,11},{9,10},{10,... | collective-permute-start | bytes 516104 | tf_op jit(solution)/shard_map/ppermute | solution.py:69
  123.4 13.4 %collective-permute-start.32 = (bf16[112,768]{1,0:T(8,128)(2,1)S(1)}, bf16[112,768]{1,0:T(8,128)(2,1)S(1)}, u32[]{:S(2)}, u32[]{:S(2)}) collective-permute-start(bf16[112,768]{1,0:T(8,128)(2,1)S(1)} %get-tuple-element.103.refs_7_.refs_4_), channel_id=1, source_target_pairs={{0,1},{1,0},{2,3},{3,2},{4,5},{5,4},{6,7},{7,6},{8,9},{9,8},{10,11... | collective-permute-start | bytes 516104 | tf_op jit(solution)/shard_map/ppermute | solution.py:69
  124.9 13.6 %collective-permute-start.29 = (bf16[128,768]{1,0:T(8,128)(2,1)S(1)}, bf16[128,768]{1,0:T(8,128)(2,1)S(1)}, u32[]{:S(2)}, u32[]{:S(2)}) collective-permute-start(bf16[128,768]{1,0:T(8,128)(2,1)S(1)} %get-tuple-element.99), channel_id=1, source_target_pairs={{0,8},{4,12},{8,0},{12,4},{16,24},{20,28},{24,16},{28,20},{1,9},{5... | collective-permute-start | bytes 589832 | tf_op jit(solution)/shard_map/ppermute | solution.py:64
  125.9 13.2 %collective-permute-start.30 = (bf16[128,768]{1,0:T(8,128)(2,1)S(1)}, bf16[128,768]{1,0:T(8,128)(2,1)S(1)}, u32[]{:S(2)}, u32[]{:S(2)}) collective-permute-start(bf16[128,768]{1,0:T(8,128)(2,1)S(1)} %get-tuple-element.100), channel_id=1, source_target_pairs={{0,16},{4,20},{8,24},{12,28},{16,0},{20,4},{24,8},{28,12},{1,17},{... | collective-permute-start | bytes 589832 | tf_op jit(solution)/shard_map/ppermute | solution.py:64
  136.9 10.9 %collective-permute-start.37 = (bf16[112,768]{1,0:T(8,128)(2,1)S(1)}, bf16[112,768]{1,0:T(8,128)(2,1)S(1)}, u32[]{:S(2)}, u32[]{:S(2)}) collective-permute-start(bf16[112,768]{1,0:T(8,128)(2,1)S(1)} %qkv_sum.1.refs_0_), channel_id=1, source_target_pairs={{0,24},{4,28},{8,16},{12,20},{16,8},{20,12},{24,0},{28,4},{1,25},{... | collective-permute-start | bytes 516104 | tf_op jit(solution)/shard_map/ppermute | solution.py:64
  138.4 11.7 %collective-permute-start.36 = (bf16[112,768]{1,0:T(8,128)(2,1)S(1)}, bf16[112,768]{1,0:T(8,128)(2,1)S(1)}, u32[]{:S(2)}, u32[]{:S(2)}) collective-permute-start(bf16[112,768]{1,0:T(8,128)(2,1)S(1)} %qkv_sum.1.refs_0_), channel_id=1, source_target_pairs={{0,16},{4,20},{8,24},{12,28},{16,0},{20,4},{24,8},{28,12},{1,17},{... | collective-permute-start | bytes 516104 | tf_op jit(solution)/shard_map/ppermute | solution.py:64
  139.0 11.1 %collective-permute-start.35 = (bf16[112,768]{1,0:T(8,128)(2,1)S(1)}, bf16[112,768]{1,0:T(8,128)(2,1)S(1)}, u32[]{:S(2)}, u32[]{:S(2)}) collective-permute-start(bf16[112,768]{1,0:T(8,128)(2,1)S(1)} %qkv_sum.1.refs_0_), channel_id=1, source_target_pairs={{0,8},{4,12},{8,0},{12,4},{16,24},{20,28},{24,16},{28,20},{1,9},{5... | collective-permute-start | bytes 516104 | tf_op jit(solution)/shard_map/ppermute | solution.py:64
  (55 other events, 310.1 us)

commit v4 on v3

--- a/solution.py
+++ b/solution.py
@@ -41,6 +41,10 @@
     "da": 1.5,
     "qkv_to_planes": 0.8,
     "qkv_gather": 0.6,
+    "last_packet": 0.5,
+    "ffn_total": 0.4,
+    "ffn_gather": 0.5,
+    "qkv_sum": 0.4,
     "last": 0.6,
     "ffn_owned": 2.2,
     "qkv_owned": 1.7,
@@ -167,19 +171,13 @@
         copy.wait()
 
 
-def qkv_piece_kernel(where, w_qkv, w_out, gain_one, gain_two, out, rows, part, sems):
+def qkv_piece_kernel(where, w_qkv, part, gains, out, rows, sems):
     chip, core = where[0], where[1]
     half = w_qkv.shape[0] // CORES
     width = w_qkv.shape[1] // 3
     local = width // CHIPS
     size, lanes = part.shape
-    copied(
-        (
-            (w_qkv.at[rows_at(core * half, half), :], rows),
-            (w_out.at[rows_at(chip * size, size), lanes_at(core * lanes, lanes)], part),
-        ),
-        sems,
-    )
+    copied(((w_qkv.at[rows_at(core * half, half), :], rows),), sems)
     for b in range(CHIPS):
 
         @pl.when(chip == b)
@@ -188,9 +186,8 @@
                 at = p * width + b * local
                 out[:half, p * local : (p + 1) * local] = rows[:, at : at + local]
 
-    out[half : half + EXTRA, :] = extra_rows(
-        gain_one[...].astype(f32)[None], gain_two[...].astype(f32)[None], 3 * local
-    ).astype(bf16)
+    both = gains[...].astype(f32)
+    out[half : half + EXTRA, :] = extra_rows(both[0:1, :], both[1:2, :], 3 * local).astype(bf16)
     at = half + EXTRA
     out[at : at + 16, :lanes] = part[:16, :]
     out[at + 16 :, :lanes] = part[16:32, :]
@@ -244,6 +241,34 @@
 def up_pair_kernel(where, own, both, out):
     out[0] = own[...]
     out[1] = both[own.shape[0] :, :]
+
+
+def last_packet_kernel(where, total, *refs):
+    half, lanes = total.shape
+    rows, width = refs[0].shape
+    spare = lanes - width
+    for ref, out in zip(refs[: len(refs) // 2], refs[len(refs) // 2 :]):
+        out[:rows, :] = ref[...]
+        out[rows : rows + half, :] = total[:, :width]
+        for i in range(half // 32):
+            at = slice(i * spare, (i + 1) * spare)
+            out[rows + half :, at] = total[i * 32 : (i + 1) * 32, width:]
+        blank = width - half // 32 * spare
+        out[rows + half :, width - blank :] = jnp.zeros((32, blank), bf16)
+
+
+def ffn_gather_kernel(where, total, r1, r2, r3, out):
+    half, lanes = total.shape
+    width = r1.shape[1]
+    spare = lanes - width
+    rows = r1.shape[0] - half - 32
+    out[where[0]] = total[...]
+    for j, ref in enumerate((r1, r2, r3)):
+        at = where[0] ^ (j + 1)
+        out[at, :, :width] = ref[rows : rows + half, :]
+        for i in range(half // 32):
+            piece = ref[rows + half :, i * spare : (i + 1) * spare]
+            out[at, i * 32 : (i + 1) * 32, width:] = piece
 
 
 def pair_kernel(where, first, second, out):
@@ -579,9 +604,7 @@
     out[...] = (own[...] + got[...].astype(f32)).astype(out.dtype)
 
 
-def to_planes_gains_kernel(where, keep, got, gains, d1, d2, d3, own, o1, o2, o3, e1, e2, e3):
-    for ref, out in ((d1, e1), (d2, e2), (d3, e3)):
-        out[...] = ref[...]
+def to_planes_gains_kernel(where, keep, got, gains, own, o1, o2, o3):
     plane = where[2]
     half = keep.shape[1]
     own[:half, :] = keep[plane] + got[plane].astype(f32)
@@ -598,7 +621,9 @@
 
 
 def last_kernel(where, own, r1, r2, r3, x0, dh, gains, grad_out):
-    total = own[...] + r1[...].astype(f32) + r2[...].astype(f32) + r3[...].astype(f32)
+    total = own[...]
+    for ref in (r1, r2, r3):
+        total = total + ref[: own.shape[0], :].astype(f32)
     normed, factor = norm_parts(x0[...].astype(f32))
     grad = dh[...] + norm_inward(total, gains[0:1, :], normed, factor)
     grad_out[0] = grad.astype(bf16)
@@ -668,20 +693,24 @@
         "qkv_piece",
         shape(kept + 32, 3 * local),
         w_qkv,
-        w_out,
-        norm_gain,
-        ffn_gain,
-        held=2,
-        scratch=(
-            pltpu.VMEM((half, 3 * width), bf16),
-            pltpu.VMEM((out_rows, lanes), bf16),
-            pltpu.SemaphoreType.DMA((2,)),
-        ),
+        lax.dynamic_slice(w_out, (chip * out_rows, core * lanes), (out_rows, lanes)),
+        jnp.stack([norm_gain, ffn_gain]),
+        held=1,
+        scratch=(pltpu.VMEM((half, 3 * width), bf16), pltpu.SemaphoreType.DMA((1,))),
     )
     pieces = over_planes(piece)
     both = jnp.concatenate([tokens[0], cotangent[0]], axis=0)
     both_near = swap_seq(both, 2 * CORES)
     xs = [tokens[0], swap_seq(tokens[0], CORES), both_near, swap_seq(tokens[0], 3 * CORES)]
+    mine, out_own = call(
+        qkv_place_kernel,
+        "qkv_place",
+        (
+            shape(PLANES, kept, 3 * local),
+            shape(PLANES, out_rows, lanes),
+        ),
+        *pieces,
+    )
     piece = call(
         ffn_piece_kernel,
         "ffn_piece",
@@ -694,18 +723,9 @@
             pltpu.VMEM((w_back.shape[0], lanes), bf16),
             pltpu.SemaphoreType.DMA((2,)),
         ),
-        after=(piece,),
+        after=(mine,),
     )
     in_near = swap_shard(piece, 1)
-    mine, out_own = call(
-        qkv_place_kernel,
-        "qkv_place",
-        (
-            shape(PLANES, kept, 3 * local),
-            shape(PLANES, out_rows, lanes),
-        ),
-        *pieces,
-    )
     out_near = swap_seq(out_own, CORES)
     other = swap_core(mine)
 
@@ -742,10 +762,6 @@
         sine,
     )
     kv_other = swap_core(kv)
-    in_pair = call(
-        pair_kernel, "in_pair", shape(2, half, in_sent), piece, in_near, after=(gains,)
-    )
-    in_far = swap_shard(in_pair, 2)
 
     def beyond(value):
         pairs = []
@@ -761,8 +777,12 @@
         last = lax.dynamic_index_in_dim(kv, chip ^ (CHIPS - 1), 0, False)[length - HALF :]
         rim = (beyond(jnp.where(core == 0, first, last)),)
 
-    out_pair = call(pair_kernel, "out_pair", shape(2, *out_own.shape), out_own, out_near, after=(in_pair,))
+    out_pair = call(pair_kernel, "out_pair", shape(2, *out_own.shape), out_own, out_near, after=(gains,))
     out_far = swap_seq(out_pair, 2 * CORES)
+    in_pair = call(
+        pair_kernel, "in_pair", shape(2, half, in_sent), piece, in_near, after=(out_pair,)
+    )
+    in_far = swap_shard(in_pair, 2)
     up_pair = call(up_pair_kernel, "up_pair", shape(2, length, width), cotangent[0], both_near, after=(gains,))
     gys = (up_pair, swap_seq(up_pair, CORES))
     attn = call(
@@ -774,9 +794,9 @@
         kv_other,
         bias,
         *rim,
-        after=(gys[1],),
-    )
-    attns = over_chips(attn)
+    )
+    last_attn = call(copy_kernel, "attn_copy", shape(*attn.shape), attn, after=(gys[1],))
+    attns = [attn, swap_seq(attn, CORES), swap_seq(attn, 2 * CORES), swap_seq(last_attn, 3 * CORES)]
     in_mine = call(
         ffn_place_kernel,
         "ffn_place",
@@ -903,6 +923,7 @@
         *rim,
         scratch=(pltpu.VMEM((width, qkv_lanes), f32), pltpu.VMEM((many, local), bf16)),
     )
+    got = swap_core(away)
     own_ffn, sent_near = call(
         ffn_near_kernel,
         "ffn_near",
@@ -917,10 +938,9 @@
         shape(half, ffn_lanes, dtype=f32 if edges else bf16),
         own_ffn,
         swap_shard(sent_near, 1),
-        after=(away,),
-    )
-    pieces_ffn = over_chips(over_groups(total, bf16))
-    got = swap_core(away)
+        after=(got,),
+    )
+    total = over_groups(total, bf16)
     last_own, o1, o2, o3, gain_sums = call(
         da_kernel,
         "da",
@@ -937,24 +957,23 @@
         to_planes_gains_kernel,
         "qkv_to_planes",
         (shape(kept, qkv_lanes, dtype=f32),)
-        + (shape(kept, qkv_lanes),) * 3
-        + (shape(length, width),) * 3,
+        + (shape(kept, qkv_lanes),) * 3,
         keep,
         got,
         gain_sums,
-        o1,
-        o2,
-        o3,
     )
     got = [swap_shard(s, i + 1) for i, s in enumerate(sent[1:4])]
-    received = [swap_seq(o, CORES * (j + 1)) for j, o in enumerate(sent[4:])]
+    packet = shape(length + half + 32, width)
+    packets = call(last_packet_kernel, "last_packet", (packet,) * 2, total, o1, o2, after=(sent[1],))
+    packets += call(last_packet_kernel, "third_packet", (packet,), total, o3, after=(got[0],))
+    received = [swap_seq(o, CORES * (j + 1)) for j, o in enumerate(packets)]
 
     mine = call(
-        functools.partial(place_kernel, 0),
+        ffn_gather_kernel,
         "ffn_gather",
         shape(CHIPS, half, ffn_lanes),
-        *pieces_ffn,
-        after=(sent[1],),
+        total,
+        *received,
     )
     owned_in, owned_back = call(
         ffn_owned_kernel,

time: 156 us -> 146 us (0.936)
  starting transfers between devices: 49.2 us -> 43 us
  local copies, waits for them, and re-layouts: 9.17 us -> 5.62 us
    unnamed x68 -> x58, local copies, waits for them, and re-layouts: 8.15 us -> 2.51 us
    ppermute x10, waiting for transfers between devices: 22.9 us -> 27.6 us  [swap_shard(): return lax.ppermute(value, 'shard', [(i, i ^ bits) for i in range(count)])]
    ppermute x35 -> x32, starting transfers between devices: 34.5 us -> 30 us  [swap_seq(): return lax.ppermute(value, 'seq', [(i, i ^ bits) for i in range(count)])]
    ppermute x35 -> x32, waiting for transfers between devices: 35.7 us -> 32.4 us  [swap_seq(): return lax.ppermute(value, 'seq', [(i, i ^ bits) for i in range(count)])]
    ppermute x10, starting transfers between devices: 14.8 us -> 13 us  [swap_shard(): return lax.ppermute(value, 'shard', [(i, i ^ bits) for i in range(count)])]
    pallas_call x27 -> x30, Pallas kernels: 32.5 us -> 31.7 us  [call(): pl.pallas_call(body, out_shape=outs, in_specs=specs, out_specs=jax.tree.m...]
  transfers between devices with their start and end apart: 45 -> 42, of which waited for: 20 -> 19; matrix products, arithmetic and copies ran while one was open for 2% -> 2% of each run, Pallas kernels for 15% -> 16%
where the time goes in v4:
time: 146 us; the launch traced here: 145 us
  waiting for transfers between devices  60 us (41%)
  starting transfers between devices  43 us (29%)
  Pallas kernels  31.7 us (22%)
  local copies, waits for them, and re-layouts  5.62 us (4%)
  between operations  3.85 us (3%)
    ppermute x32, waiting for transfers between devices, swap_seq(): return lax.ppermute(value, 'seq', [(i, i ^ bits) for i in range(count)])  32.4 us
    pallas_call x30, Pallas kernels, call(): pl.pallas_call(body, out_shape=outs, in_specs=specs, out_specs=jax.tree.m...  31.7 us
    ppermute x32, starting transfers between devices, swap_seq(): return lax.ppermute(value, 'seq', [(i, i ^ bits) for i in range(count)])  30 us
    ppermute x10, waiting for transfers between devices, swap_shard(): return lax.ppermute(value, 'shard', [(i, i ^ bits) for i in range(count)])  27.6 us
    ppermute x10, starting transfers between devices, swap_shard(): return lax.ppermute(value, 'shard', [(i, i ^ bits) for i in range(count)])  13 us
  transfers between devices with their start and end apart: 42, of which 19 were waited for; matrix products, arithmetic and copies ran while one was open for 2% of the time, Pallas kernels for 16%

profile of v4, /device:TPU:0, one launch (start us, length us, event | category | flops | bytes accessed | tf_op | source)
XLA Modules:
  0.0 145.4 jit_solution(16906618342673501732)
XLA Ops:
  4.4 5.1 %collective-permute-start.5 = (bf16[144,576]{1,0:T(8,128)(2,1)S(1)}, bf16[144,576]{1,0:T(8,128)(2,1)S(1)}, u32[]{:S(2)}, u32[]{:S(2)}) collective-permute-start(bf16[144,576]{1,0:T(8,128)(2,1)S(1)} %qkv_piece.1.refs_0_), channel_id=1, source_target_pairs={{0,3},{1,2},{2,1},{3,0},{4,7},{5,6},{6,5},{7,4},{8,11},{9,10},{10,... | collective-permute-start | bytes 497672 | tf_op jit(solution)/shard_map/ppermute | solution.py:73
  10.1 2.6 %collective-permute-start.2 = (bf16[128,768]{1,0:T(8,128)(2,1)S(1)}, bf16[128,768]{1,0:T(8,128)(2,1)S(1)}, u32[]{:S(2)}, u32[]{:S(2)}) collective-permute-start(bf16[128,768]{1,0:T(8,128)(2,1)S(1)} %bitcast.19), channel_id=1, source_target_pairs={{0,24},{4,28},{8,16},{12,20},{16,8},{20,12},{24,0},{28,4},{1,25},{... | collective-permute-start | bytes 589832 | tf_op jit(solution)/shard_map/ppermute | solution.py:68
  18.8 6.4 %collective-permute-done.4.refs_2_ = bf16[144,576]{1,0:T(8,128)(2,1)S(1)} collective-permute-done((bf16[144,576]{1,0:T(8,128)(2,1)S(1)}, bf16[144,576]{1,0:T(8,128)(2,1)S(1)}, u32[]{:S(2)}, u32[]{:S(2)}) %collective-permute-start.4) | collective-permute-done | bytes 165920 | tf_op jit(solution)/shard_map/ppermute | solution.py:73
  34.7 2.7 %collective-permute-start.14 = (bf16[2,96,960]{2,1,0:T(8,128)(2,1)S(1)}, bf16[2,96,960]{2,1,0:T(8,128)(2,1)S(1)}, u32[]{:S(2)}, u32[]{:S(2)}) collective-permute-start(bf16[2,96,960]{2,1,0:T(8,128)(2,1)S(1)} %in_pair.1.refs_0_), channel_id=1, source_target_pairs={{0,2},{1,3},{2,0},{3,1},{4,6},{5,7},{6,4},{7,5},{8,10},{9,11},{10,... | collective-permute-start | bytes 1105928 | tf_op jit(solution)/shard_map/ppermute | solution.py:73
  37.4 2.3 %attend.1.refs_0_.refs_6_ = bf16[4,128,192]{2,1,0:T(8,128)(2,1)S(1)} custom-call(bf16[4,128,192]{2,1,0:T(8,128)(2,1)S(1)} %get-tuple-element.62.refs_0_, bf16[4,128,384]{2,1,0:T(8,128)(2,1)S(1)} %get-tuple-element.63.refs_1_, bf16[4,128,384]{2,1,0:T(8,128)(2,1)S(1)} %collective-permute-done.7.refs_2_, f32[4,128,256]{2,1,0:T(8,128)S(1)} %and_select_fusion.refs_3_), custom_call_target="tpu_custom_call" | custom-call | flops 46000001024 | bytes 23 | tf_op jit(solution)/shard_map/attend/pallas_call | solution.py:113
  39.8 3.2 %collective-permute-done.10.refs_1_.refs_9_.refs_4_ = bf16[2,128,768]{2,1,0:T(8,128)(2,1)S(1)} collective-permute-done((bf16[2,128,768]{2,1,0:T(8,128)(2,1)S(1)}, bf16[2,128,768]{2,1,0:T(8,128)(2,1)S(1)}, u32[]{:S(2)}, u32[]{:S(2)}) %collective-permute-start.10) | collective-permute-done | bytes 393248 | tf_op jit(solution)/shard_map/ppermute | solution.py:68
  46.6 9.0 %collective-permute-done.14.refs_1_ = bf16[2,96,960]{2,1,0:T(8,128)(2,1)S(1)} collective-permute-done((bf16[2,96,960]{2,1,0:T(8,128)(2,1)S(1)}, bf16[2,96,960]{2,1,0:T(8,128)(2,1)S(1)}, u32[]{:S(2)}, u32[]{:S(2)}) %collective-permute-start.14) | collective-permute-done | bytes 368672 | tf_op jit(solution)/shard_map/ppermute | solution.py:73
  56.4 3.1 %collective-permute-done.16.refs_11_ = bf16[4,96,1728]{2,1,0:T(8,128)(2,1)S(1)} collective-permute-done((bf16[4,96,1728]{2,1,0:T(8,128)(2,1)S(1)}, bf16[4,96,1728]{2,1,0:T(8,128)(2,1)S(1)}, u32[]{:S(2)}, u32[]{:S(2)}) %collective-permute-start.16) | collective-permute-done | bytes 1327136 | tf_op jit(solution)/shard_map/ppermute | solution.py:68
  59.5 4.5 %ffn.1 = (f32[128,768]{1,0:T(8,128)S(1)}, bf16[128,768]{1,0:T(8,128)(2,1)S(1)}, bf16[128,768]{1,0:T(8,128)(2,1)S(1)}, bf16[128,768]{1,0:T(8,128)(2,1)S(1)}, f32[...) custom-call(bf16[4,128,192]{2,1,0:T(8,128)(2,1)S(1)} %attend.1.refs_, ...), custom_call_target="tpu_custom_call" | custom-call | flops 89999998976 | bytes 45 | tf_op jit(solution)/shard_map/ffn/pallas_call | solution.py:113
  67.4 1.9 %collective-permute-start.19 = (bf16[128,768]{1,0:T(8,128)(2,1)S(1)}, bf16[128,768]{1,0:T(8,128)(2,1)S(1)}, u32[]{:S(2)}, u32[]{:S(2)}) collective-permute-start(bf16[128,768]{1,0:T(8,128)(2,1)S(1)} %get-tuple-element.71), channel_id=1, source_target_pairs={{0,24},{4,28},{8,16},{12,20},{16,8},{20,12},{24,0},{28,4},{1,25},{... | collective-permute-start | bytes 589832 | tf_op jit(solution)/shard_map/ppermute | solution.py:68
  70.1 3.4 %collective-permute-done.17.refs_1_ = bf16[128,768]{1,0:T(8,128)(2,1)S(1)} collective-permute-done((bf16[128,768]{1,0:T(8,128)(2,1)S(1)}, bf16[128,768]{1,0:T(8,128)(2,1)S(1)}, u32[]{:S(2)}, u32[]{:S(2)}) %collective-permute-start.17) | collective-permute-done | bytes 196640 | tf_op jit(solution)/shard_map/ppermute | solution.py:68
  73.5 4.5 %collective-permute-done.19.refs_3_ = bf16[128,768]{1,0:T(8,128)(2,1)S(1)} collective-permute-done((bf16[128,768]{1,0:T(8,128)(2,1)S(1)}, bf16[128,768]{1,0:T(8,128)(2,1)S(1)}, u32[]{:S(2)}, u32[]{:S(2)}) %collective-permute-start.19) | collective-permute-done | bytes 196640 | tf_op jit(solution)/shard_map/ppermute | solution.py:68
  78.4 1.8 %collective-permute-start.26 = (bf16[128,768]{1,0:T(8,128)(2,1)S(1)}, bf16[128,768]{1,0:T(8,128)(2,1)S(1)}, u32[]{:S(2)}, u32[]{:S(2)}) collective-permute-start(bf16[128,768]{1,0:T(8,128)(2,1)S(1)} %get-tuple-element.78.refs_2_.refs_4_.refs_10_), channel_id=1, source_target_pairs={{0,24},{4,28},{8,16},{12,20},{16,8},{20,12},{24,0},{28,4},{1,25},{... | collective-permute-start | bytes 589832 | tf_op jit(solution)/shard_map/ppermute | solution.py:68
  83.6 3.6 %collective-permute-done.26.refs_7_.refs_13_ = bf16[128,768]{1,0:T(8,128)(2,1)S(1)} collective-permute-done((bf16[128,768]{1,0:T(8,128)(2,1)S(1)}, bf16[128,768]{1,0:T(8,128)(2,1)S(1)}, u32[]{:S(2)}, u32[]{:S(2)}) %collective-permute-start.26) | collective-permute-done | bytes 196640 | tf_op jit(solution)/shard_map/ppermute | solution.py:68
  87.9 2.2 %collective-permute-done.25.refs_6_.refs_12_ = bf16[128,768]{1,0:T(8,128)(2,1)S(1)} collective-permute-done((bf16[128,768]{1,0:T(8,128)(2,1)S(1)}, bf16[128,768]{1,0:T(8,128)(2,1)S(1)}, u32[]{:S(2)}, u32[]{:S(2)}) %collective-permute-start.25) | collective-permute-done | bytes 196640 | tf_op jit(solution)/shard_map/ppermute | solution.py:68
  91.5 7.0 %attend_back.1 = (f32[4,128,192]{2,1,0:T(8,128)S(1)}, f32[4,128,384]{2,1,0:T(8,128)S(1)}, bf16[4,128,384]{2,1,0:T(8,128)(2,1)S(1)}) custom-call(bf16[4,128,192]{2,1,0:T(8,128)(2,1)S(1)} %copy-done.27, bf16[4,128,384]{2,1,0:T(8,128)(2,1)S(1)} %copy-done.12, bf16[4,128,384]{2,1,0:T(8,128)(2,1)S(1)} %copy-done.14, f32[4,128,256]{2,1,0:T(8,128)S(1)} %copy-done.1, ...), custom_call_target="tpu_custom_call" | custom-call | flops 138000007168 | bytes 69 | tf_op jit(solution)/shard_map/attend_back/pallas_call | solution.py:113
  99.4 1.8 %collective-permute-done.28.refs_1_ = bf16[2,96,960]{2,1,0:T(8,128)(2,1)} collective-permute-done((bf16[2,96,960]{2,1,0:T(8,128)(2,1)}, bf16[2,96,960]{2,1,0:T(8,128)(2,1)}, u32[]{:S(2)}, u32[]{:S(2)}) %collective-permute-start.28) | collective-permute-done | bytes 368672 | tf_op jit(solution)/shard_map/ppermute | solution.py:73
  102.6 2.3 %qkv_grads.1 = (f32[4,96,768]{2,1,0:T(8,128)S(1)}, bf16[4,96,768]{2,1,0:T(8,128)(2,1)S(1)}, bf16[512,576]{1,0:T(8,128)(2,1)S(1)}) custom-call(f32[4,128,192]{2,1,0:T(8,128)S(1)} %get-tuple-element.84.refs_5_.refs_0_.refs_2_, f32[4,128,384]{2,1,0:T(8,128)S(1)} %get-tuple-element.85.refs_1_, bf16[4,128,384]{2,1,0:T(8,128)(2,1)S(1)} %collective-permute-done.27.refs_2_, ...), custom_call_target="tpu_custom_call" | custom-call | flops 48000000000 | bytes 24 | tf_op jit(solution)/shard_map/qkv_grads/pallas_call | solution.py:113
  107.2 1.9 %collective-permute-start.35 = (bf16[112,768]{1,0:T(8,128)(2,1)S(1)}, bf16[112,768]{1,0:T(8,128)(2,1)S(1)}, u32[]{:S(2)}, u32[]{:S(2)}) collective-permute-start(bf16[112,768]{1,0:T(8,128)(2,1)S(1)} %get-tuple-element.106), channel_id=1, source_target_pairs={{0,2},{1,3},{2,0},{3,1},{4,6},{5,7},{6,4},{7,5},{8,10},{9,11},{10,... | collective-permute-start | bytes 516104 | tf_op jit(solution)/shard_map/ppermute | solution.py:73
  109.1 2.5 %collective-permute-start.36 = (bf16[112,768]{1,0:T(8,128)(2,1)S(1)}, bf16[112,768]{1,0:T(8,128)(2,1)S(1)}, u32[]{:S(2)}, u32[]{:S(2)}) collective-permute-start(bf16[112,768]{1,0:T(8,128)(2,1)S(1)} %get-tuple-element.107), channel_id=1, source_target_pairs={{0,3},{1,2},{2,1},{3,0},{4,7},{5,6},{6,5},{7,4},{8,11},{9,10},{10,... | collective-permute-start | bytes 516104 | tf_op jit(solution)/shard_map/ppermute | solution.py:73
  113.9 9.4 %collective-permute-done.33.refs_2_.refs_1_ = bf16[112,768]{1,0:T(8,128)(2,1)S(1)} collective-permute-done((bf16[112,768]{1,0:T(8,128)(2,1)S(1)}, bf16[112,768]{1,0:T(8,128)(2,1)S(1)}, u32[]{:S(2)}, u32[]{:S(2)}) %collective-permute-start.33) | collective-permute-done | bytes 172064 | tf_op jit(solution)/shard_map/ppermute | solution.py:73
  128.6 7.0 %collective-permute-done.34.refs_3_ = bf16[256,768]{1,0:T(8,128)(2,1)S(1)} collective-permute-done((bf16[256,768]{1,0:T(8,128)(2,1)S(1)}, bf16[256,768]{1,0:T(8,128)(2,1)S(1)}, u32[]{:S(2)}, u32[]{:S(2)}) %collective-permute-start.34) | collective-permute-done | bytes 393248 | tf_op jit(solution)/shard_map/ppermute | solution.py:68
  138.0 2.3 %ffn_owned.1 = (f32[192,2304]{1,0:T(8,128)}, f32[288,768]{1,0:T(8,128)}) custom-call(bf16[4,96,960]{2,1,0:T(8,128)(2,1)S(1)} %ffn_gather.1.refs_0_, bf16[4,96,960]{2,1,0:T(8,128)(2,1)S(1)} %collective-permute-done.40.refs_1_), custom_call_target="tpu_custom_call" | custom-call | flops 44000002048 | bytes 22 | tf_op jit(solution)/shard_map/ffn_owned/pallas_call | solution.py:113
  141.8 2.0 %collective-permute-done.41.refs_1_ = bf16[4,112,768]{2,1,0:T(8,128)(2,1)S(1)} collective-permute-done((bf16[4,112,768]{2,1,0:T(8,128)(2,1)S(1)}, bf16[4,112,768]{2,1,0:T(8,128)(2,1)S(1)}, u32[]{:S(2)}, u32[]{:S(2)}) %collective-permute-start.41) | collective-permute-done | bytes 688160 | tf_op jit(solution)/shard_map/ppermute | solution.py:68
  (168 shorter events, 49.1 us)
Async XLA Ops:
  4.4 14.0 %collective-permute-start.5 = (bf16[144,576]{1,0:T(8,128)(2,1)S(1)}, bf16[144,576]{1,0:T(8,128)(2,1)S(1)}, u32[]{:S(2)}, u32[]{:S(2)}) collective-permute-start(bf16[144,576]{1,0:T(8,128)(2,1)S(1)} %qkv_piece.1.refs_0_), channel_id=1, source_target_pairs={{0,3},{1,2},{2,1},{3,0},{4,7},{5,6},{6,5},{7,4},{8,11},{9,10},{10,... | collective-permute-start | bytes 497672 | tf_op jit(solution)/shard_map/ppermute | solution.py:73
  9.5 15.6 %collective-permute-start.4 = (bf16[144,576]{1,0:T(8,128)(2,1)S(1)}, bf16[144,576]{1,0:T(8,128)(2,1)S(1)}, u32[]{:S(2)}, u32[]{:S(2)}) collective-permute-start(bf16[144,576]{1,0:T(8,128)(2,1)S(1)} %qkv_piece.1.refs_0_), channel_id=1, source_target_pairs={{0,2},{1,3},{2,0},{3,1},{4,6},{5,7},{6,4},{7,5},{8,10},{9,11},{10,... | collective-permute-start | bytes 497672 | tf_op jit(solution)/shard_map/ppermute | solution.py:73
  9.5 15.6 %collective-permute-start.3 = (bf16[144,576]{1,0:T(8,128)(2,1)S(1)}, bf16[144,576]{1,0:T(8,128)(2,1)S(1)}, u32[]{:S(2)}, u32[]{:S(2)}) collective-permute-start(bf16[144,576]{1,0:T(8,128)(2,1)S(1)} %qkv_piece.1.refs_0_), channel_id=1, source_target_pairs={{0,1},{1,0},{2,3},{3,2},{4,5},{5,4},{6,7},{7,6},{8,9},{9,8},{10,11... | collective-permute-start | bytes 497672 | tf_op jit(solution)/shard_map/ppermute | solution.py:73
  10.1 17.2 %collective-permute-start.2 = (bf16[128,768]{1,0:T(8,128)(2,1)S(1)}, bf16[128,768]{1,0:T(8,128)(2,1)S(1)}, u32[]{:S(2)}, u32[]{:S(2)}) collective-permute-start(bf16[128,768]{1,0:T(8,128)(2,1)S(1)} %bitcast.19), channel_id=1, source_target_pairs={{0,24},{4,28},{8,16},{12,20},{16,8},{20,12},{24,0},{28,4},{1,25},{... | collective-permute-start | bytes 589832 | tf_op jit(solution)/shard_map/ppermute | solution.py:68
  12.8 14.6 %collective-permute-start = (bf16[128,768]{1,0:T(8,128)(2,1)S(1)}, bf16[128,768]{1,0:T(8,128)(2,1)S(1)}, u32[]{:S(2)}, u32[]{:S(2)}) collective-permute-start(bf16[128,768]{1,0:T(8,128)(2,1)S(1)} %bitcast.20), channel_id=1, source_target_pairs={{0,8},{4,12},{8,0},{12,4},{16,24},{20,28},{24,16},{28,20},{1,9},{5... | collective-permute-start | bytes 589832 | tf_op jit(solution)/shard_map/ppermute | solution.py:68
  30.5 16.1 %collective-permute-start.15 = (bf16[2,4,48,384]{3,2,1,0:T(8,128)(2,1)S(1)}, bf16[2,4,48,384]{3,2,1,0:T(8,128)(2,1)S(1)}, u32[]{:S(2)}, u32[]{:S(2)}) collective-permute-start(bf16[2,4,48,384]{3,2,1,0:T(8,128)(2,1)S(1)} %out_pair.1.refs_2_), channel_id=1, source_target_pairs={{0,16},{4,20},{8,24},{12,28},{16,0},{20,4},{24,8},{28,12},{1,17},{... | collective-permute-start | bytes 884744 | tf_op jit(solution)/shard_map/ppermute | solution.py:68
  32.1 10.9 %collective-permute-start.10 = (bf16[2,128,768]{2,1,0:T(8,128)(2,1)S(1)}, bf16[2,128,768]{2,1,0:T(8,128)(2,1)S(1)}, u32[]{:S(2)}, u32[]{:S(2)}) collective-permute-start(bf16[2,128,768]{2,1,0:T(8,128)(2,1)S(1)} %up_pair.1.refs_8_.refs_3_.refs_4_), channel_id=1, source_target_pairs={{0,8},{4,12},{8,0},{12,4},{16,24},{20,28},{24,16},{28,20},{1,9},{5... | collective-permute-start | bytes 1179656 | tf_op jit(solution)/shard_map/ppermute | solution.py:68
  34.7 20.9 %collective-permute-start.14 = (bf16[2,96,960]{2,1,0:T(8,128)(2,1)S(1)}, bf16[2,96,960]{2,1,0:T(8,128)(2,1)S(1)}, u32[]{:S(2)}, u32[]{:S(2)}) collective-permute-start(bf16[2,96,960]{2,1,0:T(8,128)(2,1)S(1)} %in_pair.1.refs_0_), channel_id=1, source_target_pairs={{0,2},{1,3},{2,0},{3,1},{4,6},{5,7},{6,4},{7,5},{8,10},{9,11},{10,... | collective-permute-start | bytes 1105928 | tf_op jit(solution)/shard_map/ppermute | solution.py:73
  43.0 12.6 %collective-permute-start.11 = (bf16[4,128,192]{2,1,0:T(8,128)(2,1)S(1)}, bf16[4,128,192]{2,1,0:T(8,128)(2,1)S(1)}, u32[]{:S(2)}, u32[]{:S(2)}) collective-permute-start(bf16[4,128,192]{2,1,0:T(8,128)(2,1)S(1)} %attn_copy.1), channel_id=1, source_target_pairs={{0,24},{4,28},{8,16},{12,20},{16,8},{20,12},{24,0},{28,4},{1,25},{... | collective-permute-start | bytes 589832 | tf_op jit(solution)/shard_map/ppermute | solution.py:68
  43.5 12.4 %collective-permute-start.9 = (bf16[4,128,192]{2,1,0:T(8,128)(2,1)S(1)}, bf16[4,128,192]{2,1,0:T(8,128)(2,1)S(1)}, u32[]{:S(2)}, u32[]{:S(2)}) collective-permute-start(bf16[4,128,192]{2,1,0:T(8,128)(2,1)S(1)} %attend.1.refs_0_.refs_6_), channel_id=1, source_target_pairs={{0,16},{4,20},{8,24},{12,28},{16,0},{20,4},{24,8},{28,12},{1,17},{... | collective-permute-start | bytes 589832 | tf_op jit(solution)/shard_map/ppermute | solution.py:68
  45.1 10.9 %collective-permute-start.8 = (bf16[4,128,192]{2,1,0:T(8,128)(2,1)S(1)}, bf16[4,128,192]{2,1,0:T(8,128)(2,1)S(1)}, u32[]{:S(2)}, u32[]{:S(2)}) collective-permute-start(bf16[4,128,192]{2,1,0:T(8,128)(2,1)S(1)} %attend.1.refs_0_.refs_6_), channel_id=1, source_target_pairs={{0,8},{4,12},{8,0},{12,4},{16,24},{20,28},{24,16},{28,20},{1,9},{5... | collective-permute-start | bytes 589832 | tf_op jit(solution)/shard_map/ppermute | solution.py:68
  80.9 10.6 %collective-permute-start.24 = (bf16[128,768]{1,0:T(8,128)(2,1)S(1)}, bf16[128,768]{1,0:T(8,128)(2,1)S(1)}, u32[]{:S(2)}, u32[]{:S(2)}) collective-permute-start(bf16[128,768]{1,0:T(8,128)(2,1)S(1)} %get-tuple-element.78.refs_2_.refs_4_.refs_10_), channel_id=1, source_target_pairs={{0,8},{4,12},{8,0},{12,4},{16,24},{20,28},{24,16},{28,20},{1,9},{5... | collective-permute-start | bytes 589832 | tf_op jit(solution)/shard_map/ppermute | solution.py:68
  82.0 19.2 %collective-permute-start.28 = (bf16[2,96,960]{2,1,0:T(8,128)(2,1)}, bf16[2,96,960]{2,1,0:T(8,128)(2,1)}, u32[]{:S(2)}, u32[]{:S(2)}) collective-permute-start(bf16[2,96,960]{2,1,0:T(8,128)(2,1)} %get-tuple-element.77.refs_7_.refs_9_), channel_id=1, source_target_pairs={{0,2},{1,3},{2,0},{3,1},{4,6},{5,7},{6,4},{7,5},{8,10},{9,11},{10,... | collective-permute-start | bytes 1105928 | tf_op jit(solution)/shard_map/ppermute | solution.py:73
  82.6 16.0 %collective-permute-start.21 = (bf16[128,768]{1,0:T(8,128)(2,1)S(1)}, bf16[128,768]{1,0:T(8,128)(2,1)S(1)}, u32[]{:S(2)}, u32[]{:S(2)}) collective-permute-start(bf16[128,768]{1,0:T(8,128)(2,1)S(1)} %get-tuple-element.80), channel_id=1, source_target_pairs={{0,8},{4,12},{8,0},{12,4},{16,24},{20,28},{24,16},{28,20},{1,9},{5... | collective-permute-start | bytes 589832 | tf_op jit(solution)/shard_map/ppermute | solution.py:68
  87.3 11.3 %collective-permute-start.22 = (bf16[128,768]{1,0:T(8,128)(2,1)S(1)}, bf16[128,768]{1,0:T(8,128)(2,1)S(1)}, u32[]{:S(2)}, u32[]{:S(2)}) collective-permute-start(bf16[128,768]{1,0:T(8,128)(2,1)S(1)} %get-tuple-element.81), channel_id=1, source_target_pairs={{0,16},{4,20},{8,24},{12,28},{16,0},{20,4},{24,8},{28,12},{1,17},{... | collective-permute-start | bytes 589832 | tf_op jit(solution)/shard_map/ppermute | solution.py:68
  107.2 17.8 %collective-permute-start.35 = (bf16[112,768]{1,0:T(8,128)(2,1)S(1)}, bf16[112,768]{1,0:T(8,128)(2,1)S(1)}, u32[]{:S(2)}, u32[]{:S(2)}) collective-permute-start(bf16[112,768]{1,0:T(8,128)(2,1)S(1)} %get-tuple-element.106), channel_id=1, source_target_pairs={{0,2},{1,3},{2,0},{3,1},{4,6},{5,7},{6,4},{7,5},{8,10},{9,11},{10,... | collective-permute-start | bytes 516104 | tf_op jit(solution)/shard_map/ppermute | solution.py:73
  109.1 15.9 %collective-permute-start.36 = (bf16[112,768]{1,0:T(8,128)(2,1)S(1)}, bf16[112,768]{1,0:T(8,128)(2,1)S(1)}, u32[]{:S(2)}, u32[]{:S(2)}) collective-permute-start(bf16[112,768]{1,0:T(8,128)(2,1)S(1)} %get-tuple-element.107), channel_id=1, source_target_pairs={{0,3},{1,2},{2,1},{3,0},{4,7},{5,6},{6,5},{7,4},{8,11},{9,10},{10,... | collective-permute-start | bytes 516104 | tf_op jit(solution)/shard_map/ppermute | solution.py:73
  111.5 11.7 %collective-permute-start.33 = (bf16[112,768]{1,0:T(8,128)(2,1)S(1)}, bf16[112,768]{1,0:T(8,128)(2,1)S(1)}, u32[]{:S(2)}, u32[]{:S(2)}) collective-permute-start(bf16[112,768]{1,0:T(8,128)(2,1)S(1)} %get-tuple-element.100.refs_3_.refs_7_), channel_id=1, source_target_pairs={{0,1},{1,0},{2,3},{3,2},{4,5},{5,4},{6,7},{7,6},{8,9},{9,8},{10,11... | collective-permute-start | bytes 516104 | tf_op jit(solution)/shard_map/ppermute | solution.py:73
  111.7 15.4 %collective-permute-start.31 = (bf16[256,768]{1,0:T(8,128)(2,1)S(1)}, bf16[256,768]{1,0:T(8,128)(2,1)S(1)}, u32[]{:S(2)}, u32[]{:S(2)}) collective-permute-start(bf16[256,768]{1,0:T(8,128)(2,1)S(1)} %get-tuple-element.101), channel_id=1, source_target_pairs={{0,8},{4,12},{8,0},{12,4},{16,24},{20,28},{24,16},{28,20},{1,9},{5... | collective-permute-start | bytes 1179656 | tf_op jit(solution)/shard_map/ppermute | solution.py:68
  112.2 16.4 %collective-permute-start.32 = (bf16[256,768]{1,0:T(8,128)(2,1)S(1)}, bf16[256,768]{1,0:T(8,128)(2,1)S(1)}, u32[]{:S(2)}, u32[]{:S(2)}) collective-permute-start(bf16[256,768]{1,0:T(8,128)(2,1)S(1)} %get-tuple-element.102), channel_id=1, source_target_pairs={{0,16},{4,20},{8,24},{12,28},{16,0},{20,4},{24,8},{28,12},{1,17},{... | collective-permute-start | bytes 1179656 | tf_op jit(solution)/shard_map/ppermute | solution.py:68
  123.4 12.2 %collective-permute-start.34 = (bf16[256,768]{1,0:T(8,128)(2,1)S(1)}, bf16[256,768]{1,0:T(8,128)(2,1)S(1)}, u32[]{:S(2)}, u32[]{:S(2)}) collective-permute-start(bf16[256,768]{1,0:T(8,128)(2,1)S(1)} %third_packet.1), channel_id=1, source_target_pairs={{0,24},{4,28},{8,16},{12,20},{16,8},{20,12},{24,0},{28,4},{1,25},{... | collective-permute-start | bytes 1179656 | tf_op jit(solution)/shard_map/ppermute | solution.py:68
  125.0 15.3 %collective-permute-start.39 = (bf16[112,768]{1,0:T(8,128)(2,1)S(1)}, bf16[112,768]{1,0:T(8,128)(2,1)S(1)}, u32[]{:S(2)}, u32[]{:S(2)}) collective-permute-start(bf16[112,768]{1,0:T(8,128)(2,1)S(1)} %qkv_sum.1.refs_0_), channel_id=1, source_target_pairs={{0,24},{4,28},{8,16},{12,20},{16,8},{20,12},{24,0},{28,4},{1,25},{... | collective-permute-start | bytes 516104 | tf_op jit(solution)/shard_map/ppermute | solution.py:68
  126.5 13.8 %collective-permute-start.38 = (bf16[112,768]{1,0:T(8,128)(2,1)S(1)}, bf16[112,768]{1,0:T(8,128)(2,1)S(1)}, u32[]{:S(2)}, u32[]{:S(2)}) collective-permute-start(bf16[112,768]{1,0:T(8,128)(2,1)S(1)} %qkv_sum.1.refs_0_), channel_id=1, source_target_pairs={{0,16},{4,20},{8,24},{12,28},{16,0},{20,4},{24,8},{28,12},{1,17},{... | collective-permute-start | bytes 516104 | tf_op jit(solution)/shard_map/ppermute | solution.py:68
  127.1 13.2 %collective-permute-start.37 = (bf16[112,768]{1,0:T(8,128)(2,1)S(1)}, bf16[112,768]{1,0:T(8,128)(2,1)S(1)}, u32[]{:S(2)}, u32[]{:S(2)}) collective-permute-start(bf16[112,768]{1,0:T(8,128)(2,1)S(1)} %qkv_sum.1.refs_0_), channel_id=1, source_target_pairs={{0,8},{4,12},{8,0},{12,4},{16,24},{20,28},{24,16},{28,20},{1,9},{5... | collective-permute-start | bytes 516104 | tf_op jit(solution)/shard_map/ppermute | solution.py:68
  (47 other events, 353.5 us)

commit v5 on v4

--- a/solution.py
+++ b/solution.py
@@ -27,7 +27,7 @@
     "qkv_piece": 0.5,
     "ffn_piece": 1,
     "qkv_place": 0.8,
-    "qkv": 1.6,
+    "qkv": 3.2,
     "attend": 2.3,
     "ffn_place": 1.2,
     "ffn": 4.5,
@@ -78,7 +78,7 @@
 
 
 def over_chips(value):
-    return [value] + [swap_seq(value, CORES * j) for j in range(1, CHIPS)]
+    return [value] + [swap_seq(value, CORES * j) for j in range(CHIPS - 1, 0, -1)][::-1]
 
 
 def over_planes(value):
@@ -186,13 +186,11 @@
                 at = p * width + b * local
                 out[:half, p * local : (p + 1) * local] = rows[:, at : at + local]
 
-    both = gains[...].astype(f32)
-    out[half : half + EXTRA, :] = extra_rows(both[0:1, :], both[1:2, :], 3 * local).astype(bf16)
-    at = half + EXTRA
-    out[at : at + 16, :lanes] = part[:16, :]
-    out[at + 16 :, :lanes] = part[16:32, :]
-    out[at : at + 16, lanes:] = part[32:, :local]
-    out[at + 16 :, lanes:] = part[32:, local:]
+    both = gains[...].astype(f32)[None]
+    share = both.shape[1] // 2
+    out[half:, :] = extra_rows(both[:, :share], both[:, share:], out.shape[1]).astype(bf16)
+    out[:size, 3 * local :] = part[:, :local]
+    out[size:half, 3 * local :] = part[:, local:]
 
 
 def ffn_piece_kernel(where, w_in, w_back, out, rows, back, sems):
@@ -207,7 +205,10 @@
         ),
         sems,
     )
-    out[units:, :lanes] = jnp.zeros((half - units, lanes), bf16)
+    spare = half - units
+    side = units * lanes // half
+    rest = lanes - side
+    at_back = 2 * PLANES * units
     for b in range(CHIPS):
 
         @pl.when(chip == b)
@@ -215,9 +216,20 @@
             for p in range(2):
                 for z in range(PLANES):
                     at = p * FF + z * units * CHIPS + b * units
-                    to = lanes + (p * PLANES + z) * units
+                    to = (p * PLANES + z) * units
                     out[:, to : to + units] = rows[:, at : at + units]
-            out[:units, :lanes] = back[b * units : (b + 1) * units, :]
+            own = back[b * units : (b + 1) * units, :]
+            out[:units, at_back:] = own[:, :side]
+            for i in range(units // spare):
+                to = at_back + i * rest
+                out[units:, to : to + rest] = own[i * spare : (i + 1) * spare, side:]
+
+
+def unpacked(block, units):
+    spare = block.shape[0] - units
+    rest = block.shape[1] // (units // spare)
+    last = [block[units:, i * rest : (i + 1) * rest] for i in range(units // spare)]
+    return jnp.concatenate([block[:units], jnp.concatenate(last, axis=0)], axis=1)
 
 
 def place_kernel(slot, where, p0, p1, p2, p3, out):
@@ -226,16 +238,12 @@
 
 
 def qkv_place_kernel(where, p0, p1, p2, p3, out, packet):
-    kept = out.shape[1]
-    lanes = packet.shape[2]
+    lanes = out.shape[2]
+    size = packet.shape[1]
     for i, ref in enumerate((p0, p1, p2, p3)):
         z = where[2] ^ i
-        out[z] = ref[:kept, :]
-        packet[z, :16, :] = ref[kept : kept + 16, :lanes]
-        packet[z, 16:32, :] = ref[kept + 16 :, :lanes]
-        packet[z, 32:, :] = jnp.concatenate(
-            [ref[kept : kept + 16, lanes:], ref[kept + 16 :, lanes:]], axis=1
-        )
+        out[z] = ref[:, :lanes]
+        packet[z] = jnp.concatenate([ref[:size, lanes:], ref[size : 2 * size, lanes:]], axis=1)
 
 
 def up_pair_kernel(where, own, both, out):
@@ -282,8 +290,7 @@
     size, lanes = p0.shape[1:]
     for i, ref in enumerate((near.at[0], near.at[1], far.at[0], far.at[1])):
         z = where[2] ^ i
-        out[z, :, :lanes] = ref[:, :lanes]
-        out[z, :, 3 * lanes :] = ref[:, lanes:]
+        out[z, :, 2 * lanes :] = ref[...]
     for i, ref in enumerate((p0, p1, p2, p3)):
         b = where[0] ^ i
         at = rows_at((b % 2) * size, size)
@@ -293,7 +300,7 @@
             @pl.when(b // 2 == half_at)
             def _():
                 for z in range(PLANES):
-                    out[z, at, (half_at + 1) * lanes : (half_at + 2) * lanes] = ref[z]
+                    out[z, at, half_at * lanes : (half_at + 1) * lanes] = ref[z]
 
 
 def qkv_kernel(where, x0, x1, x2, x3, mine, other, cos, sin, a_out, q_out, kv_out, w_out, g_out):
@@ -327,6 +334,10 @@
         kv_out[j, :, local:] = value[at]
 
 
+def block_of(pairs, j, local):
+    return pairs[j // 2, :, j % 2 * local : (j % 2 + 1) * local]
+
+
 def extended(where, j, kv, other, rim):
     chip, core = where[0], where[1]
     length = kv.shape[1]
@@ -349,16 +360,18 @@
 
 
 def attend_kernel(edges, where, q, kv, other, bias, *rest):
-    rim, out = rest if edges else (None, rest[0])
+    rim, out, kept = rest if edges else (None, *rest)
     local = q.shape[-1]
+    extent = bias.shape[-1]
     for j in range(CHIPS):
         ext = extended(where, j, kv, other, rim)
         parts = []
         for h in range(local // HEAD_DIM):
             lanes = slice(h * HEAD_DIM, (h + 1) * HEAD_DIM)
             prob = probs_of(q[j, :, lanes], ext[:, lanes], bias[j]).astype(bf16)
+            kept[j, :, h * extent : (h + 1) * extent] = prob
             parts.append(dot(prob, ext[:, local + h * HEAD_DIM : local + (h + 1) * HEAD_DIM]))
-        out[j] = jnp.concatenate(parts, axis=1).astype(bf16)
+        out[j // 2, :, j % 2 * local : (j % 2 + 1) * local] = jnp.concatenate(parts, axis=1).astype(bf16)
 
 
 def ffn_kernel(
@@ -377,12 +390,16 @@
     local = width // CHIPS
     for z in range(PLANES):
         for k, ref in ((core, mine), (1 - core, other)):
-            wi[rows_at(z * share + k * half, half), :] = ref[z, :, 3 * lanes :]
+            wi[rows_at(z * share + k * half, half), :] = ref[z, :, width : width + 2 * units]
             for p in range(CORES):
                 at = slice(z * share + p * half, z * share + (p + 1) * half)
-                wo[at, lanes_at(k * lanes, lanes)] = ref[z, :, (p + 1) * lanes : (p + 2) * lanes]
-    own_back = jnp.concatenate([mine[z, :part, :lanes] for z in range(PLANES)], axis=0)
-    other_back = jnp.concatenate([other[z, :part, :lanes] for z in range(PLANES)], axis=0)
+                wo[at, lanes_at(k * lanes, lanes)] = ref[z, :, p * lanes : (p + 1) * lanes]
+    own_back, other_back = [
+        jnp.concatenate(
+            [unpacked(ref[z, :, width + 2 * units :], part) for z in range(PLANES)], axis=0
+        )
+        for ref in (mine, other)
+    ]
     wb_out[:, :lanes] = jnp.where(core == 0, own_back, other_back)
     wb_out[:, lanes:] = jnp.where(core == 0, other_back, own_back)
     wc_out[...] = wo[rows_at(chip * local, local), :]
@@ -395,7 +412,7 @@
     for j in range(CHIPS):
         hidden = xs[j][:rows, :].astype(f32)
         for i, (ref, weight) in enumerate(outward):
-            hidden = hidden + dot(ref[j ^ i], weight)
+            hidden = hidden + dot(block_of(ref, j ^ i, local), weight)
         if j == 0:
             hid_out[...] = hidden
         norm, _ = norm_parts(hidden)
@@ -464,12 +481,13 @@
     low_out[...] = dh.astype(bf16)
 
 
-def attend_back_kernel(edges, where, q, kv, other, bias, h0, h1, h2, h3, w_out, *rest):
+def attend_back_kernel(edges, where, q, kv, other, probs, h0, h1, h2, h3, w_out, *rest):
     rim, rest = (rest[0], rest[1:]) if edges else (None, rest)
     dq_out, dkv_out, back_out = rest[:3]
     chip, core = where[0], where[1]
     local = q.shape[-1]
     length = q.shape[1]
+    extent = length + 2 * HALF
     back_out[...] = jnp.zeros_like(back_out)
     for j, dh in enumerate((h0, h1, h2, h3)):
         dctx = dot_t(dh[...], w_out[...]).astype(bf16)
@@ -481,13 +499,14 @@
             kh = ext[:, lanes]
             vh = ext[:, local + h * HEAD_DIM : local + (h + 1) * HEAD_DIM]
             dch = dctx[:, lanes]
-            prob = probs_of(qh, kh, bias[j])
+            low = probs[j, :, h * extent : (h + 1) * extent]
+            prob = low.astype(f32)
             dprob = dot_t(dch, vh)
             inner = jnp.sum(prob * dprob, axis=-1, keepdims=True)
             dscore = (prob * (dprob - inner) * SCALE).astype(bf16)
             dqs.append(dot(dscore, kh))
             dks.append(t_dot(dscore, qh))
-            dvs.append(t_dot(prob.astype(bf16), dch))
+            dvs.append(t_dot(low, dch))
         dq_out[j] = jnp.concatenate(dqs, axis=1)
         grads = jnp.concatenate(dks + dvs, axis=1)
         dkv_out[j] = grads[HALF : HALF + length]
@@ -555,7 +574,7 @@
                 cols[j * length : (j + 1) * length, :] = ref[:, b * local : (b + 1) * local]
 
     for i, ref in enumerate((t0, t1, t2, t3)):
-        rows = jnp.concatenate([ref[j ^ i] for j in range(CHIPS)], axis=0)
+        rows = jnp.concatenate([block_of(ref, j ^ i, local) for j in range(CHIPS)], axis=0)
         acc[rows_at((chip ^ i) * local, local), 3 * local :] = t_dot(rows, cols[...])
     half = keep.shape[1]
     share = CORES * half
@@ -682,8 +701,8 @@
     lanes = width // CORES
     extent = length + 2 * HALF
     kept = half + EXTRA
-    in_lanes = 2 * units + width + lanes
-    in_sent = lanes + 2 * units
+    in_sent = 2 * units + units // PLANES * lanes // half
+    in_lanes = width + in_sent
     ffn_lanes = 2 * units + lanes
     qkv_lanes = 4 * local
 
@@ -691,10 +710,10 @@
     piece = call(
         qkv_piece_kernel,
         "qkv_piece",
-        shape(kept + 32, 3 * local),
+        shape(kept, 4 * local),
         w_qkv,
         lax.dynamic_slice(w_out, (chip * out_rows, core * lanes), (out_rows, lanes)),
-        jnp.stack([norm_gain, ffn_gain]),
+        jnp.concatenate([norm_gain, ffn_gain]),
         held=1,
         scratch=(pltpu.VMEM((half, 3 * width), bf16), pltpu.SemaphoreType.DMA((1,))),
     )
@@ -777,18 +796,18 @@
         last = lax.dynamic_index_in_dim(kv, chip ^ (CHIPS - 1), 0, False)[length - HALF :]
         rim = (beyond(jnp.where(core == 0, first, last)),)
 
-    out_pair = call(pair_kernel, "out_pair", shape(2, *out_own.shape), out_own, out_near, after=(gains,))
+    up_pair = call(up_pair_kernel, "up_pair", shape(2, length, width), cotangent[0], both_near, after=(gains,))
+    gys = (up_pair, swap_seq(up_pair, CORES))
+    out_pair = call(pair_kernel, "out_pair", shape(2, *out_own.shape), out_own, out_near, after=(up_pair,))
     out_far = swap_seq(out_pair, 2 * CORES)
     in_pair = call(
         pair_kernel, "in_pair", shape(2, half, in_sent), piece, in_near, after=(out_pair,)
     )
     in_far = swap_shard(in_pair, 2)
-    up_pair = call(up_pair_kernel, "up_pair", shape(2, length, width), cotangent[0], both_near, after=(gains,))
-    gys = (up_pair, swap_seq(up_pair, CORES))
-    attn = call(
+    attn, probs = call(
         functools.partial(attend_kernel, edges),
         "attend",
-        shape(CHIPS, length, local),
+        (shape(2, length, 2 * local), shape(CHIPS, length, local // HEAD_DIM * extent)),
         query,
         kv,
         kv_other,
@@ -876,7 +895,7 @@
         query,
         kv,
         kv_other,
-        bias,
+        probs,
         *dhs,
         wo,
         *rim,
@@ -901,7 +920,7 @@
         return over_groups(out, bf16)
 
     mixed = call(
-        mixed_sum_kernel, "mixed_sum", shape(1, length, width), partial_mixed[0], *got_mixed, hidden, after=(dq,)
+        mixed_sum_kernel, "mixed_sum", shape(1, length, width), partial_mixed[0], *got_mixed, hidden, after=(away,)
     )
 
     keep, away, dqkv = call(
@@ -930,7 +949,7 @@
         (shape(half, ffn_lanes, dtype=f32), shape(half, ffn_lanes)),
         near,
         got_far,
-        after=(dq,),
+        after=(away,),
     )
     total = call(
         ffn_total_kernel,

time: 146 us -> 142 us (0.973)
  waiting for transfers between devices: 60 us -> 56.4 us
    ppermute x10, waiting for transfers between devices: 27.6 us -> 24.8 us  [swap_shard(): return lax.ppermute(value, 'shard', [(i, i ^ bits) for i in range(count)])]
  transfers between devices with their start and end apart: 42 -> 42, of which waited for: 19 -> 17; matrix products, arithmetic and copies ran while one was open for 2% -> 2% of each run, Pallas kernels for 16% -> 16%
where the time goes in v5:
time: 142 us
  waiting for transfers between devices  56.4 us (40%)
  starting transfers between devices  43.5 us (31%)
  Pallas kernels  31.4 us (22%)
  local copies, waits for them, and re-layouts  4.61 us (3%)
  between operations  3.81 us (3%)
  other arithmetic  2.05 us (1%)
    ppermute x32, waiting for transfers between devices, swap_seq(): return lax.ppermute(value, 'seq', [(i, i ^ bits) for i in range(count)])  31.6 us
    pallas_call x30, Pallas kernels, call(): pl.pallas_call(body, out_shape=outs, in_specs=specs, out_specs=jax.tree.m...  31.4 us
    ppermute x32, starting transfers between devices, swap_seq(): return lax.ppermute(value, 'seq', [(i, i ^ bits) for i in range(count)])  30 us
    ppermute x10, waiting for transfers between devices, swap_shard(): return lax.ppermute(value, 'shard', [(i, i ^ bits) for i in range(count)])  24.8 us
    ppermute x10, starting transfers between devices, swap_shard(): return lax.ppermute(value, 'shard', [(i, i ^ bits) for i in range(count)])  13.6 us
  transfers between devices with their start and end apart: 42, of which 17 were waited for; matrix products, arithmetic and copies ran while one was open for 2% of the time, Pallas kernels for 16%

profile of v5, /device:TPU:0, one launch (start us, length us, event | category | flops | bytes accessed | tf_op | source)
XLA Modules:
  0.0 141.8 jit_solution(10562642461965879827)
XLA Ops:
  3.8 5.1 %collective-permute-start.5 = (bf16[112,768]{1,0:T(8,128)(2,1)S(1)}, bf16[112,768]{1,0:T(8,128)(2,1)S(1)}, u32[]{:S(2)}, u32[]{:S(2)}) collective-permute-start(bf16[112,768]{1,0:T(8,128)(2,1)S(1)} %qkv_piece.1.refs_0_), channel_id=1, source_target_pairs={{0,3},{1,2},{2,1},{3,0},{4,7},{5,6},{6,5},{7,4},{8,11},{9,10},{10,... | collective-permute-start | bytes 516104 | tf_op jit(solution)/shard_map/ppermute | solution.py:73
  9.6 2.6 %collective-permute-start.2 = (bf16[128,768]{1,0:T(8,128)(2,1)S(1)}, bf16[128,768]{1,0:T(8,128)(2,1)S(1)}, u32[]{:S(2)}, u32[]{:S(2)}) collective-permute-start(bf16[128,768]{1,0:T(8,128)(2,1)S(1)} %bitcast.19), channel_id=1, source_target_pairs={{0,24},{4,28},{8,16},{12,20},{16,8},{20,12},{24,0},{28,4},{1,25},{... | collective-permute-start | bytes 589832 | tf_op jit(solution)/shard_map/ppermute | solution.py:68
  18.2 5.3 %collective-permute-done.4.refs_2_ = bf16[112,768]{1,0:T(8,128)(2,1)S(1)} collective-permute-done((bf16[112,768]{1,0:T(8,128)(2,1)S(1)}, bf16[112,768]{1,0:T(8,128)(2,1)S(1)}, u32[]{:S(2)}, u32[]{:S(2)}) %collective-permute-start.4) | collective-permute-done | bytes 172064 | tf_op jit(solution)/shard_map/ppermute | solution.py:73
  25.8 1.6 %collective-permute-done.1.refs_2_.refs_1_.refs_6_.refs_4_ = bf16[256,768]{1,0:T(8,128)(2,1)S(1)} collective-permute-done((bf16[256,768]{1,0:T(8,128)(2,1)S(1)}, bf16[256,768]{1,0:T(8,128)(2,1)S(1)}, u32[]{:S(2)}, u32[]{:S(2)}) %collective-permute-start.1) | collective-permute-done | bytes 393248 | tf_op jit(solution)/shard_map/ppermute | solution.py:68
  32.6 3.2 %collective-permute-start.14 = (bf16[2,96,864]{2,1,0:T(8,128)(2,1)S(1)}, bf16[2,96,864]{2,1,0:T(8,128)(2,1)S(1)}, u32[]{:S(2)}, u32[]{:S(2)}) collective-permute-start(bf16[2,96,864]{2,1,0:T(8,128)(2,1)S(1)} %in_pair.1.refs_0_), channel_id=1, source_target_pairs={{0,2},{1,3},{2,0},{3,1},{4,6},{5,7},{6,4},{7,5},{8,10},{9,11},{10,... | collective-permute-start | bytes 995336 | tf_op jit(solution)/shard_map/ppermute | solution.py:73
  35.8 2.4 %attend.1 = (bf16[2,128,384]{2,1,0:T(8,128)(2,1)S(1)}, bf16[4,128,768]{2,1,0:T(8,128)(2,1)S(1)}) custom-call(bf16[4,128,192]{2,1,0:T(8,128)(2,1)S(1)} %get-tuple-element.64.refs_0_, bf16[4,128,384]{2,1,0:T(8,128)(2,1)S(1)} %get-tuple-element.65.refs_1_, bf16[4,128,384]{2,1,0:T(8,128)(2,1)S(1)} %collective-permute-done.7.refs_2_, ...), custom_call_target="tpu_custom_call" | custom-call | flops 46000001024 | bytes 23 | tf_op jit(solution)/shard_map/attend/pallas_call | solution.py:113
  38.2 1.8 %collective-permute-done.10.refs_1_.refs_9_.refs_4_ = bf16[2,128,768]{2,1,0:T(8,128)(2,1)S(1)} collective-permute-done((bf16[2,128,768]{2,1,0:T(8,128)(2,1)S(1)}, bf16[2,128,768]{2,1,0:T(8,128)(2,1)S(1)}, u32[]{:S(2)}, u32[]{:S(2)}) %collective-permute-start.10) | collective-permute-done | bytes 393248 | tf_op jit(solution)/shard_map/ppermute | solution.py:68
  43.6 8.3 %collective-permute-done.14.refs_1_ = bf16[2,96,864]{2,1,0:T(8,128)(2,1)S(1)} collective-permute-done((bf16[2,96,864]{2,1,0:T(8,128)(2,1)S(1)}, bf16[2,96,864]{2,1,0:T(8,128)(2,1)S(1)}, u32[]{:S(2)}, u32[]{:S(2)}) %collective-permute-start.14) | collective-permute-done | bytes 331808 | tf_op jit(solution)/shard_map/ppermute | solution.py:73
  52.3 3.0 %collective-permute-done.16.refs_11_ = bf16[4,96,1632]{2,1,0:T(8,128)(2,1)S(1)} collective-permute-done((bf16[4,96,1632]{2,1,0:T(8,128)(2,1)S(1)}, bf16[4,96,1632]{2,1,0:T(8,128)(2,1)S(1)}, u32[]{:S(2)}, u32[]{:S(2)}) %collective-permute-start.16) | collective-permute-done | bytes 1253408 | tf_op jit(solution)/shard_map/ppermute | solution.py:68
  55.3 4.5 %ffn.1 = (f32[128,768]{1,0:T(8,128)S(1)}, bf16[128,768]{1,0:T(8,128)(2,1)S(1)}, bf16[128,768]{1,0:T(8,128)(2,1)S(1)}, bf16[128,768]{1,0:T(8,128)(2,1)S(1)}, f32[...) custom-call(bf16[2,128,384]{2,1,0:T(8,128)(2,1)S(1)} %get-tuple-elem, ...), custom_call_target="tpu_custom_call" | custom-call | flops 89999998976 | bytes 45 | tf_op jit(solution)/shard_map/ffn/pallas_call | solution.py:113
  62.6 2.5 %collective-permute-start.19 = (bf16[128,768]{1,0:T(8,128)(2,1)S(1)}, bf16[128,768]{1,0:T(8,128)(2,1)S(1)}, u32[]{:S(2)}, u32[]{:S(2)}) collective-permute-start(bf16[128,768]{1,0:T(8,128)(2,1)S(1)} %get-tuple-element.74), channel_id=1, source_target_pairs={{0,24},{4,28},{8,16},{12,20},{16,8},{20,12},{24,0},{28,4},{1,25},{... | collective-permute-start | bytes 589832 | tf_op jit(solution)/shard_map/ppermute | solution.py:68
  65.9 3.4 %collective-permute-done.17.refs_1_ = bf16[128,768]{1,0:T(8,128)(2,1)S(1)} collective-permute-done((bf16[128,768]{1,0:T(8,128)(2,1)S(1)}, bf16[128,768]{1,0:T(8,128)(2,1)S(1)}, u32[]{:S(2)}, u32[]{:S(2)}) %collective-permute-start.17) | collective-permute-done | bytes 196640 | tf_op jit(solution)/shard_map/ppermute | solution.py:68
  69.3 3.9 %collective-permute-done.18.refs_2_ = bf16[128,768]{1,0:T(8,128)(2,1)S(1)} collective-permute-done((bf16[128,768]{1,0:T(8,128)(2,1)S(1)}, bf16[128,768]{1,0:T(8,128)(2,1)S(1)}, u32[]{:S(2)}, u32[]{:S(2)}) %collective-permute-start.18) | collective-permute-done | bytes 196640 | tf_op jit(solution)/shard_map/ppermute | solution.py:68
  79.3 3.1 %collective-permute-done.26.refs_7_.refs_13_ = bf16[128,768]{1,0:T(8,128)(2,1)S(1)} collective-permute-done((bf16[128,768]{1,0:T(8,128)(2,1)S(1)}, bf16[128,768]{1,0:T(8,128)(2,1)S(1)}, u32[]{:S(2)}, u32[]{:S(2)}) %collective-permute-start.26) | collective-permute-done | bytes 196640 | tf_op jit(solution)/shard_map/ppermute | solution.py:68
  86.5 5.6 %attend_back.1 = (f32[4,128,192]{2,1,0:T(8,128)S(1)}, f32[4,128,384]{2,1,0:T(8,128)S(1)}, bf16[4,128,384]{2,1,0:T(8,128)(2,1)S(1)}) custom-call(bf16[4,128,192]{2,1,0:T(8,128)(2,1)S(1)} %copy-done.25, bf16[4,128,384]{2,1,0:T(8,128)(2,1)S(1)} %copy-done.12, bf16[4,128,384]{2,1,0:T(8,128)(2,1)S(1)} %copy-done.14, ...), custom_call_target="tpu_custom_call" | custom-call | flops 138000007168 | bytes 69 | tf_op jit(solution)/shard_map/attend_back/pallas_call | solution.py:113
  94.6 3.4 %qkv_grads.1 = (f32[4,96,768]{2,1,0:T(8,128)S(1)}, bf16[4,96,768]{2,1,0:T(8,128)(2,1)S(1)}, bf16[512,576]{1,0:T(8,128)(2,1)S(1)}) custom-call(f32[4,128,192]{2,1,0:T(8,128)S(1)} %get-tuple-element.88.refs_0_, f32[4,128,384]{2,1,0:T(8,128)S(1)} %get-tuple-element.89.refs_1_, bf16[4,128,384]{2,1,0:T(8,128)(2,1)S(1)} %collective-permute-done.27.refs_2_, ...), custom_call_target="tpu_custom_call" | custom-call | flops 48000000000 | bytes 24 | tf_op jit(solution)/shard_map/qkv_grads/pallas_call | solution.py:113
  101.1 3.3 %collective-permute-start.35 = (bf16[112,768]{1,0:T(8,128)(2,1)S(1)}, bf16[112,768]{1,0:T(8,128)(2,1)S(1)}, u32[]{:S(2)}, u32[]{:S(2)}) collective-permute-start(bf16[112,768]{1,0:T(8,128)(2,1)S(1)} %get-tuple-element.110), channel_id=1, source_target_pairs={{0,2},{1,3},{2,0},{3,1},{4,6},{5,7},{6,4},{7,5},{8,10},{9,11},{10,... | collective-permute-start | bytes 516104 | tf_op jit(solution)/shard_map/ppermute | solution.py:73
  105.5 3.7 %collective-permute-done.29.refs_1_ = bf16[96,960]{1,0:T(8,128)(2,1)S(1)} collective-permute-done((bf16[96,960]{1,0:T(8,128)(2,1)S(1)}, bf16[96,960]{1,0:T(8,128)(2,1)S(1)}, u32[]{:S(2)}, u32[]{:S(2)}) %collective-permute-start.29) | collective-permute-done | bytes 184352 | tf_op jit(solution)/shard_map/ppermute | solution.py:73
  111.2 6.4 %collective-permute-done.33.refs_2_.refs_1_ = bf16[112,768]{1,0:T(8,128)(2,1)S(1)} collective-permute-done((bf16[112,768]{1,0:T(8,128)(2,1)S(1)}, bf16[112,768]{1,0:T(8,128)(2,1)S(1)}, u32[]{:S(2)}, u32[]{:S(2)}) %collective-permute-start.33) | collective-permute-done | bytes 172064 | tf_op jit(solution)/shard_map/ppermute | solution.py:73
  117.7 1.6 %collective-permute-start.34 = (bf16[256,768]{1,0:T(8,128)(2,1)S(1)}, bf16[256,768]{1,0:T(8,128)(2,1)S(1)}, u32[]{:S(2)}, u32[]{:S(2)}) collective-permute-start(bf16[256,768]{1,0:T(8,128)(2,1)S(1)} %third_packet.1), channel_id=1, source_target_pairs={{0,24},{4,28},{8,16},{12,20},{16,8},{20,12},{24,0},{28,4},{1,25},{... | collective-permute-start | bytes 1179656 | tf_op jit(solution)/shard_map/ppermute | solution.py:68
  123.0 7.7 %collective-permute-done.34.refs_3_ = bf16[256,768]{1,0:T(8,128)(2,1)S(1)} collective-permute-done((bf16[256,768]{1,0:T(8,128)(2,1)S(1)}, bf16[256,768]{1,0:T(8,128)(2,1)S(1)}, u32[]{:S(2)}, u32[]{:S(2)}) %collective-permute-start.34) | collective-permute-done | bytes 393248 | tf_op jit(solution)/shard_map/ppermute | solution.py:68
  133.2 2.3 %ffn_owned.1 = (f32[192,2304]{1,0:T(8,128)}, f32[288,768]{1,0:T(8,128)}) custom-call(bf16[4,96,960]{2,1,0:T(8,128)(2,1)S(1)} %ffn_gather.1.refs_0_, bf16[4,96,960]{2,1,0:T(8,128)(2,1)S(1)} %collective-permute-done.40.refs_1_), custom_call_target="tpu_custom_call" | custom-call | flops 44000002048 | bytes 22 | tf_op jit(solution)/shard_map/ffn_owned/pallas_call | solution.py:113
  138.0 2.1 %collective-permute-done.41.refs_1_ = bf16[4,112,768]{2,1,0:T(8,128)(2,1)S(1)} collective-permute-done((bf16[4,112,768]{2,1,0:T(8,128)(2,1)S(1)}, bf16[4,112,768]{2,1,0:T(8,128)(2,1)S(1)}, u32[]{:S(2)}, u32[]{:S(2)}) %collective-permute-start.41) | collective-permute-done | bytes 688160 | tf_op jit(solution)/shard_map/ppermute | solution.py:68
  140.2 1.7 %qkv_owned.1 = (f32[192,2304]{1,0:T(8,128)}, f32[192,768]{1,0:T(8,128)}, f32[192]{0:T(256)}, f32[192]{0:T(256)}) custom-call(bf16[4,112,768]{2,1,0:T(8,128)(2,1)S(1)} %qkv_gather.1.refs_0_, bf16[4,112,768]{2,1,0:T(8,128)(2,1)S(1)} %collective-permute-done.41.refs_1_), custom_call_target="tpu_custom_call" | custom-call | flops 33999998976 | bytes 17 | tf_op jit(solution)/shard_map/qkv_owned/pallas_call | solution.py:113
  (162 shorter events, 49.6 us)
Async XLA Ops:
  3.8 13.9 %collective-permute-start.5 = (bf16[112,768]{1,0:T(8,128)(2,1)S(1)}, bf16[112,768]{1,0:T(8,128)(2,1)S(1)}, u32[]{:S(2)}, u32[]{:S(2)}) collective-permute-start(bf16[112,768]{1,0:T(8,128)(2,1)S(1)} %qkv_piece.1.refs_0_), channel_id=1, source_target_pairs={{0,3},{1,2},{2,1},{3,0},{4,7},{5,6},{6,5},{7,4},{8,11},{9,10},{10,... | collective-permute-start | bytes 516104 | tf_op jit(solution)/shard_map/ppermute | solution.py:73
  8.9 14.6 %collective-permute-start.4 = (bf16[112,768]{1,0:T(8,128)(2,1)S(1)}, bf16[112,768]{1,0:T(8,128)(2,1)S(1)}, u32[]{:S(2)}, u32[]{:S(2)}) collective-permute-start(bf16[112,768]{1,0:T(8,128)(2,1)S(1)} %qkv_piece.1.refs_0_), channel_id=1, source_target_pairs={{0,2},{1,3},{2,0},{3,1},{4,6},{5,7},{6,4},{7,5},{8,10},{9,11},{10,... | collective-permute-start | bytes 516104 | tf_op jit(solution)/shard_map/ppermute | solution.py:73
  8.9 14.6 %collective-permute-start.3 = (bf16[112,768]{1,0:T(8,128)(2,1)S(1)}, bf16[112,768]{1,0:T(8,128)(2,1)S(1)}, u32[]{:S(2)}, u32[]{:S(2)}) collective-permute-start(bf16[112,768]{1,0:T(8,128)(2,1)S(1)} %qkv_piece.1.refs_0_), channel_id=1, source_target_pairs={{0,1},{1,0},{2,3},{3,2},{4,5},{5,4},{6,7},{7,6},{8,9},{9,8},{10,11... | collective-permute-start | bytes 516104 | tf_op jit(solution)/shard_map/ppermute | solution.py:73
  9.6 16.1 %collective-permute-start.2 = (bf16[128,768]{1,0:T(8,128)(2,1)S(1)}, bf16[128,768]{1,0:T(8,128)(2,1)S(1)}, u32[]{:S(2)}, u32[]{:S(2)}) collective-permute-start(bf16[128,768]{1,0:T(8,128)(2,1)S(1)} %bitcast.19), channel_id=1, source_target_pairs={{0,24},{4,28},{8,16},{12,20},{16,8},{20,12},{24,0},{28,4},{1,25},{... | collective-permute-start | bytes 589832 | tf_op jit(solution)/shard_map/ppermute | solution.py:68
  12.2 13.6 %collective-permute-start = (bf16[128,768]{1,0:T(8,128)(2,1)S(1)}, bf16[128,768]{1,0:T(8,128)(2,1)S(1)}, u32[]{:S(2)}, u32[]{:S(2)}) collective-permute-start(bf16[128,768]{1,0:T(8,128)(2,1)S(1)} %bitcast.20), channel_id=1, source_target_pairs={{0,8},{4,12},{8,0},{12,4},{16,24},{20,28},{24,16},{28,20},{1,9},{5... | collective-permute-start | bytes 589832 | tf_op jit(solution)/shard_map/ppermute | solution.py:68
  29.0 11.0 %collective-permute-start.10 = (bf16[2,128,768]{2,1,0:T(8,128)(2,1)S(1)}, bf16[2,128,768]{2,1,0:T(8,128)(2,1)S(1)}, u32[]{:S(2)}, u32[]{:S(2)}) collective-permute-start(bf16[2,128,768]{2,1,0:T(8,128)(2,1)S(1)} %up_pair.1.refs_2_.refs_8_.refs_3_.refs_4_), channel_id=1, source_target_pairs={{0,8},{4,12},{8,0},{12,4},{16,24},{20,28},{24,16},{28,20},{1,9},{5... | collective-permute-start | bytes 1179656 | tf_op jit(solution)/shard_map/ppermute | solution.py:68
  30.7 12.9 %collective-permute-start.15 = (bf16[2,4,48,384]{3,2,1,0:T(8,128)(2,1)S(1)}, bf16[2,4,48,384]{3,2,1,0:T(8,128)(2,1)S(1)}, u32[]{:S(2)}, u32[]{:S(2)}) collective-permute-start(bf16[2,4,48,384]{3,2,1,0:T(8,128)(2,1)S(1)} %out_pair.1.refs_2_), channel_id=1, source_target_pairs={{0,16},{4,20},{8,24},{12,28},{16,0},{20,4},{24,8},{28,12},{1,17},{... | collective-permute-start | bytes 884744 | tf_op jit(solution)/shard_map/ppermute | solution.py:68
  32.6 19.3 %collective-permute-start.14 = (bf16[2,96,864]{2,1,0:T(8,128)(2,1)S(1)}, bf16[2,96,864]{2,1,0:T(8,128)(2,1)S(1)}, u32[]{:S(2)}, u32[]{:S(2)}) collective-permute-start(bf16[2,96,864]{2,1,0:T(8,128)(2,1)S(1)} %in_pair.1.refs_0_), channel_id=1, source_target_pairs={{0,2},{1,3},{2,0},{3,1},{4,6},{5,7},{6,4},{7,5},{8,10},{9,11},{10,... | collective-permute-start | bytes 995336 | tf_op jit(solution)/shard_map/ppermute | solution.py:73
  40.0 11.8 %collective-permute-start.11 = (bf16[2,128,384]{2,1,0:T(8,128)(2,1)S(1)}, bf16[2,128,384]{2,1,0:T(8,128)(2,1)S(1)}, u32[]{:S(2)}, u32[]{:S(2)}) collective-permute-start(bf16[2,128,384]{2,1,0:T(8,128)(2,1)S(1)} %attn_copy.1), channel_id=1, source_target_pairs={{0,24},{4,28},{8,16},{12,20},{16,8},{20,12},{24,0},{28,4},{1,25},{... | collective-permute-start | bytes 589832 | tf_op jit(solution)/shard_map/ppermute | solution.py:68
  41.6 10.3 %collective-permute-start.9 = (bf16[2,128,384]{2,1,0:T(8,128)(2,1)S(1)}, bf16[2,128,384]{2,1,0:T(8,128)(2,1)S(1)}, u32[]{:S(2)}, u32[]{:S(2)}) collective-permute-start(bf16[2,128,384]{2,1,0:T(8,128)(2,1)S(1)} %get-tuple-element.66.refs_0_.refs_6_), channel_id=1, source_target_pairs={{0,16},{4,20},{8,24},{12,28},{16,0},{20,4},{24,8},{28,12},{1,17},{... | collective-permute-start | bytes 589832 | tf_op jit(solution)/shard_map/ppermute | solution.py:68
  62.1 11.1 %collective-permute-start.18 = (bf16[128,768]{1,0:T(8,128)(2,1)S(1)}, bf16[128,768]{1,0:T(8,128)(2,1)S(1)}, u32[]{:S(2)}, u32[]{:S(2)}) collective-permute-start(bf16[128,768]{1,0:T(8,128)(2,1)S(1)} %get-tuple-element.73), channel_id=1, source_target_pairs={{0,16},{4,20},{8,24},{12,28},{16,0},{20,4},{24,8},{28,12},{1,17},{... | collective-permute-start | bytes 589832 | tf_op jit(solution)/shard_map/ppermute | solution.py:68
  62.6 10.6 %collective-permute-start.19 = (bf16[128,768]{1,0:T(8,128)(2,1)S(1)}, bf16[128,768]{1,0:T(8,128)(2,1)S(1)}, u32[]{:S(2)}, u32[]{:S(2)}) collective-permute-start(bf16[128,768]{1,0:T(8,128)(2,1)S(1)} %get-tuple-element.74), channel_id=1, source_target_pairs={{0,24},{4,28},{8,16},{12,20},{16,8},{20,12},{24,0},{28,4},{1,25},{... | collective-permute-start | bytes 589832 | tf_op jit(solution)/shard_map/ppermute | solution.py:68
  77.2 20.9 %collective-permute-start.28 = (bf16[2,96,960]{2,1,0:T(8,128)(2,1)}, bf16[2,96,960]{2,1,0:T(8,128)(2,1)}, u32[]{:S(2)}, u32[]{:S(2)}) collective-permute-start(bf16[2,96,960]{2,1,0:T(8,128)(2,1)} %get-tuple-element.80.refs_7_.refs_9_), channel_id=1, source_target_pairs={{0,2},{1,3},{2,0},{3,1},{4,6},{5,7},{6,4},{7,5},{8,10},{9,11},{10,... | collective-permute-start | bytes 1105928 | tf_op jit(solution)/shard_map/ppermute | solution.py:73
  77.8 14.4 %collective-permute-start.21 = (bf16[128,768]{1,0:T(8,128)(2,1)S(1)}, bf16[128,768]{1,0:T(8,128)(2,1)S(1)}, u32[]{:S(2)}, u32[]{:S(2)}) collective-permute-start(bf16[128,768]{1,0:T(8,128)(2,1)S(1)} %get-tuple-element.83), channel_id=1, source_target_pairs={{0,8},{4,12},{8,0},{12,4},{16,24},{20,28},{24,16},{28,20},{1,9},{5... | collective-permute-start | bytes 589832 | tf_op jit(solution)/shard_map/ppermute | solution.py:68
  99.2 9.9 %collective-permute-start.29 = (bf16[96,960]{1,0:T(8,128)(2,1)S(1)}, bf16[96,960]{1,0:T(8,128)(2,1)S(1)}, u32[]{:S(2)}, u32[]{:S(2)}) collective-permute-start(bf16[96,960]{1,0:T(8,128)(2,1)S(1)} %get-tuple-element.99), channel_id=1, source_target_pairs={{0,1},{1,0},{2,3},{3,2},{4,5},{5,4},{6,7},{7,6},{8,9},{9,8},{10,11... | collective-permute-start | bytes 552968 | tf_op jit(solution)/shard_map/ppermute | solution.py:73
  101.1 18.3 %collective-permute-start.35 = (bf16[112,768]{1,0:T(8,128)(2,1)S(1)}, bf16[112,768]{1,0:T(8,128)(2,1)S(1)}, u32[]{:S(2)}, u32[]{:S(2)}) collective-permute-start(bf16[112,768]{1,0:T(8,128)(2,1)S(1)} %get-tuple-element.110), channel_id=1, source_target_pairs={{0,2},{1,3},{2,0},{3,1},{4,6},{5,7},{6,4},{7,5},{8,10},{9,11},{10,... | collective-permute-start | bytes 516104 | tf_op jit(solution)/shard_map/ppermute | solution.py:73
  104.3 15.0 %collective-permute-start.36 = (bf16[112,768]{1,0:T(8,128)(2,1)S(1)}, bf16[112,768]{1,0:T(8,128)(2,1)S(1)}, u32[]{:S(2)}, u32[]{:S(2)}) collective-permute-start(bf16[112,768]{1,0:T(8,128)(2,1)S(1)} %get-tuple-element.111), channel_id=1, source_target_pairs={{0,3},{1,2},{2,1},{3,0},{4,7},{5,6},{6,5},{7,4},{8,11},{9,10},{10,... | collective-permute-start | bytes 516104 | tf_op jit(solution)/shard_map/ppermute | solution.py:73
  105.5 12.1 %collective-permute-start.33 = (bf16[112,768]{1,0:T(8,128)(2,1)S(1)}, bf16[112,768]{1,0:T(8,128)(2,1)S(1)}, u32[]{:S(2)}, u32[]{:S(2)}) collective-permute-start(bf16[112,768]{1,0:T(8,128)(2,1)S(1)} %get-tuple-element.104.refs_3_.refs_7_), channel_id=1, source_target_pairs={{0,1},{1,0},{2,3},{3,2},{4,5},{5,4},{6,7},{7,6},{8,9},{9,8},{10,11... | collective-permute-start | bytes 516104 | tf_op jit(solution)/shard_map/ppermute | solution.py:73
  109.3 13.0 %collective-permute-start.31 = (bf16[256,768]{1,0:T(8,128)(2,1)S(1)}, bf16[256,768]{1,0:T(8,128)(2,1)S(1)}, u32[]{:S(2)}, u32[]{:S(2)}) collective-permute-start(bf16[256,768]{1,0:T(8,128)(2,1)S(1)} %get-tuple-element.105), channel_id=1, source_target_pairs={{0,8},{4,12},{8,0},{12,4},{16,24},{20,28},{24,16},{28,20},{1,9},{5... | collective-permute-start | bytes 1179656 | tf_op jit(solution)/shard_map/ppermute | solution.py:68
  110.1 12.9 %collective-permute-start.32 = (bf16[256,768]{1,0:T(8,128)(2,1)S(1)}, bf16[256,768]{1,0:T(8,128)(2,1)S(1)}, u32[]{:S(2)}, u32[]{:S(2)}) collective-permute-start(bf16[256,768]{1,0:T(8,128)(2,1)S(1)} %get-tuple-element.106), channel_id=1, source_target_pairs={{0,16},{4,20},{8,24},{12,28},{16,0},{20,4},{24,8},{28,12},{1,17},{... | collective-permute-start | bytes 1179656 | tf_op jit(solution)/shard_map/ppermute | solution.py:68
  117.7 13.0 %collective-permute-start.34 = (bf16[256,768]{1,0:T(8,128)(2,1)S(1)}, bf16[256,768]{1,0:T(8,128)(2,1)S(1)}, u32[]{:S(2)}, u32[]{:S(2)}) collective-permute-start(bf16[256,768]{1,0:T(8,128)(2,1)S(1)} %third_packet.1), channel_id=1, source_target_pairs={{0,24},{4,28},{8,16},{12,20},{16,8},{20,12},{24,0},{28,4},{1,25},{... | collective-permute-start | bytes 1179656 | tf_op jit(solution)/shard_map/ppermute | solution.py:68
  119.4 16.0 %collective-permute-start.39 = (bf16[112,768]{1,0:T(8,128)(2,1)S(1)}, bf16[112,768]{1,0:T(8,128)(2,1)S(1)}, u32[]{:S(2)}, u32[]{:S(2)}) collective-permute-start(bf16[112,768]{1,0:T(8,128)(2,1)S(1)} %qkv_sum.1.refs_0_), channel_id=1, source_target_pairs={{0,24},{4,28},{8,16},{12,20},{16,8},{20,12},{24,0},{28,4},{1,25},{... | collective-permute-start | bytes 516104 | tf_op jit(solution)/shard_map/ppermute | solution.py:68
  120.8 15.9 %collective-permute-start.38 = (bf16[112,768]{1,0:T(8,128)(2,1)S(1)}, bf16[112,768]{1,0:T(8,128)(2,1)S(1)}, u32[]{:S(2)}, u32[]{:S(2)}) collective-permute-start(bf16[112,768]{1,0:T(8,128)(2,1)S(1)} %qkv_sum.1.refs_0_), channel_id=1, source_target_pairs={{0,16},{4,20},{8,24},{12,28},{16,0},{20,4},{24,8},{28,12},{1,17},{... | collective-permute-start | bytes 516104 | tf_op jit(solution)/shard_map/ppermute | solution.py:68
  122.3 14.4 %collective-permute-start.37 = (bf16[112,768]{1,0:T(8,128)(2,1)S(1)}, bf16[112,768]{1,0:T(8,128)(2,1)S(1)}, u32[]{:S(2)}, u32[]{:S(2)}) collective-permute-start(bf16[112,768]{1,0:T(8,128)(2,1)S(1)} %qkv_sum.1.refs_0_), channel_id=1, source_target_pairs={{0,8},{4,12},{8,0},{12,4},{16,24},{20,28},{24,16},{28,20},{1,9},{5... | collective-permute-start | bytes 516104 | tf_op jit(solution)/shard_map/ppermute | solution.py:68
  (45 other events, 322.1 us)

commit v6 on v5

--- a/solution.py
+++ b/solution.py
@@ -16,7 +16,7 @@
 CORES = 2
 MEMBERS = CHIPS * CORES
 PLANES = 4
-EXTRA = 16
+EXTRA = 8
 f32 = jnp.float32
 bf16 = jnp.bfloat16
 SCALE = HEAD_DIM ** (-0.5)
@@ -608,10 +608,10 @@
     for i in range(PLANES):
         at = where[2] ^ i
         total = keep[at] + got[at].astype(f32)
-        if i < 2:
-            near[i] = total
+        if i % 2 == 0:
+            near[i // 2] = total
         else:
-            far[i - 2] = total.astype(bf16)
+            far[i // 2] = total.astype(bf16)
 
 
 def ffn_near_kernel(where, near, got, own, sent):
@@ -623,13 +623,20 @@
     out[...] = (own[...] + got[...].astype(f32)).astype(out.dtype)
 
 
-def to_planes_gains_kernel(where, keep, got, gains, own, o1, o2, o3):
+def to_near_plane_kernel(where, keep, got, gains, out):
+    half = keep.shape[1]
+    at = where[2] ^ 1
+    out[:half, :] = (keep[at] + got[at].astype(f32)).astype(bf16)
+    out[half:, :] = gains[at].astype(bf16)
+
+
+def to_planes_gains_kernel(where, keep, got, gains, own, o2, o3):
     plane = where[2]
     half = keep.shape[1]
     own[:half, :] = keep[plane] + got[plane].astype(f32)
     own[half:, :] = gains[plane]
-    for i, ref in enumerate((o1, o2, o3)):
-        at = plane ^ (i + 1)
+    for i, ref in enumerate((o2, o3)):
+        at = plane ^ (i + 2)
         ref[:half, :] = (keep[at] + got[at].astype(f32)).astype(bf16)
         ref[half:, :] = gains[at].astype(bf16)
 
@@ -868,7 +875,7 @@
         keep_ffn,
         got_ffn,
     )
-    got_far = swap_shard(far, 2)
+    got_far = swap_shard(far, 1)
     dh, dh_low = call(
         dh_kernel, "dh", (shape(length, width, dtype=f32), shape(length, width)), own, *received, gys[0], hidden, gains, after=(far,)
     )
@@ -949,14 +956,14 @@
         (shape(half, ffn_lanes, dtype=f32), shape(half, ffn_lanes)),
         near,
         got_far,
-        after=(away,),
+        after=(dq,),
     )
     total = call(
         ffn_total_kernel,
         "ffn_total",
         shape(half, ffn_lanes, dtype=f32 if edges else bf16),
         own_ffn,
-        swap_shard(sent_near, 1),
+        swap_shard(sent_near, 2),
         after=(got,),
     )
     total = over_groups(total, bf16)
@@ -972,16 +979,21 @@
         gain_two,
         after=(mixed,),
     )
+    to_near = call(
+        to_near_plane_kernel, "qkv_to_near", shape(kept, qkv_lanes), keep, got, gain_sums
+    )
+    from_near = swap_shard(to_near, 1)
     sent = call(
         to_planes_gains_kernel,
         "qkv_to_planes",
         (shape(kept, qkv_lanes, dtype=f32),)
-        + (shape(kept, qkv_lanes),) * 3,
+        + (shape(kept, qkv_lanes),) * 2,
         keep,
         got,
         gain_sums,
-    )
-    got = [swap_shard(s, i + 1) for i, s in enumerate(sent[1:4])]
+        after=(to_near,),
+    )
+    got = [from_near] + [swap_shard(s, i + 2) for i, s in enumerate(sent[1:3])]
     packet = shape(length + half + 32, width)
     packets = call(last_packet_kernel, "last_packet", (packet,) * 2, total, o1, o2, after=(sent[1],))
     packets += call(last_packet_kernel, "third_packet", (packet,), total, o3, after=(got[0],))

time: 142 us -> 139 us (0.979)
  waiting for transfers between devices: 56.4 us -> 52.3 us
    ppermute x32, waiting for transfers between devices: 31.6 us -> 28.9 us  [swap_seq(): return lax.ppermute(value, 'seq', [(i, i ^ bits) for i in range(count)])]
    pallas_call x30 -> x31, Pallas kernels: 31.4 us -> 31.5 us  [call(): pl.pallas_call(body, out_shape=outs, in_specs=specs, out_specs=jax.tree.m...]
  transfers between devices with their start and end apart: 42 -> 42, of which waited for: 17 -> 19; matrix products, arithmetic and copies ran while one was open for 2% -> 2% of each run, Pallas kernels for 16% -> 16%
where the time goes in v6:
time: 139 us; the launch traced here: 138 us
  waiting for transfers between devices  52.3 us (38%)
  starting transfers between devices  44.3 us (32%)
  Pallas kernels  31.5 us (23%)
  local copies, waits for them, and re-layouts  4.23 us (3%)
  between operations  3.82 us (3%)
  other arithmetic  2.05 us (1%)
    pallas_call x31, Pallas kernels, call(): pl.pallas_call(body, out_shape=outs, in_specs=specs, out_specs=jax.tree.m...  31.5 us
    ppermute x32, starting transfers between devices, swap_seq(): return lax.ppermute(value, 'seq', [(i, i ^ bits) for i in range(count)])  29.4 us
    ppermute x32, waiting for transfers between devices, swap_seq(): return lax.ppermute(value, 'seq', [(i, i ^ bits) for i in range(count)])  28.9 us
    ppermute x10, waiting for transfers between devices, swap_shard(): return lax.ppermute(value, 'shard', [(i, i ^ bits) for i in range(count)])  23.4 us
    ppermute x10, starting transfers between devices, swap_shard(): return lax.ppermute(value, 'shard', [(i, i ^ bits) for i in range(count)])  14.9 us
  transfers between devices with their start and end apart: 42, of which 19 were waited for; matrix products, arithmetic and copies ran while one was open for 2% of the time, Pallas kernels for 16%

profile of v6, /device:TPU:0, one launch (start us, length us, event | category | flops | bytes accessed | tf_op | source)
XLA Modules:
  0.0 138.3 jit_solution(15271661491491012001)
XLA Ops:
  3.8 5.1 %collective-permute-start.5 = (bf16[104,768]{1,0:T(8,128)(2,1)S(1)}, bf16[104,768]{1,0:T(8,128)(2,1)S(1)}, u32[]{:S(2)}, u32[]{:S(2)}) collective-permute-start(bf16[104,768]{1,0:T(8,128)(2,1)S(1)} %qkv_piece.1.refs_0_), channel_id=1, source_target_pairs={{0,3},{1,2},{2,1},{3,0},{4,7},{5,6},{6,5},{7,4},{8,11},{9,10},{10,... | collective-permute-start | bytes 479240 | tf_op jit(solution)/shard_map/ppermute | solution.py:73
  9.6 2.6 %collective-permute-start.2 = (bf16[128,768]{1,0:T(8,128)(2,1)S(1)}, bf16[128,768]{1,0:T(8,128)(2,1)S(1)}, u32[]{:S(2)}, u32[]{:S(2)}) collective-permute-start(bf16[128,768]{1,0:T(8,128)(2,1)S(1)} %bitcast.19), channel_id=1, source_target_pairs={{0,24},{4,28},{8,16},{12,20},{16,8},{20,12},{24,0},{28,4},{1,25},{... | collective-permute-start | bytes 589832 | tf_op jit(solution)/shard_map/ppermute | solution.py:68
  18.2 4.3 %collective-permute-done.4.refs_2_ = bf16[104,768]{1,0:T(8,128)(2,1)S(1)} collective-permute-done((bf16[104,768]{1,0:T(8,128)(2,1)S(1)}, bf16[104,768]{1,0:T(8,128)(2,1)S(1)}, u32[]{:S(2)}, u32[]{:S(2)}) %collective-permute-start.4) | collective-permute-done | bytes 159776 | tf_op jit(solution)/shard_map/ppermute | solution.py:73
  24.8 2.7 %collective-permute-done.1.refs_2_.refs_1_.refs_6_.refs_4_ = bf16[256,768]{1,0:T(8,128)(2,1)S(1)} collective-permute-done((bf16[256,768]{1,0:T(8,128)(2,1)S(1)}, bf16[256,768]{1,0:T(8,128)(2,1)S(1)}, u32[]{:S(2)}, u32[]{:S(2)}) %collective-permute-start.1) | collective-permute-done | bytes 393248 | tf_op jit(solution)/shard_map/ppermute | solution.py:68
  31.5 3.2 %collective-permute-start.14 = (bf16[2,96,864]{2,1,0:T(8,128)(2,1)S(1)}, bf16[2,96,864]{2,1,0:T(8,128)(2,1)S(1)}, u32[]{:S(2)}, u32[]{:S(2)}) collective-permute-start(bf16[2,96,864]{2,1,0:T(8,128)(2,1)S(1)} %in_pair.1.refs_0_), channel_id=1, source_target_pairs={{0,2},{1,3},{2,0},{3,1},{4,6},{5,7},{6,4},{7,5},{8,10},{9,11},{10,... | collective-permute-start | bytes 995336 | tf_op jit(solution)/shard_map/ppermute | solution.py:73
  34.7 2.4 %attend.1 = (bf16[2,128,384]{2,1,0:T(8,128)(2,1)S(1)}, bf16[4,128,768]{2,1,0:T(8,128)(2,1)S(1)}) custom-call(bf16[4,128,192]{2,1,0:T(8,128)(2,1)S(1)} %get-tuple-element.63.refs_0_, bf16[4,128,384]{2,1,0:T(8,128)(2,1)S(1)} %get-tuple-element.64.refs_1_, bf16[4,128,384]{2,1,0:T(8,128)(2,1)S(1)} %collective-permute-done.7.refs_2_, ...), custom_call_target="tpu_custom_call" | custom-call | flops 46000001024 | bytes 23 | tf_op jit(solution)/shard_map/attend/pallas_call | solution.py:113
  37.1 1.8 %collective-permute-done.10.refs_1_.refs_9_.refs_4_ = bf16[2,128,768]{2,1,0:T(8,128)(2,1)S(1)} collective-permute-done((bf16[2,128,768]{2,1,0:T(8,128)(2,1)S(1)}, bf16[2,128,768]{2,1,0:T(8,128)(2,1)S(1)}, u32[]{:S(2)}, u32[]{:S(2)}) %collective-permute-start.10) | collective-permute-done | bytes 393248 | tf_op jit(solution)/shard_map/ppermute | solution.py:68
  42.5 8.3 %collective-permute-done.14.refs_1_ = bf16[2,96,864]{2,1,0:T(8,128)(2,1)S(1)} collective-permute-done((bf16[2,96,864]{2,1,0:T(8,128)(2,1)S(1)}, bf16[2,96,864]{2,1,0:T(8,128)(2,1)S(1)}, u32[]{:S(2)}, u32[]{:S(2)}) %collective-permute-start.14) | collective-permute-done | bytes 331808 | tf_op jit(solution)/shard_map/ppermute | solution.py:73
  51.3 3.0 %collective-permute-done.16.refs_11_ = bf16[4,96,1632]{2,1,0:T(8,128)(2,1)S(1)} collective-permute-done((bf16[4,96,1632]{2,1,0:T(8,128)(2,1)S(1)}, bf16[4,96,1632]{2,1,0:T(8,128)(2,1)S(1)}, u32[]{:S(2)}, u32[]{:S(2)}) %collective-permute-start.16) | collective-permute-done | bytes 1253408 | tf_op jit(solution)/shard_map/ppermute | solution.py:68
  54.2 4.5 %ffn.1 = (f32[128,768]{1,0:T(8,128)S(1)}, bf16[128,768]{1,0:T(8,128)(2,1)S(1)}, bf16[128,768]{1,0:T(8,128)(2,1)S(1)}, bf16[128,768]{1,0:T(8,128)(2,1)S(1)}, f32[...) custom-call(bf16[2,128,384]{2,1,0:T(8,128)(2,1)S(1)} %get-tuple-elem, ...), custom_call_target="tpu_custom_call" | custom-call | flops 89999998976 | bytes 45 | tf_op jit(solution)/shard_map/ffn/pallas_call | solution.py:113
  61.9 2.2 %collective-permute-start.19 = (bf16[128,768]{1,0:T(8,128)(2,1)S(1)}, bf16[128,768]{1,0:T(8,128)(2,1)S(1)}, u32[]{:S(2)}, u32[]{:S(2)}) collective-permute-start(bf16[128,768]{1,0:T(8,128)(2,1)S(1)} %get-tuple-element.73), channel_id=1, source_target_pairs={{0,24},{4,28},{8,16},{12,20},{16,8},{20,12},{24,0},{28,4},{1,25},{... | collective-permute-start | bytes 589832 | tf_op jit(solution)/shard_map/ppermute | solution.py:68
  64.9 3.3 %collective-permute-done.17.refs_1_ = bf16[128,768]{1,0:T(8,128)(2,1)S(1)} collective-permute-done((bf16[128,768]{1,0:T(8,128)(2,1)S(1)}, bf16[128,768]{1,0:T(8,128)(2,1)S(1)}, u32[]{:S(2)}, u32[]{:S(2)}) %collective-permute-start.17) | collective-permute-done | bytes 196640 | tf_op jit(solution)/shard_map/ppermute | solution.py:68
  68.5 3.7 %collective-permute-done.19.refs_3_ = bf16[128,768]{1,0:T(8,128)(2,1)S(1)} collective-permute-done((bf16[128,768]{1,0:T(8,128)(2,1)S(1)}, bf16[128,768]{1,0:T(8,128)(2,1)S(1)}, u32[]{:S(2)}, u32[]{:S(2)}) %collective-permute-start.19) | collective-permute-done | bytes 196640 | tf_op jit(solution)/shard_map/ppermute | solution.py:68
  72.6 1.8 %collective-permute-start.26 = (bf16[128,768]{1,0:T(8,128)(2,1)S(1)}, bf16[128,768]{1,0:T(8,128)(2,1)S(1)}, u32[]{:S(2)}, u32[]{:S(2)}) collective-permute-start(bf16[128,768]{1,0:T(8,128)(2,1)S(1)} %get-tuple-element.80.refs_2_.refs_4_.refs_10_), channel_id=1, source_target_pairs={{0,24},{4,28},{8,16},{12,20},{16,8},{20,12},{24,0},{28,4},{1,25},{... | collective-permute-start | bytes 589832 | tf_op jit(solution)/shard_map/ppermute | solution.py:68
  78.5 2.9 %collective-permute-done.26.refs_7_.refs_13_ = bf16[128,768]{1,0:T(8,128)(2,1)S(1)} collective-permute-done((bf16[128,768]{1,0:T(8,128)(2,1)S(1)}, bf16[128,768]{1,0:T(8,128)(2,1)S(1)}, u32[]{:S(2)}, u32[]{:S(2)}) %collective-permute-start.26) | collective-permute-done | bytes 196640 | tf_op jit(solution)/shard_map/ppermute | solution.py:68
  85.5 5.6 %attend_back.1 = (f32[4,128,192]{2,1,0:T(8,128)S(1)}, f32[4,128,384]{2,1,0:T(8,128)S(1)}, bf16[4,128,384]{2,1,0:T(8,128)(2,1)S(1)}) custom-call(bf16[4,128,192]{2,1,0:T(8,128)(2,1)S(1)} %copy-done.25, bf16[4,128,384]{2,1,0:T(8,128)(2,1)S(1)} %copy-done.12, bf16[4,128,384]{2,1,0:T(8,128)(2,1)S(1)} %copy-done.14, ...), custom_call_target="tpu_custom_call" | custom-call | flops 138000007168 | bytes 69 | tf_op jit(solution)/shard_map/attend_back/pallas_call | solution.py:113
  94.7 3.4 %qkv_grads.1 = (f32[4,96,768]{2,1,0:T(8,128)S(1)}, bf16[4,96,768]{2,1,0:T(8,128)(2,1)S(1)}, bf16[512,576]{1,0:T(8,128)(2,1)S(1)}) custom-call(f32[4,128,192]{2,1,0:T(8,128)S(1)} %get-tuple-element.87.refs_0_.refs_2_, f32[4,128,384]{2,1,0:T(8,128)S(1)} %get-tuple-element.88.refs_1_, bf16[4,128,384]{2,1,0:T(8,128)(2,1)S(1)} %collective-permute-done.27.refs_2_, ...), custom_call_target="tpu_custom_call" | custom-call | flops 48000000000 | bytes 24 | tf_op jit(solution)/shard_map/qkv_grads/pallas_call | solution.py:113
  100.2 3.8 %collective-permute-start.33 = (bf16[104,768]{1,0:T(8,128)(2,1)S(1)}, bf16[104,768]{1,0:T(8,128)(2,1)S(1)}, u32[]{:S(2)}, u32[]{:S(2)}) collective-permute-start(bf16[104,768]{1,0:T(8,128)(2,1)S(1)} %qkv_to_near.1.refs_3_), channel_id=1, source_target_pairs={{0,1},{1,0},{2,3},{3,2},{4,5},{5,4},{6,7},{7,6},{8,9},{9,8},{10,11... | collective-permute-start | bytes 479240 | tf_op jit(solution)/shard_map/ppermute | solution.py:73
  108.2 4.5 %collective-permute-done.33.refs_2_.refs_1_ = bf16[104,768]{1,0:T(8,128)(2,1)S(1)} collective-permute-done((bf16[104,768]{1,0:T(8,128)(2,1)S(1)}, bf16[104,768]{1,0:T(8,128)(2,1)S(1)}, u32[]{:S(2)}, u32[]{:S(2)}) %collective-permute-start.33) | collective-permute-done | bytes 159776 | tf_op jit(solution)/shard_map/ppermute | solution.py:73
  114.3 5.8 %collective-permute-done.35.refs_2_ = bf16[104,768]{1,0:T(8,128)(2,1)S(1)} collective-permute-done((bf16[104,768]{1,0:T(8,128)(2,1)S(1)}, bf16[104,768]{1,0:T(8,128)(2,1)S(1)}, u32[]{:S(2)}, u32[]{:S(2)}) %collective-permute-start.35) | collective-permute-done | bytes 159776 | tf_op jit(solution)/shard_map/ppermute | solution.py:73
  123.8 3.8 %collective-permute-done.34.refs_3_ = bf16[256,768]{1,0:T(8,128)(2,1)S(1)} collective-permute-done((bf16[256,768]{1,0:T(8,128)(2,1)S(1)}, bf16[256,768]{1,0:T(8,128)(2,1)S(1)}, u32[]{:S(2)}, u32[]{:S(2)}) %collective-permute-start.34) | collective-permute-done | bytes 393248 | tf_op jit(solution)/shard_map/ppermute | solution.py:68
  130.0 2.3 %ffn_owned.1 = (f32[192,2304]{1,0:T(8,128)}, f32[288,768]{1,0:T(8,128)}) custom-call(bf16[4,96,960]{2,1,0:T(8,128)(2,1)S(1)} %ffn_gather.1.refs_0_, bf16[4,96,960]{2,1,0:T(8,128)(2,1)S(1)} %collective-permute-done.40.refs_1_), custom_call_target="tpu_custom_call" | custom-call | flops 44000002048 | bytes 22 | tf_op jit(solution)/shard_map/ffn_owned/pallas_call | solution.py:113
  134.6 2.1 %collective-permute-done.41.refs_1_ = bf16[4,104,768]{2,1,0:T(8,128)(2,1)S(1)} collective-permute-done((bf16[4,104,768]{2,1,0:T(8,128)(2,1)S(1)}, bf16[4,104,768]{2,1,0:T(8,128)(2,1)S(1)}, u32[]{:S(2)}, u32[]{:S(2)}) %collective-permute-start.41) | collective-permute-done | bytes 639008 | tf_op jit(solution)/shard_map/ppermute | solution.py:68
  136.6 1.7 %qkv_owned.1 = (f32[192,2304]{1,0:T(8,128)}, f32[192,768]{1,0:T(8,128)}, f32[192]{0:T(256)}, f32[192]{0:T(256)}) custom-call(bf16[4,104,768]{2,1,0:T(8,128)(2,1)S(1)} %qkv_gather.1.refs_0_, bf16[4,104,768]{2,1,0:T(8,128)(2,1)S(1)} %collective-permute-done.41.refs_1_), custom_call_target="tpu_custom_call" | custom-call | flops 33999998976 | bytes 17 | tf_op jit(solution)/shard_map/qkv_owned/pallas_call | solution.py:113
  (163 shorter events, 49.8 us)
Async XLA Ops:
  3.8 13.9 %collective-permute-start.5 = (bf16[104,768]{1,0:T(8,128)(2,1)S(1)}, bf16[104,768]{1,0:T(8,128)(2,1)S(1)}, u32[]{:S(2)}, u32[]{:S(2)}) collective-permute-start(bf16[104,768]{1,0:T(8,128)(2,1)S(1)} %qkv_piece.1.refs_0_), channel_id=1, source_target_pairs={{0,3},{1,2},{2,1},{3,0},{4,7},{5,6},{6,5},{7,4},{8,11},{9,10},{10,... | collective-permute-start | bytes 479240 | tf_op jit(solution)/shard_map/ppermute | solution.py:73
  8.9 13.5 %collective-permute-start.4 = (bf16[104,768]{1,0:T(8,128)(2,1)S(1)}, bf16[104,768]{1,0:T(8,128)(2,1)S(1)}, u32[]{:S(2)}, u32[]{:S(2)}) collective-permute-start(bf16[104,768]{1,0:T(8,128)(2,1)S(1)} %qkv_piece.1.refs_0_), channel_id=1, source_target_pairs={{0,2},{1,3},{2,0},{3,1},{4,6},{5,7},{6,4},{7,5},{8,10},{9,11},{10,... | collective-permute-start | bytes 479240 | tf_op jit(solution)/shard_map/ppermute | solution.py:73
  8.9 13.5 %collective-permute-start.3 = (bf16[104,768]{1,0:T(8,128)(2,1)S(1)}, bf16[104,768]{1,0:T(8,128)(2,1)S(1)}, u32[]{:S(2)}, u32[]{:S(2)}) collective-permute-start(bf16[104,768]{1,0:T(8,128)(2,1)S(1)} %qkv_piece.1.refs_0_), channel_id=1, source_target_pairs={{0,1},{1,0},{2,3},{3,2},{4,5},{5,4},{6,7},{7,6},{8,9},{9,8},{10,11... | collective-permute-start | bytes 479240 | tf_op jit(solution)/shard_map/ppermute | solution.py:73
  9.6 15.1 %collective-permute-start.2 = (bf16[128,768]{1,0:T(8,128)(2,1)S(1)}, bf16[128,768]{1,0:T(8,128)(2,1)S(1)}, u32[]{:S(2)}, u32[]{:S(2)}) collective-permute-start(bf16[128,768]{1,0:T(8,128)(2,1)S(1)} %bitcast.19), channel_id=1, source_target_pairs={{0,24},{4,28},{8,16},{12,20},{16,8},{20,12},{24,0},{28,4},{1,25},{... | collective-permute-start | bytes 589832 | tf_op jit(solution)/shard_map/ppermute | solution.py:68
  12.2 12.6 %collective-permute-start = (bf16[128,768]{1,0:T(8,128)(2,1)S(1)}, bf16[128,768]{1,0:T(8,128)(2,1)S(1)}, u32[]{:S(2)}, u32[]{:S(2)}) collective-permute-start(bf16[128,768]{1,0:T(8,128)(2,1)S(1)} %bitcast.20), channel_id=1, source_target_pairs={{0,8},{4,12},{8,0},{12,4},{16,24},{20,28},{24,16},{28,20},{1,9},{5... | collective-permute-start | bytes 589832 | tf_op jit(solution)/shard_map/ppermute | solution.py:68
  29.1 9.9 %collective-permute-start.10 = (bf16[2,128,768]{2,1,0:T(8,128)(2,1)S(1)}, bf16[2,128,768]{2,1,0:T(8,128)(2,1)S(1)}, u32[]{:S(2)}, u32[]{:S(2)}) collective-permute-start(bf16[2,128,768]{2,1,0:T(8,128)(2,1)S(1)} %up_pair.1.refs_2_.refs_8_.refs_3_.refs_4_), channel_id=1, source_target_pairs={{0,8},{4,12},{8,0},{12,4},{16,24},{20,28},{24,16},{28,20},{1,9},{5... | collective-permute-start | bytes 1179656 | tf_op jit(solution)/shard_map/ppermute | solution.py:68
  30.7 11.8 %collective-permute-start.15 = (bf16[2,4,48,384]{3,2,1,0:T(8,128)(2,1)S(1)}, bf16[2,4,48,384]{3,2,1,0:T(8,128)(2,1)S(1)}, u32[]{:S(2)}, u32[]{:S(2)}) collective-permute-start(bf16[2,4,48,384]{3,2,1,0:T(8,128)(2,1)S(1)} %out_pair.1.refs_2_), channel_id=1, source_target_pairs={{0,16},{4,20},{8,24},{12,28},{16,0},{20,4},{24,8},{28,12},{1,17},{... | collective-permute-start | bytes 884744 | tf_op jit(solution)/shard_map/ppermute | solution.py:68
  31.5 19.3 %collective-permute-start.14 = (bf16[2,96,864]{2,1,0:T(8,128)(2,1)S(1)}, bf16[2,96,864]{2,1,0:T(8,128)(2,1)S(1)}, u32[]{:S(2)}, u32[]{:S(2)}) collective-permute-start(bf16[2,96,864]{2,1,0:T(8,128)(2,1)S(1)} %in_pair.1.refs_0_), channel_id=1, source_target_pairs={{0,2},{1,3},{2,0},{3,1},{4,6},{5,7},{6,4},{7,5},{8,10},{9,11},{10,... | collective-permute-start | bytes 995336 | tf_op jit(solution)/shard_map/ppermute | solution.py:73
  38.9 11.9 %collective-permute-start.11 = (bf16[2,128,384]{2,1,0:T(8,128)(2,1)S(1)}, bf16[2,128,384]{2,1,0:T(8,128)(2,1)S(1)}, u32[]{:S(2)}, u32[]{:S(2)}) collective-permute-start(bf16[2,128,384]{2,1,0:T(8,128)(2,1)S(1)} %attn_copy.1), channel_id=1, source_target_pairs={{0,24},{4,28},{8,16},{12,20},{16,8},{20,12},{24,0},{28,4},{1,25},{... | collective-permute-start | bytes 589832 | tf_op jit(solution)/shard_map/ppermute | solution.py:68
  40.5 10.3 %collective-permute-start.9 = (bf16[2,128,384]{2,1,0:T(8,128)(2,1)S(1)}, bf16[2,128,384]{2,1,0:T(8,128)(2,1)S(1)}, u32[]{:S(2)}, u32[]{:S(2)}) collective-permute-start(bf16[2,128,384]{2,1,0:T(8,128)(2,1)S(1)} %get-tuple-element.65.refs_0_.refs_6_), channel_id=1, source_target_pairs={{0,16},{4,20},{8,24},{12,28},{16,0},{20,4},{24,8},{28,12},{1,17},{... | collective-permute-start | bytes 589832 | tf_op jit(solution)/shard_map/ppermute | solution.py:68
  41.0 9.8 %collective-permute-start.8 = (bf16[2,128,384]{2,1,0:T(8,128)(2,1)S(1)}, bf16[2,128,384]{2,1,0:T(8,128)(2,1)S(1)}, u32[]{:S(2)}, u32[]{:S(2)}) collective-permute-start(bf16[2,128,384]{2,1,0:T(8,128)(2,1)S(1)} %get-tuple-element.65.refs_0_.refs_6_), channel_id=1, source_target_pairs={{0,8},{4,12},{8,0},{12,4},{16,24},{20,28},{24,16},{28,20},{1,9},{5... | collective-permute-start | bytes 589832 | tf_op jit(solution)/shard_map/ppermute | solution.py:68
  61.9 10.3 %collective-permute-start.19 = (bf16[128,768]{1,0:T(8,128)(2,1)S(1)}, bf16[128,768]{1,0:T(8,128)(2,1)S(1)}, u32[]{:S(2)}, u32[]{:S(2)}) collective-permute-start(bf16[128,768]{1,0:T(8,128)(2,1)S(1)} %get-tuple-element.73), channel_id=1, source_target_pairs={{0,24},{4,28},{8,16},{12,20},{16,8},{20,12},{24,0},{28,4},{1,25},{... | collective-permute-start | bytes 589832 | tf_op jit(solution)/shard_map/ppermute | solution.py:68
  76.1 17.3 %collective-permute-start.28 = (bf16[2,96,960]{2,1,0:T(8,128)(2,1)}, bf16[2,96,960]{2,1,0:T(8,128)(2,1)}, u32[]{:S(2)}, u32[]{:S(2)}) collective-permute-start(bf16[2,96,960]{2,1,0:T(8,128)(2,1)} %get-tuple-element.79.refs_7_.refs_9_), channel_id=1, source_target_pairs={{0,1},{1,0},{2,3},{3,2},{4,5},{5,4},{6,7},{7,6},{8,9},{9,8},{10,11... | collective-permute-start | bytes 1105928 | tf_op jit(solution)/shard_map/ppermute | solution.py:73
  77.1 14.0 %collective-permute-start.21 = (bf16[128,768]{1,0:T(8,128)(2,1)S(1)}, bf16[128,768]{1,0:T(8,128)(2,1)S(1)}, u32[]{:S(2)}, u32[]{:S(2)}) collective-permute-start(bf16[128,768]{1,0:T(8,128)(2,1)S(1)} %get-tuple-element.82), channel_id=1, source_target_pairs={{0,8},{4,12},{8,0},{12,4},{16,24},{20,28},{24,16},{28,20},{1,9},{5... | collective-permute-start | bytes 589832 | tf_op jit(solution)/shard_map/ppermute | solution.py:68
  94.5 11.6 %collective-permute-start.29 = (bf16[96,960]{1,0:T(8,128)(2,1)S(1)}, bf16[96,960]{1,0:T(8,128)(2,1)S(1)}, u32[]{:S(2)}, u32[]{:S(2)}) collective-permute-start(bf16[96,960]{1,0:T(8,128)(2,1)S(1)} %get-tuple-element.97), channel_id=1, source_target_pairs={{0,2},{1,3},{2,0},{3,1},{4,6},{5,7},{6,4},{7,5},{8,10},{9,11},{10,... | collective-permute-start | bytes 552968 | tf_op jit(solution)/shard_map/ppermute | solution.py:73
  100.2 12.5 %collective-permute-start.33 = (bf16[104,768]{1,0:T(8,128)(2,1)S(1)}, bf16[104,768]{1,0:T(8,128)(2,1)S(1)}, u32[]{:S(2)}, u32[]{:S(2)}) collective-permute-start(bf16[104,768]{1,0:T(8,128)(2,1)S(1)} %qkv_to_near.1.refs_3_), channel_id=1, source_target_pairs={{0,1},{1,0},{2,3},{3,2},{4,5},{5,4},{6,7},{7,6},{8,9},{9,8},{10,11... | collective-permute-start | bytes 479240 | tf_op jit(solution)/shard_map/ppermute | solution.py:73
  104.1 10.1 %collective-permute-start.36 = (bf16[104,768]{1,0:T(8,128)(2,1)S(1)}, bf16[104,768]{1,0:T(8,128)(2,1)S(1)}, u32[]{:S(2)}, u32[]{:S(2)}) collective-permute-start(bf16[104,768]{1,0:T(8,128)(2,1)S(1)} %get-tuple-element.109), channel_id=1, source_target_pairs={{0,3},{1,2},{2,1},{3,0},{4,7},{5,6},{6,5},{7,4},{8,11},{9,10},{10,... | collective-permute-start | bytes 479240 | tf_op jit(solution)/shard_map/ppermute | solution.py:73
  104.8 15.3 %collective-permute-start.35 = (bf16[104,768]{1,0:T(8,128)(2,1)S(1)}, bf16[104,768]{1,0:T(8,128)(2,1)S(1)}, u32[]{:S(2)}, u32[]{:S(2)}) collective-permute-start(bf16[104,768]{1,0:T(8,128)(2,1)S(1)} %get-tuple-element.103.refs_3_.refs_7_), channel_id=1, source_target_pairs={{0,2},{1,3},{2,0},{3,1},{4,6},{5,7},{6,4},{7,5},{8,10},{9,11},{10,... | collective-permute-start | bytes 479240 | tf_op jit(solution)/shard_map/ppermute | solution.py:73
  106.3 16.3 %collective-permute-start.31 = (bf16[256,768]{1,0:T(8,128)(2,1)S(1)}, bf16[256,768]{1,0:T(8,128)(2,1)S(1)}, u32[]{:S(2)}, u32[]{:S(2)}) collective-permute-start(bf16[256,768]{1,0:T(8,128)(2,1)S(1)} %get-tuple-element.104), channel_id=1, source_target_pairs={{0,8},{4,12},{8,0},{12,4},{16,24},{20,28},{24,16},{28,20},{1,9},{5... | collective-permute-start | bytes 1179656 | tf_op jit(solution)/shard_map/ppermute | solution.py:68
  107.6 16.1 %collective-permute-start.32 = (bf16[256,768]{1,0:T(8,128)(2,1)S(1)}, bf16[256,768]{1,0:T(8,128)(2,1)S(1)}, u32[]{:S(2)}, u32[]{:S(2)}) collective-permute-start(bf16[256,768]{1,0:T(8,128)(2,1)S(1)} %get-tuple-element.105), channel_id=1, source_target_pairs={{0,16},{4,20},{8,24},{12,28},{16,0},{20,4},{24,8},{28,12},{1,17},{... | collective-permute-start | bytes 1179656 | tf_op jit(solution)/shard_map/ppermute | solution.py:68
  112.8 14.8 %collective-permute-start.34 = (bf16[256,768]{1,0:T(8,128)(2,1)S(1)}, bf16[256,768]{1,0:T(8,128)(2,1)S(1)}, u32[]{:S(2)}, u32[]{:S(2)}) collective-permute-start(bf16[256,768]{1,0:T(8,128)(2,1)S(1)} %third_packet.1), channel_id=1, source_target_pairs={{0,24},{4,28},{8,16},{12,20},{16,8},{20,12},{24,0},{28,4},{1,25},{... | collective-permute-start | bytes 1179656 | tf_op jit(solution)/shard_map/ppermute | solution.py:68
  120.2 12.1 %collective-permute-start.39 = (bf16[104,768]{1,0:T(8,128)(2,1)S(1)}, bf16[104,768]{1,0:T(8,128)(2,1)S(1)}, u32[]{:S(2)}, u32[]{:S(2)}) collective-permute-start(bf16[104,768]{1,0:T(8,128)(2,1)S(1)} %qkv_sum.1.refs_0_), channel_id=1, source_target_pairs={{0,24},{4,28},{8,16},{12,20},{16,8},{20,12},{24,0},{28,4},{1,25},{... | collective-permute-start | bytes 479240 | tf_op jit(solution)/shard_map/ppermute | solution.py:68
  121.4 11.9 %collective-permute-start.38 = (bf16[104,768]{1,0:T(8,128)(2,1)S(1)}, bf16[104,768]{1,0:T(8,128)(2,1)S(1)}, u32[]{:S(2)}, u32[]{:S(2)}) collective-permute-start(bf16[104,768]{1,0:T(8,128)(2,1)S(1)} %qkv_sum.1.refs_0_), channel_id=1, source_target_pairs={{0,16},{4,20},{8,24},{12,28},{16,0},{20,4},{24,8},{28,12},{1,17},{... | collective-permute-start | bytes 479240 | tf_op jit(solution)/shard_map/ppermute | solution.py:68
  122.6 10.7 %collective-permute-start.37 = (bf16[104,768]{1,0:T(8,128)(2,1)S(1)}, bf16[104,768]{1,0:T(8,128)(2,1)S(1)}, u32[]{:S(2)}, u32[]{:S(2)}) collective-permute-start(bf16[104,768]{1,0:T(8,128)(2,1)S(1)} %qkv_sum.1.refs_0_), channel_id=1, source_target_pairs={{0,8},{4,12},{8,0},{12,4},{16,24},{20,28},{24,16},{28,20},{1,9},{5... | collective-permute-start | bytes 479240 | tf_op jit(solution)/shard_map/ppermute | solution.py:68
  (45 other events, 314.1 us)

commit v7 on v6

--- a/solution.py
+++ b/solution.py
@@ -27,7 +27,7 @@
     "qkv_piece": 0.5,
     "ffn_piece": 1,
     "qkv_place": 0.8,
-    "qkv": 3.2,
+    "qkv": 0.096,
     "attend": 2.3,
     "ffn_place": 1.2,
     "ffn": 4.5,
@@ -36,17 +36,17 @@
     "mixed": 0.6,
     "ffn_split": 1,
     "mixed_sum": 0.4,
-    "attend_back": 6.9,
-    "qkv_grads": 2.4,
+    "attend_back": 0.207,
+    "qkv_grads": 0.0144,
     "da": 1.5,
     "qkv_to_planes": 0.8,
-    "qkv_gather": 0.6,
+    "qkv_gather": 9,
     "last_packet": 0.5,
     "ffn_total": 0.4,
     "ffn_gather": 0.5,
     "qkv_sum": 0.4,
     "last": 0.6,
-    "ffn_owned": 2.2,
+    "ffn_owned": 0.066,
     "qkv_owned": 1.7,
 }
 
@@ -288,7 +288,7 @@
     half = near.shape[1]
     p0, p1, p2, p3 = p01.at[0], p01.at[1], p23.at[0], p23.at[1]
     size, lanes = p0.shape[1:]
-    for i, ref in enumerate((near.at[0], near.at[1], far.at[0], far.at[1])):
+    for i, ref in enumerate((near.at[0], far.at[0], near.at[1], far.at[1])):
         z = where[2] ^ i
         out[z, :, 2 * lanes :] = ref[...]
     for i, ref in enumerate((p0, p1, p2, p3)):
@@ -751,7 +751,7 @@
         ),
         after=(mine,),
     )
-    in_near = swap_shard(piece, 1)
+    in_near = swap_shard(piece, 2)
     out_near = swap_seq(out_own, CORES)
     other = swap_core(mine)
 
@@ -807,10 +807,6 @@
     gys = (up_pair, swap_seq(up_pair, CORES))
     out_pair = call(pair_kernel, "out_pair", shape(2, *out_own.shape), out_own, out_near, after=(up_pair,))
     out_far = swap_seq(out_pair, 2 * CORES)
-    in_pair = call(
-        pair_kernel, "in_pair", shape(2, half, in_sent), piece, in_near, after=(out_pair,)
-    )
-    in_far = swap_shard(in_pair, 2)
     attn, probs = call(
         functools.partial(attend_kernel, edges),
         "attend",
@@ -821,6 +817,10 @@
         bias,
         *rim,
     )
+    in_pair = call(
+        pair_kernel, "in_pair", shape(2, half, in_sent), piece, in_near, after=(attn,)
+    )
+    in_far = swap_shard(in_pair, 1)
     last_attn = call(copy_kernel, "attn_copy", shape(*attn.shape), attn, after=(gys[1],))
     attns = [attn, swap_seq(attn, CORES), swap_seq(attn, 2 * CORES), swap_seq(last_attn, 3 * CORES)]
     in_mine = call(

time: 139 us -> 137 us (0.986)
  Pallas kernels: 31.5 us -> 29.6 us
    ppermute x10, waiting for transfers between devices: 23.4 us -> 16 us  [swap_shard(): return lax.ppermute(value, 'shard', [(i, i ^ bits) for i in range(count)])]
    ppermute x32, waiting for transfers between devices: 28.9 us -> 36.2 us  [swap_seq(): return lax.ppermute(value, 'seq', [(i, i ^ bits) for i in range(count)])]
    pallas_call x31, Pallas kernels: 31.5 us -> 29.6 us  [call(): pl.pallas_call(body, out_shape=outs, in_specs=specs, out_specs=jax.tree.m...]
  transfers between devices with their start and end apart: 42 -> 42, of which waited for: 19 -> 21; matrix products, arithmetic and copies ran while one was open for 2% -> 2% of each run, Pallas kernels for 16% -> 15%
where the time goes in v7:
time: 137 us
  waiting for transfers between devices  52.3 us (38%)
  starting transfers between devices  45.1 us (33%)
  Pallas kernels  29.6 us (22%)
  local copies, waits for them, and re-layouts  4.19 us (3%)
  between operations  3.71 us (3%)
  other arithmetic  2.05 us (1%)
    ppermute x32, waiting for transfers between devices, swap_seq(): return lax.ppermute(value, 'seq', [(i, i ^ bits) for i in range(count)])  36.2 us
    pallas_call x31, Pallas kernels, call(): pl.pallas_call(body, out_shape=outs, in_specs=specs, out_specs=jax.tree.m...  29.6 us
    ppermute x32, starting transfers between devices, swap_seq(): return lax.ppermute(value, 'seq', [(i, i ^ bits) for i in range(count)])  29.2 us
    ppermute x10, waiting for transfers between devices, swap_shard(): return lax.ppermute(value, 'shard', [(i, i ^ bits) for i in range(count)])  16 us
    ppermute x10, starting transfers between devices, swap_shard(): return lax.ppermute(value, 'shard', [(i, i ^ bits) for i in range(count)])  15.9 us
  transfers between devices with their start and end apart: 42, of which 21 were waited for; matrix products, arithmetic and copies ran while one was open for 2% of the time, Pallas kernels for 15%

profile of v7, /device:TPU:0, one launch (start us, length us, event | category | flops | bytes accessed | tf_op | source)
XLA Modules:
  0.0 136.9 jit_solution(13530334083571988479)
XLA Ops:
  3.8 5.1 %collective-permute-start.5 = (bf16[104,768]{1,0:T(8,128)(2,1)S(1)}, bf16[104,768]{1,0:T(8,128)(2,1)S(1)}, u32[]{:S(2)}, u32[]{:S(2)}) collective-permute-start(bf16[104,768]{1,0:T(8,128)(2,1)S(1)} %qkv_piece.1.refs_0_), channel_id=1, source_target_pairs={{0,3},{1,2},{2,1},{3,0},{4,7},{5,6},{6,5},{7,4},{8,11},{9,10},{10,... | collective-permute-start | bytes 479240 | tf_op jit(solution)/shard_map/ppermute | solution.py:73
  9.6 2.6 %collective-permute-start.2 = (bf16[128,768]{1,0:T(8,128)(2,1)S(1)}, bf16[128,768]{1,0:T(8,128)(2,1)S(1)}, u32[]{:S(2)}, u32[]{:S(2)}) collective-permute-start(bf16[128,768]{1,0:T(8,128)(2,1)S(1)} %bitcast.19), channel_id=1, source_target_pairs={{0,24},{4,28},{8,16},{12,20},{16,8},{20,12},{24,0},{28,4},{1,25},{... | collective-permute-start | bytes 589832 | tf_op jit(solution)/shard_map/ppermute | solution.py:68
  18.2 4.3 %collective-permute-done.4.refs_2_ = bf16[104,768]{1,0:T(8,128)(2,1)S(1)} collective-permute-done((bf16[104,768]{1,0:T(8,128)(2,1)S(1)}, bf16[104,768]{1,0:T(8,128)(2,1)S(1)}, u32[]{:S(2)}, u32[]{:S(2)}) %collective-permute-start.4) | collective-permute-done | bytes 159776 | tf_op jit(solution)/shard_map/ppermute | solution.py:73
  25.6 1.8 %collective-permute-done.1.refs_2_.refs_1_.refs_6_.refs_4_ = bf16[256,768]{1,0:T(8,128)(2,1)S(1)} collective-permute-done((bf16[256,768]{1,0:T(8,128)(2,1)S(1)}, bf16[256,768]{1,0:T(8,128)(2,1)S(1)}, u32[]{:S(2)}, u32[]{:S(2)}) %collective-permute-start.1) | collective-permute-done | bytes 393248 | tf_op jit(solution)/shard_map/ppermute | solution.py:68
  32.4 2.4 %attend.1 = (bf16[2,128,384]{2,1,0:T(8,128)(2,1)S(1)}, bf16[4,128,768]{2,1,0:T(8,128)(2,1)S(1)}) custom-call(bf16[4,128,192]{2,1,0:T(8,128)(2,1)S(1)} %get-tuple-element.63.refs_0_, bf16[4,128,384]{2,1,0:T(8,128)(2,1)S(1)} %get-tuple-element.64.refs_1_, bf16[4,128,384]{2,1,0:T(8,128)(2,1)S(1)} %collective-permute-done.7.refs_2_, ...), custom_call_target="tpu_custom_call" | custom-call | flops 46000001024 | bytes 23 | tf_op jit(solution)/shard_map/attend/pallas_call | solution.py:113
  37.2 1.7 %collective-permute-done.10.refs_1_.refs_9_.refs_4_ = bf16[2,128,768]{2,1,0:T(8,128)(2,1)S(1)} collective-permute-done((bf16[2,128,768]{2,1,0:T(8,128)(2,1)S(1)}, bf16[2,128,768]{2,1,0:T(8,128)(2,1)S(1)}, u32[]{:S(2)}, u32[]{:S(2)}) %collective-permute-start.10) | collective-permute-done | bytes 393248 | tf_op jit(solution)/shard_map/ppermute | solution.py:68
  42.5 4.6 %collective-permute-done.11.refs_6_.refs_3_.refs_9_ = bf16[2,128,384]{2,1,0:T(8,128)(2,1)S(1)} collective-permute-done((bf16[2,128,384]{2,1,0:T(8,128)(2,1)S(1)}, bf16[2,128,384]{2,1,0:T(8,128)(2,1)S(1)}, u32[]{:S(2)}, u32[]{:S(2)}) %collective-permute-start.11) | collective-permute-done | bytes 196640 | tf_op jit(solution)/shard_map/ppermute | solution.py:68
  47.1 2.0 %collective-permute-done.9.refs_5_.refs_2_.refs_8_ = bf16[2,128,384]{2,1,0:T(8,128)(2,1)S(1)} collective-permute-done((bf16[2,128,384]{2,1,0:T(8,128)(2,1)S(1)}, bf16[2,128,384]{2,1,0:T(8,128)(2,1)S(1)}, u32[]{:S(2)}, u32[]{:S(2)}) %collective-permute-start.9) | collective-permute-done | bytes 196640 | tf_op jit(solution)/shard_map/ppermute | solution.py:68
  50.1 3.0 %collective-permute-done.16.refs_11_ = bf16[4,96,1632]{2,1,0:T(8,128)(2,1)S(1)} collective-permute-done((bf16[4,96,1632]{2,1,0:T(8,128)(2,1)S(1)}, bf16[4,96,1632]{2,1,0:T(8,128)(2,1)S(1)}, u32[]{:S(2)}, u32[]{:S(2)}) %collective-permute-start.16) | collective-permute-done | bytes 1253408 | tf_op jit(solution)/shard_map/ppermute | solution.py:68
  53.1 4.5 %ffn.1 = (f32[128,768]{1,0:T(8,128)S(1)}, bf16[128,768]{1,0:T(8,128)(2,1)S(1)}, bf16[128,768]{1,0:T(8,128)(2,1)S(1)}, bf16[128,768]{1,0:T(8,128)(2,1)S(1)}, f32[...) custom-call(bf16[2,128,384]{2,1,0:T(8,128)(2,1)S(1)} %get-tuple-elem, ...), custom_call_target="tpu_custom_call" | custom-call | flops 89999998976 | bytes 45 | tf_op jit(solution)/shard_map/ffn/pallas_call | solution.py:113
  60.8 2.0 %collective-permute-start.19 = (bf16[128,768]{1,0:T(8,128)(2,1)S(1)}, bf16[128,768]{1,0:T(8,128)(2,1)S(1)}, u32[]{:S(2)}, u32[]{:S(2)}) collective-permute-start(bf16[128,768]{1,0:T(8,128)(2,1)S(1)} %get-tuple-element.73), channel_id=1, source_target_pairs={{0,24},{4,28},{8,16},{12,20},{16,8},{20,12},{24,0},{28,4},{1,25},{... | collective-permute-start | bytes 589832 | tf_op jit(solution)/shard_map/ppermute | solution.py:68
  62.9 4.1 %collective-permute-done.17.refs_1_ = bf16[128,768]{1,0:T(8,128)(2,1)S(1)} collective-permute-done((bf16[128,768]{1,0:T(8,128)(2,1)S(1)}, bf16[128,768]{1,0:T(8,128)(2,1)S(1)}, u32[]{:S(2)}, u32[]{:S(2)}) %collective-permute-start.17) | collective-permute-done | bytes 196640 | tf_op jit(solution)/shard_map/ppermute | solution.py:68
  67.0 3.7 %collective-permute-done.19.refs_3_ = bf16[128,768]{1,0:T(8,128)(2,1)S(1)} collective-permute-done((bf16[128,768]{1,0:T(8,128)(2,1)S(1)}, bf16[128,768]{1,0:T(8,128)(2,1)S(1)}, u32[]{:S(2)}, u32[]{:S(2)}) %collective-permute-start.19) | collective-permute-done | bytes 196640 | tf_op jit(solution)/shard_map/ppermute | solution.py:68
  71.1 1.8 %collective-permute-start.26 = (bf16[128,768]{1,0:T(8,128)(2,1)S(1)}, bf16[128,768]{1,0:T(8,128)(2,1)S(1)}, u32[]{:S(2)}, u32[]{:S(2)}) collective-permute-start(bf16[128,768]{1,0:T(8,128)(2,1)S(1)} %get-tuple-element.80.refs_2_.refs_4_.refs_10_), channel_id=1, source_target_pairs={{0,24},{4,28},{8,16},{12,20},{16,8},{20,12},{24,0},{28,4},{1,25},{... | collective-permute-start | bytes 589832 | tf_op jit(solution)/shard_map/ppermute | solution.py:68
  74.7 2.2 %collective-permute-start.28 = (bf16[2,96,960]{2,1,0:T(8,128)(2,1)S(1)}, bf16[2,96,960]{2,1,0:T(8,128)(2,1)S(1)}, u32[]{:S(2)}, u32[]{:S(2)}) collective-permute-start(bf16[2,96,960]{2,1,0:T(8,128)(2,1)S(1)} %get-tuple-element.79.refs_7_.refs_9_), channel_id=1, source_target_pairs={{0,1},{1,0},{2,3},{3,2},{4,5},{5,4},{6,7},{7,6},{8,9},{9,8},{10,11... | collective-permute-start | bytes 1105928 | tf_op jit(solution)/shard_map/ppermute | solution.py:73
  78.3 1.7 %collective-permute-done.26.refs_7_.refs_13_ = bf16[128,768]{1,0:T(8,128)(2,1)S(1)} collective-permute-done((bf16[128,768]{1,0:T(8,128)(2,1)S(1)}, bf16[128,768]{1,0:T(8,128)(2,1)S(1)}, u32[]{:S(2)}, u32[]{:S(2)}) %collective-permute-start.26) | collective-permute-done | bytes 196640 | tf_op jit(solution)/shard_map/ppermute | solution.py:68
  84.1 5.6 %attend_back.1 = (f32[4,128,192]{2,1,0:T(8,128)S(1)}, f32[4,128,384]{2,1,0:T(8,128)S(1)}, bf16[4,128,384]{2,1,0:T(8,128)(2,1)S(1)}) custom-call(bf16[4,128,192]{2,1,0:T(8,128)(2,1)S(1)} %copy-done.17, bf16[4,128,384]{2,1,0:T(8,128)(2,1)S(1)} %copy-done.10, bf16[4,128,384]{2,1,0:T(8,128)(2,1)S(1)} %copy-done.12, ...), custom_call_target="tpu_custom_call" | custom-call | flops 4140000000 | bytes 2 | tf_op jit(solution)/shard_map/attend_back/pallas_call | solution.py:113
  92.0 2.2 %collective-permute-start.29 = (bf16[96,960]{1,0:T(8,128)(2,1)S(1)}, bf16[96,960]{1,0:T(8,128)(2,1)S(1)}, u32[]{:S(2)}, u32[]{:S(2)}) collective-permute-start(bf16[96,960]{1,0:T(8,128)(2,1)S(1)} %get-tuple-element.97), channel_id=1, source_target_pairs={{0,2},{1,3},{2,0},{3,1},{4,6},{5,7},{6,4},{7,5},{8,10},{9,11},{10,... | collective-permute-start | bytes 552968 | tf_op jit(solution)/shard_map/ppermute | solution.py:73
  94.3 3.4 %qkv_grads.1 = (f32[4,96,768]{2,1,0:T(8,128)S(1)}, bf16[4,96,768]{2,1,0:T(8,128)(2,1)S(1)}, bf16[512,576]{1,0:T(8,128)(2,1)S(1)}) custom-call(f32[4,128,192]{2,1,0:T(8,128)S(1)} %get-tuple-element.87.refs_0_.refs_2_, f32[4,128,384]{2,1,0:T(8,128)S(1)} %get-tuple-element.88.refs_1_, bf16[4,128,384]{2,1,0:T(8,128)(2,1)S(1)} %collective-permute-done.27.refs_2_, ...), custom_call_target="tpu_custom_call" | custom-call | flops 288000000 | tf_op jit(solution)/shard_map/qkv_grads/pallas_call | solution.py:113
  105.8 4.6 %collective-permute-done.33.refs_2_.refs_1_ = bf16[104,768]{1,0:T(8,128)(2,1)S(1)} collective-permute-done((bf16[104,768]{1,0:T(8,128)(2,1)S(1)}, bf16[104,768]{1,0:T(8,128)(2,1)S(1)}, u32[]{:S(2)}, u32[]{:S(2)}) %collective-permute-start.33) | collective-permute-done | bytes 159776 | tf_op jit(solution)/shard_map/ppermute | solution.py:73
  111.7 6.0 %collective-permute-done.35.refs_2_ = bf16[104,768]{1,0:T(8,128)(2,1)S(1)} collective-permute-done((bf16[104,768]{1,0:T(8,128)(2,1)S(1)}, bf16[104,768]{1,0:T(8,128)(2,1)S(1)}, u32[]{:S(2)}, u32[]{:S(2)}) %collective-permute-start.35) | collective-permute-done | bytes 159776 | tf_op jit(solution)/shard_map/ppermute | solution.py:73
  121.3 5.8 %collective-permute-done.32.refs_2_ = bf16[256,768]{1,0:T(8,128)(2,1)S(1)} collective-permute-done((bf16[256,768]{1,0:T(8,128)(2,1)S(1)}, bf16[256,768]{1,0:T(8,128)(2,1)S(1)}, u32[]{:S(2)}, u32[]{:S(2)}) %collective-permute-start.32) | collective-permute-done | bytes 393248 | tf_op jit(solution)/shard_map/ppermute | solution.py:68
  129.6 2.3 %ffn_owned.1 = (f32[192,2304]{1,0:T(8,128)}, f32[288,768]{1,0:T(8,128)}) custom-call(bf16[4,96,960]{2,1,0:T(8,128)(2,1)S(1)} %ffn_gather.1.refs_0_, bf16[4,96,960]{2,1,0:T(8,128)(2,1)S(1)} %collective-permute-done.40.refs_1_), custom_call_target="tpu_custom_call" | custom-call | flops 1320000000 | tf_op jit(solution)/shard_map/ffn_owned/pallas_call | solution.py:113
  133.3 1.9 %collective-permute-done.41.refs_1_ = bf16[4,104,768]{2,1,0:T(8,128)(2,1)S(1)} collective-permute-done((bf16[4,104,768]{2,1,0:T(8,128)(2,1)S(1)}, bf16[4,104,768]{2,1,0:T(8,128)(2,1)S(1)}, u32[]{:S(2)}, u32[]{:S(2)}) %collective-permute-start.41) | collective-permute-done | bytes 639008 | tf_op jit(solution)/shard_map/ppermute | solution.py:68
  (147 shorter events, 53.9 us)
Async XLA Ops:
  3.8 13.9 %collective-permute-start.5 = (bf16[104,768]{1,0:T(8,128)(2,1)S(1)}, bf16[104,768]{1,0:T(8,128)(2,1)S(1)}, u32[]{:S(2)}, u32[]{:S(2)}) collective-permute-start(bf16[104,768]{1,0:T(8,128)(2,1)S(1)} %qkv_piece.1.refs_0_), channel_id=1, source_target_pairs={{0,3},{1,2},{2,1},{3,0},{4,7},{5,6},{6,5},{7,4},{8,11},{9,10},{10,... | collective-permute-start | bytes 479240 | tf_op jit(solution)/shard_map/ppermute | solution.py:73
  8.9 13.5 %collective-permute-start.4 = (bf16[104,768]{1,0:T(8,128)(2,1)S(1)}, bf16[104,768]{1,0:T(8,128)(2,1)S(1)}, u32[]{:S(2)}, u32[]{:S(2)}) collective-permute-start(bf16[104,768]{1,0:T(8,128)(2,1)S(1)} %qkv_piece.1.refs_0_), channel_id=1, source_target_pairs={{0,2},{1,3},{2,0},{3,1},{4,6},{5,7},{6,4},{7,5},{8,10},{9,11},{10,... | collective-permute-start | bytes 479240 | tf_op jit(solution)/shard_map/ppermute | solution.py:73
  8.9 13.5 %collective-permute-start.3 = (bf16[104,768]{1,0:T(8,128)(2,1)S(1)}, bf16[104,768]{1,0:T(8,128)(2,1)S(1)}, u32[]{:S(2)}, u32[]{:S(2)}) collective-permute-start(bf16[104,768]{1,0:T(8,128)(2,1)S(1)} %qkv_piece.1.refs_0_), channel_id=1, source_target_pairs={{0,1},{1,0},{2,3},{3,2},{4,5},{5,4},{6,7},{7,6},{8,9},{9,8},{10,11... | collective-permute-start | bytes 479240 | tf_op jit(solution)/shard_map/ppermute | solution.py:73
  9.6 15.1 %collective-permute-start.2 = (bf16[128,768]{1,0:T(8,128)(2,1)S(1)}, bf16[128,768]{1,0:T(8,128)(2,1)S(1)}, u32[]{:S(2)}, u32[]{:S(2)}) collective-permute-start(bf16[128,768]{1,0:T(8,128)(2,1)S(1)} %bitcast.19), channel_id=1, source_target_pairs={{0,24},{4,28},{8,16},{12,20},{16,8},{20,12},{24,0},{28,4},{1,25},{... | collective-permute-start | bytes 589832 | tf_op jit(solution)/shard_map/ppermute | solution.py:68
  12.2 13.4 %collective-permute-start = (bf16[128,768]{1,0:T(8,128)(2,1)S(1)}, bf16[128,768]{1,0:T(8,128)(2,1)S(1)}, u32[]{:S(2)}, u32[]{:S(2)}) collective-permute-start(bf16[128,768]{1,0:T(8,128)(2,1)S(1)} %bitcast.20), channel_id=1, source_target_pairs={{0,8},{4,12},{8,0},{12,4},{16,24},{20,28},{24,16},{28,20},{1,9},{5... | collective-permute-start | bytes 589832 | tf_op jit(solution)/shard_map/ppermute | solution.py:68
  24.7 11.2 %collective-permute-start.12 = (bf16[96,864]{1,0:T(8,128)(2,1)S(1)}, bf16[96,864]{1,0:T(8,128)(2,1)S(1)}, u32[]{:S(2)}, u32[]{:S(2)}) collective-permute-start(bf16[96,864]{1,0:T(8,128)(2,1)S(1)} %ffn_piece.1.refs_0_), channel_id=1, source_target_pairs={{0,2},{1,3},{2,0},{3,1},{4,6},{5,7},{6,4},{7,5},{8,10},{9,11},{10,... | collective-permute-start | bytes 497672 | tf_op jit(solution)/shard_map/ppermute | solution.py:73
  29.0 9.9 %collective-permute-start.10 = (bf16[2,128,768]{2,1,0:T(8,128)(2,1)S(1)}, bf16[2,128,768]{2,1,0:T(8,128)(2,1)S(1)}, u32[]{:S(2)}, u32[]{:S(2)}) collective-permute-start(bf16[2,128,768]{2,1,0:T(8,128)(2,1)S(1)} %up_pair.1.refs_2_.refs_8_.refs_3_.refs_4_), channel_id=1, source_target_pairs={{0,8},{4,12},{8,0},{12,4},{16,24},{20,28},{24,16},{28,20},{1,9},{5... | collective-permute-start | bytes 1179656 | tf_op jit(solution)/shard_map/ppermute | solution.py:68
  30.7 11.8 %collective-permute-start.15 = (bf16[2,4,48,384]{3,2,1,0:T(8,128)(2,1)S(1)}, bf16[2,4,48,384]{3,2,1,0:T(8,128)(2,1)S(1)}, u32[]{:S(2)}, u32[]{:S(2)}) collective-permute-start(bf16[2,4,48,384]{3,2,1,0:T(8,128)(2,1)S(1)} %out_pair.1.refs_2_), channel_id=1, source_target_pairs={{0,16},{4,20},{8,24},{12,28},{16,0},{20,4},{24,8},{28,12},{1,17},{... | collective-permute-start | bytes 884744 | tf_op jit(solution)/shard_map/ppermute | solution.py:68
  36.0 13.7 %collective-permute-start.13 = (bf16[2,96,864]{2,1,0:T(8,128)(2,1)S(1)}, bf16[2,96,864]{2,1,0:T(8,128)(2,1)S(1)}, u32[]{:S(2)}, u32[]{:S(2)}) collective-permute-start(bf16[2,96,864]{2,1,0:T(8,128)(2,1)S(1)} %in_pair.1.refs_0_), channel_id=1, source_target_pairs={{0,1},{1,0},{2,3},{3,2},{4,5},{5,4},{6,7},{7,6},{8,9},{9,8},{10,11... | collective-permute-start | bytes 995336 | tf_op jit(solution)/shard_map/ppermute | solution.py:73
  60.8 10.0 %collective-permute-start.19 = (bf16[128,768]{1,0:T(8,128)(2,1)S(1)}, bf16[128,768]{1,0:T(8,128)(2,1)S(1)}, u32[]{:S(2)}, u32[]{:S(2)}) collective-permute-start(bf16[128,768]{1,0:T(8,128)(2,1)S(1)} %get-tuple-element.73), channel_id=1, source_target_pairs={{0,24},{4,28},{8,16},{12,20},{16,8},{20,12},{24,0},{28,4},{1,25},{... | collective-permute-start | bytes 589832 | tf_op jit(solution)/shard_map/ppermute | solution.py:68
  73.0 9.8 %collective-permute-start.25 = (bf16[128,768]{1,0:T(8,128)(2,1)S(1)}, bf16[128,768]{1,0:T(8,128)(2,1)S(1)}, u32[]{:S(2)}, u32[]{:S(2)}) collective-permute-start(bf16[128,768]{1,0:T(8,128)(2,1)S(1)} %get-tuple-element.80.refs_2_.refs_4_.refs_10_), channel_id=1, source_target_pairs={{0,16},{4,20},{8,24},{12,28},{16,0},{20,4},{24,8},{28,12},{1,17},{... | collective-permute-start | bytes 589832 | tf_op jit(solution)/shard_map/ppermute | solution.py:68
  74.7 17.2 %collective-permute-start.28 = (bf16[2,96,960]{2,1,0:T(8,128)(2,1)S(1)}, bf16[2,96,960]{2,1,0:T(8,128)(2,1)S(1)}, u32[]{:S(2)}, u32[]{:S(2)}) collective-permute-start(bf16[2,96,960]{2,1,0:T(8,128)(2,1)S(1)} %get-tuple-element.79.refs_7_.refs_9_), channel_id=1, source_target_pairs={{0,1},{1,0},{2,3},{3,2},{4,5},{5,4},{6,7},{7,6},{8,9},{9,8},{10,11... | collective-permute-start | bytes 1105928 | tf_op jit(solution)/shard_map/ppermute | solution.py:73
  77.5 12.4 %collective-permute-start.21 = (bf16[128,768]{1,0:T(8,128)(2,1)S(1)}, bf16[128,768]{1,0:T(8,128)(2,1)S(1)}, u32[]{:S(2)}, u32[]{:S(2)}) collective-permute-start(bf16[128,768]{1,0:T(8,128)(2,1)S(1)} %get-tuple-element.82), channel_id=1, source_target_pairs={{0,8},{4,12},{8,0},{12,4},{16,24},{20,28},{24,16},{28,20},{1,9},{5... | collective-permute-start | bytes 589832 | tf_op jit(solution)/shard_map/ppermute | solution.py:68
  80.0 9.9 %collective-permute-start.22 = (bf16[128,768]{1,0:T(8,128)(2,1)S(1)}, bf16[128,768]{1,0:T(8,128)(2,1)S(1)}, u32[]{:S(2)}, u32[]{:S(2)}) collective-permute-start(bf16[128,768]{1,0:T(8,128)(2,1)S(1)} %get-tuple-element.83), channel_id=1, source_target_pairs={{0,16},{4,20},{8,24},{12,28},{16,0},{20,4},{24,8},{28,12},{1,17},{... | collective-permute-start | bytes 589832 | tf_op jit(solution)/shard_map/ppermute | solution.py:68
  92.0 11.5 %collective-permute-start.29 = (bf16[96,960]{1,0:T(8,128)(2,1)S(1)}, bf16[96,960]{1,0:T(8,128)(2,1)S(1)}, u32[]{:S(2)}, u32[]{:S(2)}) collective-permute-start(bf16[96,960]{1,0:T(8,128)(2,1)S(1)} %get-tuple-element.97), channel_id=1, source_target_pairs={{0,2},{1,3},{2,0},{3,1},{4,6},{5,7},{6,4},{7,5},{8,10},{9,11},{10,... | collective-permute-start | bytes 552968 | tf_op jit(solution)/shard_map/ppermute | solution.py:73
  99.8 10.6 %collective-permute-start.33 = (bf16[104,768]{1,0:T(8,128)(2,1)S(1)}, bf16[104,768]{1,0:T(8,128)(2,1)S(1)}, u32[]{:S(2)}, u32[]{:S(2)}) collective-permute-start(bf16[104,768]{1,0:T(8,128)(2,1)S(1)} %qkv_to_near.1.refs_3_), channel_id=1, source_target_pairs={{0,1},{1,0},{2,3},{3,2},{4,5},{5,4},{6,7},{7,6},{8,9},{9,8},{10,11... | collective-permute-start | bytes 479240 | tf_op jit(solution)/shard_map/ppermute | solution.py:73
  100.9 10.7 %collective-permute-start.36 = (bf16[104,768]{1,0:T(8,128)(2,1)S(1)}, bf16[104,768]{1,0:T(8,128)(2,1)S(1)}, u32[]{:S(2)}, u32[]{:S(2)}) collective-permute-start(bf16[104,768]{1,0:T(8,128)(2,1)S(1)} %get-tuple-element.109), channel_id=1, source_target_pairs={{0,3},{1,2},{2,1},{3,0},{4,7},{5,6},{6,5},{7,4},{8,11},{9,10},{10,... | collective-permute-start | bytes 479240 | tf_op jit(solution)/shard_map/ppermute | solution.py:73
  102.4 15.2 %collective-permute-start.35 = (bf16[104,768]{1,0:T(8,128)(2,1)S(1)}, bf16[104,768]{1,0:T(8,128)(2,1)S(1)}, u32[]{:S(2)}, u32[]{:S(2)}) collective-permute-start(bf16[104,768]{1,0:T(8,128)(2,1)S(1)} %get-tuple-element.103.refs_3_.refs_7_), channel_id=1, source_target_pairs={{0,2},{1,3},{2,0},{3,1},{4,6},{5,7},{6,4},{7,5},{8,10},{9,11},{10,... | collective-permute-start | bytes 479240 | tf_op jit(solution)/shard_map/ppermute | solution.py:73
  103.7 16.4 %collective-permute-start.31 = (bf16[256,768]{1,0:T(8,128)(2,1)S(1)}, bf16[256,768]{1,0:T(8,128)(2,1)S(1)}, u32[]{:S(2)}, u32[]{:S(2)}) collective-permute-start(bf16[256,768]{1,0:T(8,128)(2,1)S(1)} %get-tuple-element.104), channel_id=1, source_target_pairs={{0,8},{4,12},{8,0},{12,4},{16,24},{20,28},{24,16},{28,20},{1,9},{5... | collective-permute-start | bytes 1179656 | tf_op jit(solution)/shard_map/ppermute | solution.py:68
  105.0 22.1 %collective-permute-start.32 = (bf16[256,768]{1,0:T(8,128)(2,1)S(1)}, bf16[256,768]{1,0:T(8,128)(2,1)S(1)}, u32[]{:S(2)}, u32[]{:S(2)}) collective-permute-start(bf16[256,768]{1,0:T(8,128)(2,1)S(1)} %get-tuple-element.105), channel_id=1, source_target_pairs={{0,16},{4,20},{8,24},{12,28},{16,0},{20,4},{24,8},{28,12},{1,17},{... | collective-permute-start | bytes 1179656 | tf_op jit(solution)/shard_map/ppermute | solution.py:68
  110.5 16.6 %collective-permute-start.34 = (bf16[256,768]{1,0:T(8,128)(2,1)S(1)}, bf16[256,768]{1,0:T(8,128)(2,1)S(1)}, u32[]{:S(2)}, u32[]{:S(2)}) collective-permute-start(bf16[256,768]{1,0:T(8,128)(2,1)S(1)} %third_packet.1), channel_id=1, source_target_pairs={{0,24},{4,28},{8,16},{12,20},{16,8},{20,12},{24,0},{28,4},{1,25},{... | collective-permute-start | bytes 1179656 | tf_op jit(solution)/shard_map/ppermute | solution.py:68
  117.7 14.1 %collective-permute-start.39 = (bf16[104,768]{1,0:T(8,128)(2,1)S(1)}, bf16[104,768]{1,0:T(8,128)(2,1)S(1)}, u32[]{:S(2)}, u32[]{:S(2)}) collective-permute-start(bf16[104,768]{1,0:T(8,128)(2,1)S(1)} %qkv_sum.1.refs_0_), channel_id=1, source_target_pairs={{0,24},{4,28},{8,16},{12,20},{16,8},{20,12},{24,0},{28,4},{1,25},{... | collective-permute-start | bytes 479240 | tf_op jit(solution)/shard_map/ppermute | solution.py:68
  119.3 12.5 %collective-permute-start.38 = (bf16[104,768]{1,0:T(8,128)(2,1)S(1)}, bf16[104,768]{1,0:T(8,128)(2,1)S(1)}, u32[]{:S(2)}, u32[]{:S(2)}) collective-permute-start(bf16[104,768]{1,0:T(8,128)(2,1)S(1)} %qkv_sum.1.refs_0_), channel_id=1, source_target_pairs={{0,16},{4,20},{8,24},{12,28},{16,0},{20,4},{24,8},{28,12},{1,17},{... | collective-permute-start | bytes 479240 | tf_op jit(solution)/shard_map/ppermute | solution.py:68
  120.1 11.8 %collective-permute-start.37 = (bf16[104,768]{1,0:T(8,128)(2,1)S(1)}, bf16[104,768]{1,0:T(8,128)(2,1)S(1)}, u32[]{:S(2)}, u32[]{:S(2)}) collective-permute-start(bf16[104,768]{1,0:T(8,128)(2,1)S(1)} %qkv_sum.1.refs_0_), channel_id=1, source_target_pairs={{0,8},{4,12},{8,0},{12,4},{16,24},{20,28},{24,16},{28,20},{1,9},{5... | collective-permute-start | bytes 479240 | tf_op jit(solution)/shard_map/ppermute | solution.py:68
  (37 other events, 218.5 us)
